TPU v7x, 32 devices: a whole 2x2x4 slice. The times are simulated.
32 devices in a mesh: frames: 16 (over z, y, core), patch: 2 (over x).
Axes of the slice: x: 2, y: 2, z: 4, core: 2. Of those that a mesh axis runs over, the one named last changes fastest.
Arguments:
- tokens: bfloat16 [16, 1024, 1152], P('frames', 'patch'), may hold values from -6 to 6
- cotangent: bfloat16 [16, 1024, 1152], P('frames', 'patch'), may hold values from -6 to 6
- clip_embed: float32 [2, 1152], replicated, may hold values from -6 to 6
- timesteps: int32 [2], replicated, may hold values from 0 to 999
- frame_clip: int32 [16], P('frames'), may hold values from 0 to 1, never falling along the last dimension, each value on 1 to 15 neighbouring positions
- ada_weight: bfloat16 [1152, 6912], P(('frames', 'patch')), may hold values from -0.1875 to 0.1875
- ada_bias: bfloat16 [6912], P(('frames', 'patch')), may hold values from -3 to 3
- qkv_weight: bfloat16 [1152, 3456], P(('frames', 'patch')), may hold values from -0.1875 to 0.1875
- query_bias: bfloat16 [1152], P(('frames', 'patch')), may hold values from -2.5 to 2.5
- value_bias: bfloat16 [1152], P(('frames', 'patch')), may hold values from -2.5 to 2.5
- out_weight: bfloat16 [1152, 1152], P(('frames', 'patch')), may hold values from -3 to 3
- out_bias: bfloat16 [1152], P(('frames', 'patch')), may hold values from -5 to 5
- up_weight: bfloat16 [1152, 4608], P(('frames', 'patch')), may hold values from -0.1875 to 0.1875
- up_bias: bfloat16 [4608], P(('frames', 'patch')), may hold values from -2.5 to 2.5
- down_weight: bfloat16 [4608, 1152], P(('frames', 'patch')), may hold values from -0.125 to 0.125
- down_bias: bfloat16 [1152], P(('frames', 'patch')), may hold values from -5 to 5
Outputs:
- output: bfloat16 [16, 1024, 1152], P('frames', 'patch')
- tokens_grad: bfloat16 [16, 1024, 1152], P('frames', 'patch')
- clip_grad: float32 [2, 1152], replicated
- ada_weight_grad: float32 [1152, 6912], P(('frames', 'patch'))
- ada_bias_grad: float32 [6912], P(('frames', 'patch'))
- qkv_weight_grad: float32 [1152, 3456], P(('frames', 'patch'))
- query_bias_grad: float32 [1152], P(('frames', 'patch'))
- value_bias_grad: float32 [1152], P(('frames', 'patch'))
- out_weight_grad: float32 [1152, 1152], P(('frames', 'patch'))
- out_bias_grad: float32 [1152], P(('frames', 'patch'))
- up_weight_grad: float32 [1152, 4608], P(('frames', 'patch'))
- up_bias_grad: float32 [4608], P(('frames', 'patch'))
- down_weight_grad: float32 [4608, 1152], P(('frames', 'patch'))
- down_bias_grad: float32 [1152], P(('frames', 'patch'))
Inputs may be any that keep to these rules, and one draw needn't show every extreme that they name: `frame_clip`: never falls along the frames; every clip has at least one frame.
All inputs are finite; a program needn't handle non-finite values.
Results may differ from a plain program's by a relative error of at most 0.018.
Values may be sent and summed in bfloat16 or wider, within the bound.
A program may use at most 320 MiB of HBM per device.

v0:
```python
import math

import jax
import jax.numpy as jnp
from jax import lax
from jax.sharding import PartitionSpec as P

HEADS = 16
HEAD_DIM = 72


def layer_norm(values_in):
    centre = values_in - jnp.mean(values_in, axis=-1, keepdims=True)
    spread = jnp.mean(centre * centre, axis=-1, keepdims=True)
    inv_std = lax.rsqrt(spread + 1e-06)
    return (centre * inv_std, inv_std)


def norm_back(grad_normed, normed, inv_std):
    mean_grad = jnp.mean(grad_normed, axis=-1, keepdims=True)
    mean_prod = jnp.mean(grad_normed * normed, axis=-1, keepdims=True)
    return (grad_normed - mean_grad - normed * mean_prod) * inv_std


def gelu_tanh(values_in):
    inner = 0.7978845608028654 * (values_in + 0.044715 * values_in * values_in * values_in)
    return 0.5 * values_in * (1.0 + jnp.tanh(inner))


def sinusoid(steps_in, width_in):
    half_width = width_in // 2
    freqs = jnp.exp(-math.log(10000.0) * jnp.arange(half_width, dtype=jnp.float32) / half_width)
    angles = steps_in.astype(jnp.float32)[:, None] * freqs[None, :]
    return jnp.concatenate([jnp.cos(angles), jnp.sin(angles)], axis=1)


def attention_back(queries, keys_full, values_full, grad_mix, log_total, score_scale):
    frame_count, key_rows, model_width = keys_full.shape
    head_count, head_size = (queries.shape[2], queries.shape[3])
    group_count = head_count // 4

    def split_heads(array):
        return jnp.moveaxis(
            array.reshape(array.shape[0], array.shape[1], group_count, 4, head_size), 2, 0
        )

    def one_group(inputs):
        query_grp, key_grp, value_grp, grad_grp, lse_grp, row_grp = inputs
        scores = (
            jnp.einsum("fqhd,fkhd->fhqk", query_grp, key_grp, preferred_element_type=jnp.float32)
            * score_scale
        )
        attn_prob = jnp.exp(scores - lse_grp[..., None])
        grad_prob = jnp.einsum(
            "fqhd,fkhd->fhqk", grad_grp, value_grp, preferred_element_type=jnp.float32
        )
        row_dot = jnp.sum(attn_prob * grad_prob, axis=-1, keepdims=True)
        grad_score = (attn_prob * (grad_prob - row_dot)).astype(jnp.bfloat16)
        grad_key = (
            jnp.einsum("fhqk,fqhd->fkhd", grad_score, query_grp, preferred_element_type=jnp.float32)
            * score_scale
        )
        grad_value = jnp.einsum(
            "fhqk,fqhd->fkhd",
            attn_prob.astype(jnp.bfloat16),
            grad_grp,
            preferred_element_type=jnp.float32,
        )
        grad_query = (
            jnp.einsum("fhqk,fkhd->fqhd", grad_score, key_grp, preferred_element_type=jnp.float32)
            * score_scale
        )
        return (grad_query, grad_key, grad_value)

    row_groups = None
    results = lax.map(
        one_group,
        (
            split_heads(queries),
            split_heads(keys_full),
            split_heads(values_full),
            split_heads(grad_mix),
            jnp.moveaxis(log_total.reshape(frame_count, group_count, 4, log_total.shape[2]), 1, 0),
            row_groups,
        ),
    )

    def join_heads(array):
        moved = jnp.moveaxis(array, 0, 2)
        return moved.reshape(moved.shape[0], moved.shape[1], model_width)

    return tuple((join_heads(item) for item in results))


def per_device(
    tokens,
    cotangent,
    clip_embed,
    timesteps,
    frame_clip,
    ada_weight,
    ada_bias,
    qkv_weight,
    query_bias,
    value_bias,
    out_weight,
    out_bias,
    up_weight,
    up_bias,
    down_weight,
    down_bias,
):
    fr_count, patch_rows, model_width = tokens.shape
    token_rows = fr_count * patch_rows
    head_count = HEADS
    head_size = HEAD_DIM
    score_scale = 1.0 / math.sqrt(head_size)
    gathered = (
        lax.all_gather(ada_weight, ("frames", "patch"), axis=0, tiled=True),
        lax.all_gather(ada_bias, ("frames", "patch"), axis=0, tiled=True),
        lax.all_gather(qkv_weight, ("frames", "patch"), axis=0, tiled=True),
        lax.all_gather(query_bias, ("frames", "patch"), axis=0, tiled=True),
        lax.all_gather(value_bias, ("frames", "patch"), axis=0, tiled=True),
        lax.all_gather(out_weight, ("frames", "patch"), axis=0, tiled=True),
        lax.all_gather(out_bias, ("frames", "patch"), axis=0, tiled=True),
        lax.all_gather(up_weight, ("frames", "patch"), axis=0, tiled=True),
        lax.all_gather(up_bias, ("frames", "patch"), axis=0, tiled=True),
        lax.all_gather(down_weight, ("frames", "patch"), axis=0, tiled=True),
        lax.all_gather(down_bias, ("frames", "patch"), axis=0, tiled=True),
    )
    w_ada, b_ada, w_qkv, b_query, b_value, w_out, b_out, w_up, b_up, w_down, b_down = gathered
    clip_count = clip_embed.shape[0]
    condition = clip_embed + sinusoid(timesteps, model_width)
    silu_cond, silu_back = jax.vjp(jax.nn.silu, condition)
    silu_low = silu_cond.astype(jnp.bfloat16)
    modulation = jnp.dot(silu_low, w_ada, preferred_element_type=jnp.float32) + b_ada.astype(
        jnp.float32
    )
    one_hot = (frame_clip[:, None] == jnp.arange(clip_count, dtype=jnp.int32)[None, :]).astype(
        jnp.float32
    )
    frame_mod = jnp.dot(
        one_hot, modulation, precision=lax.Precision.HIGHEST, preferred_element_type=jnp.float32
    )
    parts = [
        frame_mod[:, None, column * model_width : (column + 1) * model_width] for column in range(6)
    ]
    shift_one, scale_one, gate_one, shift_two, scale_two, gate_two = parts
    input_rows = tokens.astype(jnp.float32)
    normed_one, inv_one = layer_norm(input_rows)
    hidden_one = (
        (normed_one * (1.0 + scale_one) + shift_one)
        .astype(jnp.bfloat16)
        .reshape(token_rows, model_width)
    )
    qkv_bias = jnp.concatenate([b_query, jnp.zeros_like(b_query), b_value]).astype(jnp.float32)
    projected = jnp.dot(hidden_one, w_qkv, preferred_element_type=jnp.float32) + qkv_bias
    queries = (
        projected[:, :model_width]
        .astype(jnp.bfloat16)
        .reshape(fr_count, patch_rows, head_count, head_size)
    )
    keys_local = (
        projected[:, model_width : 2 * model_width]
        .astype(jnp.bfloat16)
        .reshape(fr_count, patch_rows, model_width)
    )
    values_local = (
        projected[:, 2 * model_width :]
        .astype(jnp.bfloat16)
        .reshape(fr_count, patch_rows, model_width)
    )
    run_max = jnp.full((fr_count, head_count, patch_rows), -1e30, jnp.float32)
    key_piece = lax.all_gather(keys_local, "patch", axis=1, tiled=True)
    value_piece = lax.all_gather(values_local, "patch", axis=1, tiled=True)
    piece_rows = key_piece.shape[1]
    key_heads = key_piece.reshape(fr_count, piece_rows, head_count, head_size)
    value_heads = value_piece.reshape(fr_count, piece_rows, head_count, head_size)
    scores = (
        jnp.einsum("fqhd,fkhd->fhqk", queries, key_heads, preferred_element_type=jnp.float32)
        * score_scale
    )
    new_max = jnp.maximum(run_max, jnp.max(scores, axis=-1))
    exp_scores = jnp.exp(scores - new_max[..., None])
    new_total = jnp.sum(exp_scores, axis=-1)
    update = jnp.einsum(
        "fhqk,fkhd->fqhd",
        exp_scores.astype(jnp.bfloat16),
        value_heads,
        preferred_element_type=jnp.float32,
    )
    mixed = update / jnp.transpose(new_total, (0, 2, 1))[..., None]
    log_total = new_max + jnp.log(new_total)
    attended = mixed.reshape(token_rows, model_width).astype(jnp.bfloat16)
    branch_one = (
        jnp.dot(attended, w_out, preferred_element_type=jnp.float32) + b_out.astype(jnp.float32)
    ).reshape(fr_count, patch_rows, model_width)
    midway = input_rows + gate_one * branch_one
    normed_two, inv_two = layer_norm(midway)
    hidden_two = (
        (normed_two * (1.0 + scale_two) + shift_two)
        .astype(jnp.bfloat16)
        .reshape(token_rows, model_width)
    )
    pre_act = jnp.dot(hidden_two, w_up, preferred_element_type=jnp.float32) + b_up.astype(
        jnp.float32
    )
    act_full, gelu_back = jax.vjp(gelu_tanh, pre_act)
    act_low = act_full.astype(jnp.bfloat16)
    branch_two = (
        jnp.dot(act_low, w_down, preferred_element_type=jnp.float32) + b_down.astype(jnp.float32)
    ).reshape(fr_count, patch_rows, model_width)
    output = (midway + gate_two * branch_two).astype(jnp.bfloat16)
    grad_out = cotangent.astype(jnp.float32)
    grad_branch_two = (gate_two * grad_out).astype(jnp.bfloat16).reshape(token_rows, model_width)
    grad_gate_two = jnp.sum(grad_out * branch_two, axis=1)
    g_down_b = jnp.sum(grad_branch_two.astype(jnp.float32), axis=0)
    g_down_w = jnp.dot(act_low.T, grad_branch_two, preferred_element_type=jnp.float32)
    grad_act = jnp.dot(grad_branch_two, w_down.T, preferred_element_type=jnp.float32)
    grad_pre = gelu_back(grad_act)[0].astype(jnp.bfloat16)
    g_up_b = jnp.sum(grad_pre.astype(jnp.float32), axis=0)
    g_up_w = jnp.dot(hidden_two.T, grad_pre, preferred_element_type=jnp.float32)
    grad_hidden_two = jnp.dot(grad_pre, w_up.T, preferred_element_type=jnp.float32).reshape(
        fr_count, patch_rows, model_width
    )
    grad_shift_two = jnp.sum(grad_hidden_two, axis=1)
    grad_scale_two = jnp.sum(grad_hidden_two * normed_two, axis=1)
    grad_midway = grad_out + norm_back(grad_hidden_two * (1.0 + scale_two), normed_two, inv_two)
    grad_gate_one = jnp.sum(grad_midway * branch_one, axis=1)
    grad_branch_one = (gate_one * grad_midway).astype(jnp.bfloat16).reshape(token_rows, model_width)
    g_out_b = jnp.sum(grad_branch_one.astype(jnp.float32), axis=0)
    g_out_w = jnp.dot(attended.T, grad_branch_one, preferred_element_type=jnp.float32)
    grad_mix = (
        jnp.dot(grad_branch_one, w_out.T, preferred_element_type=jnp.float32)
        .astype(jnp.bfloat16)
        .reshape(fr_count, patch_rows, head_count, head_size)
    )
    keys_full, values_full = (
        lax.all_gather(keys_local, "patch", axis=1, tiled=True),
        lax.all_gather(values_local, "patch", axis=1, tiled=True),
    )
    grad_query, key_terms, value_terms = attention_back(
        queries, keys_full, values_full, grad_mix, log_total, score_scale
    )
    key_sum, value_sum = (
        lax.psum_scatter(
            key_terms.astype(jnp.bfloat16), "patch", scatter_dimension=1, tiled=True
        ).astype(jnp.float32),
        lax.psum_scatter(
            value_terms.astype(jnp.bfloat16), "patch", scatter_dimension=1, tiled=True
        ).astype(jnp.float32),
    )
    grad_projected = jnp.concatenate(
        [
            grad_query.astype(jnp.bfloat16),
            key_sum.astype(jnp.bfloat16),
            value_sum.astype(jnp.bfloat16),
        ],
        axis=2,
    ).reshape(token_rows, 3 * model_width)
    g_qkv_w = jnp.dot(hidden_one.T, grad_projected, preferred_element_type=jnp.float32)
    g_query_b = jnp.sum(grad_projected[:, :model_width].astype(jnp.float32), axis=0)
    g_value_b = jnp.sum(grad_projected[:, 2 * model_width :].astype(jnp.float32), axis=0)
    grad_hidden_one = jnp.dot(grad_projected, w_qkv.T, preferred_element_type=jnp.float32).reshape(
        fr_count, patch_rows, model_width
    )
    grad_shift_one = jnp.sum(grad_hidden_one, axis=1)
    grad_scale_one = jnp.sum(grad_hidden_one * normed_one, axis=1)
    tokens_grad = (
        grad_midway + norm_back(grad_hidden_one * (1.0 + scale_one), normed_one, inv_one)
    ).astype(jnp.bfloat16)
    frame_grads = jnp.concatenate(
        [
            grad_shift_one,
            grad_scale_one,
            grad_gate_one,
            grad_shift_two,
            grad_scale_two,
            grad_gate_two,
        ],
        axis=1,
    )
    clip_terms = jnp.dot(
        one_hot.T, frame_grads, precision=lax.Precision.HIGHEST, preferred_element_type=jnp.float32
    )
    mod_total = lax.psum(clip_terms, ("frames", "patch"))
    mod_low = mod_total.astype(jnp.bfloat16)
    device_count = lax.axis_size(("frames", "patch"))
    shard_index = lax.axis_index(("frames", "patch"))
    ada_rows = model_width // device_count
    bias_rows = 6 * model_width // device_count
    ada_bias_full = jnp.sum(mod_low.astype(jnp.float32), axis=0)
    ada_bias_grad = lax.dynamic_slice_in_dim(ada_bias_full, shard_index * bias_rows, bias_rows, 0)
    silu_part = lax.dynamic_slice_in_dim(silu_low, shard_index * ada_rows, ada_rows, 1)
    ada_weight_grad = jnp.dot(silu_part.T, mod_low, preferred_element_type=jnp.float32)
    grad_silu = jnp.dot(mod_low, w_ada.T, preferred_element_type=jnp.float32)
    clip_grad = silu_back(grad_silu)[0]
    all_shares = (
        lax.psum_scatter(g_qkv_w, ("frames", "patch"), scatter_dimension=0, tiled=True),
        lax.psum_scatter(g_query_b, ("frames", "patch"), scatter_dimension=0, tiled=True),
        lax.psum_scatter(g_value_b, ("frames", "patch"), scatter_dimension=0, tiled=True),
        lax.psum_scatter(g_out_w, ("frames", "patch"), scatter_dimension=0, tiled=True),
        lax.psum_scatter(g_out_b, ("frames", "patch"), scatter_dimension=0, tiled=True),
        lax.psum_scatter(g_up_w, ("frames", "patch"), scatter_dimension=0, tiled=True),
        lax.psum_scatter(g_up_b, ("frames", "patch"), scatter_dimension=0, tiled=True),
        lax.psum_scatter(g_down_w, ("frames", "patch"), scatter_dimension=0, tiled=True),
        lax.psum_scatter(g_down_b, ("frames", "patch"), scatter_dimension=0, tiled=True),
    )
    (
        share_qkv_w,
        share_query_b,
        share_value_b,
        share_out_w,
        share_out_b,
        share_up_w,
        share_up_b,
        share_down_w,
        share_down_b,
    ) = all_shares
    return (
        output,
        tokens_grad,
        clip_grad,
        ada_weight_grad,
        ada_bias_grad,
        share_qkv_w,
        share_query_b,
        share_value_b,
        share_out_w,
        share_out_b,
        share_up_w,
        share_up_b,
        share_down_w,
        share_down_b,
    )


def solution(mesh):
    placed = (
        P("frames", "patch", None),
        P("frames", "patch", None),
        P(),
        P(),
        P("frames"),
        P(("frames", "patch"), None),
        P(("frames", "patch")),
        P(("frames", "patch"), None),
        P(("frames", "patch")),
        P(("frames", "patch")),
        P(("frames", "patch"), None),
        P(("frames", "patch")),
        P(("frames", "patch"), None),
        P(("frames", "patch")),
        P(("frames", "patch"), None),
        P(("frames", "patch")),
    )
    return jax.shard_map(
        per_device,
        mesh=mesh,
        in_specs=placed,
        out_specs=(
            P("frames", "patch", None),
            P("frames", "patch", None),
            P(),
            P(("frames", "patch"), None),
            P(("frames", "patch")),
            P(("frames", "patch"), None),
            P(("frames", "patch")),
            P(("frames", "patch")),
            P(("frames", "patch"), None),
            P(("frames", "patch")),
            P(("frames", "patch"), None),
            P(("frames", "patch")),
            P(("frames", "patch"), None),
            P(("frames", "patch")),
        ),
        check_vma=False,
    )
```

profile of v0, /device:TPU:0, one launch (start us, length us, event | category | flops | bytes accessed | tf_op | source)
XLA Modules:
  0.0 2146.1 jit_solution(10805961783603189588)
XLA Ops:
  15.8 43.2 %all-reduce.18 = (bf16[1152]{0:T(1024)(128)(2,1)S(1)}, bf16[1152]{0:T(1024)(128)(2,1)S(1)}, bf16[6912]{0:T(1024)(128)(2,1)S(1)}, bf16[1152]{0:T(1024)(128)(2,1)S...) all-reduce(bf16[1152]{0:T(1024)(128)(2,1)S(1)} %dynamic-update-slic, ...), channel_id=1, replica_groups=mesh['frames'=16,'patch'=2] {'frames','patch'}, use_global_device_ids=true, to_apply=%add.2 | all-reduce | flops 16128 | bytes 64512
  62.6 30.7 %all-gather.22.cloned.1.call-done = bf16[32,36,3456]{2,1,0:T(8,128)(2,1)} async-done(((bf16[1,36,3456]{2,1,0:T(8,128)(2,1)}), bf16[32,36,3456]{2,1,0:T(8,128)(2,1)}) %all-gather.22.cloned.1.call-update) | async-done | bytes 7962640 | tf_op jit(solution)/shard_map/all_gather | solution.py:121
  105.8 108.3 %all-gather.20.cloned.1.call-done = bf16[32,36,6912]{2,1,0:T(8,128)(2,1)} async-done(((bf16[1,36,6912]{2,1,0:T(8,128)(2,1)}), bf16[32,36,6912]{2,1,0:T(8,128)(2,1)}) %all-gather.20.cloned.1.call-update) | async-done | bytes 15925264 | tf_op jit(solution)/shard_map/all_gather | solution.py:119
  214.1 18.4 reshape.458
  251.8 22.3 %all-gather.24.cloned.1.call-done = bf16[32,36,1152]{2,1,0:T(8,128)(2,1)} async-done(((bf16[1,36,1152]{2,1,0:T(8,128)(2,1)}), bf16[32,36,1152]{2,1,0:T(8,128)(2,1)}) %all-gather.24.cloned.1.call-update) | async-done | bytes 2654224 | tf_op jit(solution)/shard_map/all_gather | solution.py:124
  279.5 88.6 %all-gather.26.cloned.1.call-done = bf16[32,36,4608]{2,1,0:T(8,128)(2,1)} async-done(((bf16[1,36,4608]{2,1,0:T(8,128)(2,1)}), bf16[32,36,4608]{2,1,0:T(8,128)(2,1)}) %all-gather.26.cloned.1.call-update) | async-done | bytes 10616848 | tf_op jit(solution)/shard_map/all_gather | solution.py:126
  368.0 14.3 reshape.464
  382.9 21.5 %all-gather.16.cloned.1.call-done = bf16[1024,1152]{1,0:T(8,128)(2,1)} async-done(((bf16[512,1152]{1,0:T(8,128)(2,1)}), bf16[1024,1152]{1,0:T(8,128)(2,1)}) %all-gather.16.cloned.1.call-update) | async-done | bytes 2359312 | tf_op jit(solution)/shard_map/all_gather | solution.py:175
  408.7 33.8 %all-gather.18.cloned.1.call-done = bf16[1024,1152]{1,0:T(8,128)(2,1)} async-done(((bf16[512,1152]{1,0:T(8,128)(2,1)}), bf16[1024,1152]{1,0:T(8,128)(2,1)}) %all-gather.18.cloned.1.call-update) | async-done | bytes 2359312 | tf_op jit(solution)/shard_map/all_gather | solution.py:174
  458.9 14.9 fusion.40
  473.8 15.6 fusion.69
  496.8 13.8 fusion.109
  510.6 22.2 %all-gather.14.cloned.1.call-done = bf16[4608,1152]{1,0:T(8,128)(2,1)} async-done(((bf16[144,1152]{1,0:T(8,128)(2,1)}), bf16[4608,1152]{1,0:T(8,128)(2,1)}) %all-gather.14.cloned.1.call-update) | async-done | bytes 10616848 | tf_op jit(solution)/shard_map/all_gather | solution.py:128
  532.8 18.3 convert_reduce_fusion
  566.1 15.7 fusion.68
  592.1 60.3 %while.14 = (s32[]{:T(128)}, bf16[4,1,512,4,72]{2,4,3,1,0:T(8,128)(2,1)}, bf16[4,1,1024,4,72]{2,4,3,1,0:T(8,128)(2,1)}, bf16[4,1,1024,4,72]{2,4,3,1,0:T(8,128)(2...) while((s32[]{:T(128)}, ...), condition=%wide.region_10.11_spmd, body=%wide.region_8.0_spmd.sunk | while | flops 1535555584 | bytes 120780096 | solution.py:76
  653.7 14.8 fusion.81
  686.8 36.0 %reduce-scatter.10.cloned.1.call-done = bf16[1,512,1152]{1,2,0:T(8,128)(2,1)} async-done(((bf16[1,1024,1152]{1,2,0:T(8,128)(2,1)}), bf16[1,512,1152]{1,2,0:T(8,128)(2,1)}) %reduce-scatter.10.cloned.1.call-update) | async-done | bytes 1179664 | tf_op jit(solution)/shard_map/reduce_scatter | solution.py:246
  735.1 1110.5 %fusion.116 = (f32[48,3456]{1,0:T(8,128)S(1)}, f32[48,1152]{1,0:T(8,128)S(1)}, f32[40,4608]{1,0:T(8,128)S(1)}) fusion(f32[1152,3456]{1,0:T(8,128)} %fusion.104, f32[1152,1152]{1,0:T(8,128)} %fusion.120, f32[1152,4608]{1,0:T(8,128)} %fusion.107), kind=kCustom, calls=%all-reduce-scatter.3 | all-reduce-scatter fusion | flops 12976130 | bytes 44089344
  1846.4 32.2 %collective-permute-start.14 = (f32[48,1152]{1,0:T(8,128)S(1)}, f32[48,1152]{1,0:T(8,128)}, u32[]{:S(2)}, u32[]{:S(2)}) collective-permute-start(f32[48,1152]{1,0:T(8,128)S(1)} %get-tuple-element.143), channel_id=1, source_target_pairs={{0,7},{1,8},{2,9},{3,10},{4,11},{5,12},{6,13},{7,14},{8,15},{9,16}... | collective-permute-start | bytes 663560
  1942.1 51.0 %all-reduce.17 = (bf16[2,6912]{1,0:T(2,128)(2,1)S(1)}, f32[1152]{0:T(1024)S(1)}, f32[1152]{0:T(1024)S(1)}, f32[1152]{0:T(1024)S(1)}, f32[4608]{0:T(1024)S(1)}, /*index=5*/f32[1152]{0:T(1024)S(1)}) all-reduce(f32[2,6912]{1,0:T(2,128)S(1)} %broadcast_multiply_fusion, ...), channel_id=1, replica_groups=mesh['frames'=16,'patch'=2] {'frames','patch'}, use_global_device_ids=true, to_apply=%region_21.22 | all-reduce | flops 23040 | bytes 156672 | tf_op jit(solution)/shard_map/psum | solution.py:286
  2023.6 32.5 %collective-permute-done.3 = f32[48,3456]{1,0:T(8,128)S(1)} collective-permute-done((f32[48,3456]{1,0:T(8,128)S(1)}, f32[48,3456]{1,0:T(8,128)S(1)}, u32[]{:S(2)}, u32[]{:S(2)}) %collective-permute-start.3) | collective-permute-done | bytes 663584
  2063.9 14.8 concatenate.21
  2084.6 36.7 %concatenate.20 = f32[420,3456]{1,0:T(8,128)} concatenate(f32[36,3456]{1,0:T(8,128)} %collective-permute-done.7, f32[48,3456]{1,0:T(8,128)} %copy-done.26, f32[48,3456]{1,0:T(8,128)} %copy-done.27, f32[48,3456]{1,0:T(8,128)} %copy-done.28, f32[48,3456]{1,0:T(8,128)} %copy-done.29, f32[48,3456]{1,0:T(8,128)} %copy-done.30, f32[48,3456]{1,0:T(8,128)} %collective-permute-done.1, ...), dimensions={0} | concatenate | bytes 11612160
  (361 shorter events, 319.5 us)
Async XLA Ops:
  7.2 86.1 %all-gather.22.cloned.1.call-start = ((), (), s32[]{:S(2)}) async-start(), calls=%async_computation.10 | async-start | bytes 9123840 | tf_op jit(solution)/shard_map/all_gather | solution.py:121
  7.9 206.2 %all-gather.20.cloned.1.call-start = ((), (), s32[]{:S(2)}) async-start(), calls=%async_computation.9 | async-start | bytes 18247680 | tf_op jit(solution)/shard_map/all_gather | solution.py:119
  8.7 265.4 %all-gather.24.cloned.1.call-start = ((), (), s32[]{:S(2)}) async-start(), calls=%async_computation.11 | async-start | bytes 3041280 | tf_op jit(solution)/shard_map/all_gather | solution.py:124
  9.4 358.6 %all-gather.26.cloned.1.call-start = ((), (), s32[]{:S(2)}) async-start(), calls=%async_computation.12 | async-start | bytes 12165120 | tf_op jit(solution)/shard_map/all_gather | solution.py:126
  10.0 394.4 %all-gather.16.cloned.1.call-start = ((), (), s32[]{:S(2)}) async-start(), calls=%async_computation.7 | async-start | bytes 3538944 | tf_op jit(solution)/shard_map/all_gather | solution.py:175
  249.2 193.4 %all-gather.18.cloned.1.call-start = ((), (), s32[]{:S(2)}) async-start(), calls=%async_computation.8 | async-start | bytes 3538944 | tf_op jit(solution)/shard_map/all_gather | solution.py:174
  249.7 283.1 %all-gather.14.cloned.1.call-start = ((), (), s32[]{:S(2)}) async-start(), calls=%async_computation.3 | async-start | bytes 10948608 | tf_op jit(solution)/shard_map/all_gather | solution.py:128
  250.5 436.4 %reduce-scatter.12.cloned.1.call-start = ((), (), s32[]{:S(2)}) async-start(), calls=%async_computation.5 | async-start | bytes 3538944 | tf_op jit(solution)/shard_map/reduce_scatter | solution.py:249
  652.4 70.4 %reduce-scatter.10.cloned.1.call-start = ((), (), s32[]{:S(2)}) async-start(), calls=%async_computation.4 | async-start | bytes 3538944 | tf_op jit(solution)/shard_map/reduce_scatter | solution.py:246
  653.2 1485.7 %reduce-scatter.14.cloned.1.call-start = ((), (), s32[]{:S(2)}) async-start(), calls=%async_computation.6 | async-start | bytes 21897216 | tf_op jit(solution)/shard_map/reduce_scatter | solution.py:306
  1846.4 73.7 %collective-permute-start.14 = (f32[48,1152]{1,0:T(8,128)S(1)}, f32[48,1152]{1,0:T(8,128)}, u32[]{:S(2)}, u32[]{:S(2)}) collective-permute-start(f32[48,1152]{1,0:T(8,128)S(1)} %get-tuple-element.143), channel_id=1, source_target_pairs={{0,7},{1,8},{2,9},{3,10},{4,11},{5,12},{6,13},{7,14},{8,15},{9,16}... | collective-permute-start | bytes 663560
  1878.5 42.9 %collective-permute-start.13 = (f32[48,1152]{1,0:T(8,128)S(1)}, f32[48,1152]{1,0:T(8,128)}, u32[]{:S(2)}, u32[]{:S(2)}) collective-permute-start(f32[48,1152]{1,0:T(8,128)S(1)} %get-tuple-element.143), channel_id=1, source_target_pairs={{0,6},{1,7},{2,8},{3,9},{4,10},{5,11},{6,12},{7,13},{8,14},{9,15},... | collective-permute-start | bytes 663560
  1893.8 108.3 %collective-permute-start.6 = (f32[48,3456]{1,0:T(8,128)S(1)}, f32[48,3456]{1,0:T(8,128)S(1)}, u32[]{:S(2)}, u32[]{:S(2)}) collective-permute-start(f32[48,3456]{1,0:T(8,128)S(1)} %get-tuple-element.142), channel_id=1, source_target_pairs={{0,7},{1,8},{2,9},{3,10},{4,11},{5,12},{6,13},{7,14},{8,15},{9,16}... | collective-permute-start | bytes 1990664
  1911.9 93.0 %collective-permute-start.5 = (f32[48,3456]{1,0:T(8,128)S(1)}, f32[48,3456]{1,0:T(8,128)S(1)}, u32[]{:S(2)}, u32[]{:S(2)}) collective-permute-start(f32[48,3456]{1,0:T(8,128)S(1)} %get-tuple-element.142), channel_id=1, source_target_pairs={{0,6},{1,7},{2,8},{3,9},{4,10},{5,11},{6,12},{7,13},{8,14},{9,15},... | collective-permute-start | bytes 1990664
  1927.2 72.9 %collective-permute-start.7 = (f32[36,3456]{1,0:T(8,128)}, f32[36,3456]{1,0:T(8,128)}, u32[]{:S(2)}, u32[]{:S(2)}) collective-permute-start(f32[36,3456]{1,0:T(8,128)} %slice.58), channel_id=1, source_target_pairs={{0,8},{1,9},{2,10},{3,11},{4,12},{5,13},{6,14},{7,15},{8,16},{9,17... | collective-permute-start | bytes 1493000
  1937.7 55.4 %collective-permute-start.9 = (f32[48,1152]{1,0:T(8,128)S(1)}, f32[48,1152]{1,0:T(8,128)}, u32[]{:S(2)}, u32[]{:S(2)}) collective-permute-start(f32[48,1152]{1,0:T(8,128)S(1)} %get-tuple-element.143), channel_id=1, source_target_pairs={{0,2},{1,3},{2,4},{3,5},{4,6},{5,7},{6,8},{7,9},{8,10},{9,11},{10,... | collective-permute-start | bytes 663560
  1939.7 58.2 %collective-permute-start.8 = (f32[48,1152]{1,0:T(8,128)S(1)}, f32[48,1152]{1,0:T(8,128)}, u32[]{:S(2)}, u32[]{:S(2)}) collective-permute-start(f32[48,1152]{1,0:T(8,128)S(1)} %get-tuple-element.143), channel_id=1, source_target_pairs={{0,1},{1,2},{2,3},{3,4},{4,5},{5,6},{6,7},{7,8},{8,9},{9,10},{10,1... | collective-permute-start | bytes 663560
  1997.9 58.3 %collective-permute-start.3 = (f32[48,3456]{1,0:T(8,128)S(1)}, f32[48,3456]{1,0:T(8,128)S(1)}, u32[]{:S(2)}, u32[]{:S(2)}) collective-permute-start(f32[48,3456]{1,0:T(8,128)S(1)} %get-tuple-element.142), channel_id=1, source_target_pairs={{0,4},{1,5},{2,6},{3,7},{4,8},{5,9},{6,10},{7,11},{8,12},{9,13},{1... | collective-permute-start | bytes 1990664
  2000.1 57.9 %collective-permute-start.2 = (f32[48,3456]{1,0:T(8,128)S(1)}, f32[48,3456]{1,0:T(8,128)S(1)}, u32[]{:S(2)}, u32[]{:S(2)}) collective-permute-start(f32[48,3456]{1,0:T(8,128)S(1)} %get-tuple-element.142), channel_id=1, source_target_pairs={{0,3},{1,4},{2,5},{3,6},{4,7},{5,8},{6,9},{7,10},{8,11},{9,12},{10... | collective-permute-start | bytes 1990664
  2002.1 78.3 %collective-permute-start.1 = (f32[48,3456]{1,0:T(8,128)S(1)}, f32[48,3456]{1,0:T(8,128)}, u32[]{:S(2)}, u32[]{:S(2)}) collective-permute-start(f32[48,3456]{1,0:T(8,128)S(1)} %get-tuple-element.142), channel_id=1, source_target_pairs={{0,2},{1,3},{2,4},{3,5},{4,6},{5,7},{6,8},{7,9},{8,10},{9,11},{10,... | collective-permute-start | bytes 1990664
  2004.9 79.6 %collective-permute-start = (f32[48,3456]{1,0:T(8,128)S(1)}, f32[48,3456]{1,0:T(8,128)}, u32[]{:S(2)}, u32[]{:S(2)}) collective-permute-start(f32[48,3456]{1,0:T(8,128)S(1)} %get-tuple-element.142), channel_id=1, source_target_pairs={{0,1},{1,2},{2,3},{3,4},{4,5},{5,6},{6,7},{7,8},{8,9},{9,10},{10,1... | collective-permute-start | bytes 1990664
  2022.0 101.2 %collective-permute-start.18 = (f32[40,4608]{1,0:T(8,128)S(1)}, f32[40,4608]{1,0:T(8,128)S(1)}, u32[]{:S(2)}, u32[]{:S(2)}) collective-permute-start(f32[40,4608]{1,0:T(8,128)S(1)} %get-tuple-element.144), channel_id=1, source_target_pairs={{0,3},{1,4},{2,5},{3,6},{4,7},{5,8},{6,9},{7,10},{8,11},{9,12},{10... | collective-permute-start | bytes 2211848
  2056.1 67.1 %collective-permute-start.17 = (f32[40,4608]{1,0:T(8,128)S(1)}, f32[40,4608]{1,0:T(8,128)S(1)}, u32[]{:S(2)}, u32[]{:S(2)}) collective-permute-start(f32[40,4608]{1,0:T(8,128)S(1)} %get-tuple-element.144), channel_id=1, source_target_pairs={{0,2},{1,3},{2,4},{3,5},{4,6},{5,7},{6,8},{7,9},{8,10},{9,11},{10,... | collective-permute-start | bytes 2211848
  2058.0 67.0 %collective-permute-start.16 = (f32[40,4608]{1,0:T(8,128)S(1)}, f32[40,4608]{1,0:T(8,128)}, u32[]{:S(2)}, u32[]{:S(2)}) collective-permute-start(f32[40,4608]{1,0:T(8,128)S(1)} %get-tuple-element.144), channel_id=1, source_target_pairs={{0,1},{1,2},{2,3},{3,4},{4,5},{5,6},{6,7},{7,8},{8,9},{9,10},{10,1... | collective-permute-start | bytes 2211848
  (99 other events, 1912.9 us)
Sparse Core Ops, SparseCore 0:
  11.0 82.2 all-gather.21
  96.2 117.8 all-gather.19
  217.0 57.0 all-gather.23
  276.9 91.1 all-gather.25
  370.0 34.3 all-gather.15
  406.4 36.0 all-gather.17
  445.4 87.3 all-gather.13
  652.6 33.1 reduce-scatter.11
  688.1 34.7 reduce-scatter.9
  729.7 272.5 reduce-scatter.13
where the time goes:
time: 2160 us; the launch traced here: 2150 us
  blocking collectives  1200 us (56%)
  waiting for transfers between devices  406 us (19%)
  matrix products  213 us (10%)
  local copies, waits for them, and re-layouts  169 us (8%)
  starting transfers between devices  99.3 us (5%)
  other arithmetic  38 us (2%)
    unnamed x2, blocking collectives  1150 us
    unnamed x166, local copies, waits for them, and re-layouts  139 us
    all_gather x1, waiting for transfers between devices, per_device(): lax.all_gather(ada_weight, ('frames', 'patch'), axis=0, tiled=True)  108 us
    unnamed x20, starting transfers between devices  98.9 us
    all_gather x1, waiting for transfers between devices, per_device(): lax.all_gather(up_weight, ('frames', 'patch'), axis=0, tiled=True)  88.6 us
    psum x1, blocking collectives, per_device(): mod_total = lax.psum(clip_terms, ('frames', 'patch'))  51 us
  transfers between devices with their start and end apart: 30, of which 10 were waited for; matrix products, arithmetic and copies ran while one was open for 65% of the time, Pallas kernels for 0%

commit v1 on v0

v1 whole, which is shorter than its diff:
```python
import functools
import math

import jax
import jax.numpy as jnp
from jax import lax
from jax.experimental import pallas as pl
from jax.experimental.pallas import tpu as pltpu
from jax.sharding import Mesh
from jax.sharding import PartitionSpec as P

HEADS = 16
HEAD_DIM = 72
BF16 = jnp.bfloat16
F32 = jnp.float32
LOG2E = 1.4426950408889634
MESH_ID = pl.DeviceIdType.MESH
MIB = 2**20


def layer_norm(values_in):
    centre = values_in - jnp.mean(values_in, axis=-1, keepdims=True)
    spread = jnp.mean(centre * centre, axis=-1, keepdims=True)
    inv_std = lax.rsqrt(spread + 1e-06)
    return (centre * inv_std, inv_std)


def norm_back(grad_normed, normed, inv_std):
    mean_grad = jnp.mean(grad_normed, axis=-1, keepdims=True)
    mean_prod = jnp.mean(grad_normed * normed, axis=-1, keepdims=True)
    return (grad_normed - mean_grad - normed * mean_prod) * inv_std


def gelu_tanh(values_in):
    inner = 0.7978845608028654 * (values_in + 0.044715 * values_in * values_in * values_in)
    return 0.5 * values_in * (1.0 + jnp.tanh(inner))


def sinusoid(steps_in, width_in):
    half_width = width_in // 2
    freqs = jnp.exp(-math.log(10000.0) * jnp.arange(half_width, dtype=jnp.float32) / half_width)
    angles = steps_in.astype(jnp.float32)[:, None] * freqs[None, :]
    return jnp.concatenate([jnp.cos(angles), jnp.sin(angles)], axis=1)


def ring_place(index, size):
    along, across = index // 2, index % 2
    return (1 - across) * along + across * (size - 1 - along)


def ring_index(place, size):
    place = (place + 2 * size) % size
    back = place // (size // 2)
    return (1 - back) * 2 * place + back * (2 * (size - 1 - place) + 1)


def ring_peers(size):
    ring, core, patch = (lax.axis_index(name) for name in ("ring", "core", "patch"))
    place = ring_place(ring, size)
    right = (ring_index(place + 1, size), core, patch)
    left = (ring_index(place - 1, size), core, patch)
    return ring, place, right, left


def greet(peers):
    barrier = pltpu.get_barrier_semaphore()
    for peer in peers:
        pl.semaphore_signal(barrier, inc=1, device_id=peer, device_id_type=MESH_ID)
    pl.semaphore_wait(barrier, len(peers))


def halves(rows, columns):
    if rows % 16 == 0:
        cut = -(-rows // 32) * 16
        return (pl.ds(0, cut), slice(None)), (pl.ds(cut, rows - cut), slice(None))
    cut = -(-columns // 256) * 128
    return (slice(None), pl.ds(0, cut)), (slice(None), pl.ds(cut, columns - cut))


def ring_gather_kernel(size, count, *refs):
    ins, outs = refs[:count], refs[count : 2 * count]
    send_sem, recv_sem, local_sem = refs[2 * count :]
    ring, place, right, left = ring_peers(size)
    greet([right, left])
    local = [
        pltpu.make_async_copy(ins[at], outs[at].at[ring], local_sem.at[at]) for at in range(count)
    ]
    for copy in local:
        copy.start()
    copies = {}
    for step in range(size - 1):
        for at in range(count):
            parts = halves(*ins[at].shape)
            for way, (part, peer, sign) in enumerate(zip(parts, (right, left), (-1, 1))):
                slot = ring_index(place + sign * step, size)
                if step:
                    copies[at, way, step - 1].wait_recv()
                    source = outs[at].at[(slot,) + part]
                else:
                    source = ins[at].at[part]
                copy = pltpu.make_async_remote_copy(
                    src_ref=source,
                    dst_ref=outs[at].at[(slot,) + part],
                    send_sem=send_sem.at[at, way, step],
                    recv_sem=recv_sem.at[at, way, step],
                    device_id=peer,
                    device_id_type=MESH_ID,
                )
                copy.start()
                copies[at, way, step] = copy
    for (at, way, step), copy in copies.items():
        if step == size - 2:
            copy.wait_recv()
        copy.wait_send()
    for copy in local:
        copy.wait()


def ring_gather(blocks, size, call_id):
    count = len(blocks)
    space = pl.BlockSpec(memory_space=pl.ANY)
    moved = sum(block.size * 2 * size for block in blocks)
    return pl.pallas_call(
        functools.partial(ring_gather_kernel, size, count),
        out_shape=[jax.ShapeDtypeStruct((size,) + block.shape, block.dtype) for block in blocks],
        in_specs=[space] * count,
        out_specs=[space] * count,
        scratch_shapes=[
            pltpu.SemaphoreType.DMA((count, 2, size - 1)),
            pltpu.SemaphoreType.DMA((count, 2, size - 1)),
            pltpu.SemaphoreType.DMA((count,)),
        ],
        compiler_params=pltpu.CompilerParams(collective_id=call_id, has_side_effects=True),
        cost_estimate=pl.CostEstimate(flops=0, bytes_accessed=moved * 12, transcendentals=0),
        name=f"ring_gather_{call_id}",
    )(*blocks)


def ring_sum_kernel(size, count, *refs):
    ins, outs = refs[:count], refs[count : 2 * count]
    held, landed = refs[2 * count : 3 * count], refs[3 * count : 4 * count]
    send_sem, recv_sem = refs[4 * count :]
    ring, place, right, left = ring_peers(size)
    greet([right, left])
    copies = {}
    for step in range(size):
        for at in range(count):
            parts = halves(*ins[at].shape[1:])
            for way, (part, peer, sign) in enumerate(zip(parts, (right, left), (-1, 1))):
                slot = ring_index(place + sign * (step + 1), size)
                total = ins[at][(slot,) + part]
                if step:
                    copies[at, way, step - 1].wait_recv()
                    total = total.astype(F32) + landed[at][(step - 1,) + part].astype(F32)
                if step == size - 1:
                    outs[at][part] = total.astype(outs[at].dtype)
                    continue
                held[at][(step,) + part] = total.astype(BF16)
                copy = pltpu.make_async_remote_copy(
                    src_ref=held[at].at[(step,) + part],
                    dst_ref=landed[at].at[(step,) + part],
                    send_sem=send_sem.at[at, way, step],
                    recv_sem=recv_sem.at[at, way, step],
                    device_id=peer,
                    device_id_type=MESH_ID,
                )
                copy.start()
                copies[at, way, step] = copy
    for copy in copies.values():
        copy.wait_send()


def ring_sum(blocks, dtypes, size, call_id):
    count = len(blocks)
    space = pl.BlockSpec(memory_space=pltpu.VMEM)
    moved = sum(block.size * 2 for block in blocks)
    slots = [pltpu.VMEM((size - 1,) + block.shape[1:], BF16) for block in blocks]
    return pl.pallas_call(
        functools.partial(ring_sum_kernel, size, count),
        out_shape=[
            jax.ShapeDtypeStruct(block.shape[1:], dtype)
            for block, dtype in zip(blocks, dtypes)
        ],
        in_specs=[space] * count,
        out_specs=[space] * count,
        scratch_shapes=slots
        + slots
        + [
            pltpu.SemaphoreType.DMA((count, 2, size - 1)),
            pltpu.SemaphoreType.DMA((count, 2, size - 1)),
        ],
        compiler_params=pltpu.CompilerParams(
            collective_id=call_id, has_side_effects=True, vmem_limit_bytes=40 * MIB
        ),
        cost_estimate=pl.CostEstimate(flops=0, bytes_accessed=moved * 12, transcendentals=0),
        name=f"ring_sum_{call_id}",
    )(*blocks)


def sum_bits(sizes):
    bits = []
    for axis, size in enumerate(sizes):
        bit = 1
        while bit < size:
            bits.append((axis, bit))
            bit *= 2
    return bits


def all_sum_kernel(bits, in_ref, out_ref, held, landed, send_sem, recv_sem):
    here = [lax.axis_index(name) for name in ("ring", "core", "patch")]
    peers = []
    for axis, bit in bits:
        peer = list(here)
        peer[axis] = here[axis] + (1 - 2 * ((here[axis] // bit) % 2)) * bit
        peers.append(tuple(peer))
    greet(peers)
    held[0] = in_ref[...]
    for step, peer in enumerate(peers):
        copy = pltpu.make_async_remote_copy(
            src_ref=held.at[step],
            dst_ref=landed.at[step],
            send_sem=send_sem.at[step],
            recv_sem=recv_sem.at[step],
            device_id=peer,
            device_id_type=MESH_ID,
        )
        copy.start()
        copy.wait()
        total = held[step] + landed[step]
        if step == len(peers) - 1:
            out_ref[...] = total
        else:
            held[step + 1] = total


def all_sum(vector, sizes, call_id):
    length = vector.shape[0]
    rows = -(-length // 1024) * 8
    block = jnp.pad(vector, (0, rows * 128 - length)).reshape(rows, 128)
    bits = sum_bits(sizes)
    space = pl.BlockSpec(memory_space=pltpu.VMEM)
    total = pl.pallas_call(
        functools.partial(all_sum_kernel, bits),
        out_shape=jax.ShapeDtypeStruct(block.shape, F32),
        in_specs=[space],
        out_specs=space,
        scratch_shapes=[
            pltpu.VMEM((len(bits), rows, 128), F32),
            pltpu.VMEM((len(bits), rows, 128), F32),
            pltpu.SemaphoreType.DMA((len(bits),)),
            pltpu.SemaphoreType.DMA((len(bits),)),
        ],
        compiler_params=pltpu.CompilerParams(collective_id=call_id, has_side_effects=True),
        name=f"all_sum_{call_id}",
    )(block)
    return total.reshape(rows * 128)[:length]


def attention_kernel(factor, chunk, q_ref, k_ref, v_ref, out_ref, lse_ref):
    keys = k_ref[0].T
    values_t = v_ref[0]
    for start in range(0, q_ref.shape[2], chunk):
        span = slice(start, start + chunk)
        scores = jnp.dot(keys, q_ref[0, :, span], preferred_element_type=F32) * factor
        top = jnp.max(scores, axis=0, keepdims=True)
        probs = jnp.exp2(scores - top)
        total = jnp.sum(probs, axis=0, keepdims=True)
        mixed = jnp.dot(values_t, probs.astype(BF16), preferred_element_type=F32)
        out_ref[0, :, span] = (mixed / total).astype(BF16)
        lse_ref[0, :, span] = top + jnp.log2(total)


def attention(qkv, patches):
    triple, dim, tokens = qkv.shape
    heads = triple // 3
    frames = tokens // patches
    block = (1, dim, patches)
    factor = LOG2E / math.sqrt(HEAD_DIM)
    return pl.pallas_call(
        functools.partial(attention_kernel, factor, min(256, patches)),
        out_shape=[
            jax.ShapeDtypeStruct((heads, dim, tokens), BF16),
            jax.ShapeDtypeStruct((heads, 1, tokens), F32),
        ],
        grid=(frames, heads),
        in_specs=[
            pl.BlockSpec(block, lambda f, h: (h, 0, f)),
            pl.BlockSpec(block, lambda f, h: (heads + h, 0, f)),
            pl.BlockSpec(block, lambda f, h: (2 * heads + h, 0, f)),
        ],
        out_specs=[
            pl.BlockSpec(block, lambda f, h: (h, 0, f)),
            pl.BlockSpec((1, 1, patches), lambda f, h: (h, 0, f)),
        ],
        compiler_params=pltpu.CompilerParams(vmem_limit_bytes=32 * MIB),
        cost_estimate=pl.CostEstimate(
            flops=4 * heads * patches * tokens * 256,
            bytes_accessed=4 * heads * dim * tokens * 2,
            transcendentals=heads * patches * tokens,
        ),
        name="attention",
    )(qkv, qkv, qkv)


def attention_back_kernel(
    factor, chunk, q_ref, k_ref, v_ref, g_ref, lse_ref, dq_ref, dk_ref, dv_ref, dk_sum, dv_sum
):
    keys_t = k_ref[0]
    keys = keys_t.T
    values = v_ref[0].T
    scale = factor / LOG2E
    patches = q_ref.shape[2]
    for start in range(0, patches, chunk):
        span = slice(start, start + chunk)
        queries_t = q_ref[0, :, span]
        grad_t = g_ref[0, :, span]
        scores = jnp.dot(keys, queries_t, preferred_element_type=F32) * factor
        probs = jnp.exp2(scores - lse_ref[0, :, span])
        grad_probs = jnp.dot(values, grad_t, preferred_element_type=F32)
        row_dot = jnp.sum(probs * grad_probs, axis=0, keepdims=True)
        grad_scores = (probs * (grad_probs - row_dot)).astype(BF16)
        probs_low = probs.astype(BF16)
        dq = jnp.dot(keys_t, grad_scores, preferred_element_type=F32)
        dq_ref[0, :, span] = (dq * scale).astype(BF16)
        dims = (((1,), (1,)), ((), ()))
        dk = lax.dot_general(queries_t, grad_scores, dims, preferred_element_type=F32)
        dv = lax.dot_general(grad_t, probs_low, dims, preferred_element_type=F32)
        if start == 0:
            dk_sum[...] = dk
            dv_sum[...] = dv
        else:
            dk_sum[...] += dk
            dv_sum[...] += dv
    dk_ref[0] = (dk_sum[...] * scale).astype(BF16)
    dv_ref[0] = dv_sum[...].astype(BF16)


def attention_back(qkv, grad, lse, patches):
    triple, dim, tokens = qkv.shape
    heads = triple // 3
    frames = tokens // patches
    block = (1, dim, patches)
    factor = LOG2E / math.sqrt(HEAD_DIM)
    spec = pl.BlockSpec(block, lambda f, h: (h, 0, f))
    shape = jax.ShapeDtypeStruct((heads, dim, tokens), BF16)
    parts = pl.pallas_call(
        functools.partial(attention_back_kernel, factor, min(256, patches)),
        out_shape=[shape] * 3,
        grid=(frames, heads),
        in_specs=[
            spec,
            pl.BlockSpec(block, lambda f, h: (heads + h, 0, f)),
            pl.BlockSpec(block, lambda f, h: (2 * heads + h, 0, f)),
            spec,
            pl.BlockSpec((1, 1, patches), lambda f, h: (h, 0, f)),
        ],
        out_specs=[spec] * 3,
        scratch_shapes=[pltpu.VMEM((dim, patches), F32)] * 2,
        compiler_params=pltpu.CompilerParams(vmem_limit_bytes=40 * MIB),
        cost_estimate=pl.CostEstimate(
            flops=10 * heads * patches * tokens * 256,
            bytes_accessed=8 * heads * dim * tokens * 2,
            transcendentals=heads * patches * tokens,
        ),
        name="attention_back",
    )(qkv, qkv, qkv, grad, lse)
    return jnp.concatenate(parts, axis=0)


def from_patch(array, hops, size):
    if hops == 0:
        return array
    return lax.ppermute(array, "patch", [((to + hops) % size, to) for to in range(size)])


def from_core(array):
    return lax.ppermute(array, "core", [(0, 1), (1, 0)])


def group_gather(block, size):
    mine = jnp.concatenate([from_patch(block, hops, size) for hops in range(size)], axis=0)
    return jnp.concatenate([mine, from_core(mine)], axis=0)


def group_sum(terms, size):
    half = terms.shape[0] // 2
    mine = terms[:half].astype(F32) + from_core(terms[half:].astype(BF16)).astype(F32)
    rows = half // size
    total = mine[:rows]
    for hops in range(1, size):
        send = mine[hops * rows : (hops + 1) * rows].astype(BF16)
        total = total + from_patch(send, size - hops, size).astype(F32)
    return total


def group_swap(pieces, size):
    out = []
    for dc in range(2):
        row = []
        for dx in range(size):
            piece = pieces[dc][(size - dx) % size]
            piece = from_patch(piece, dx, size)
            row.append(from_core(piece) if dc else piece)
        out.append(row)
    return out


def natural(pieces, size):
    core, patch = lax.axis_index("core"), lax.axis_index("patch")
    if size == 2:
        swapped = [
            [jnp.where(patch == 0, row[0], row[1]), jnp.where(patch == 0, row[1], row[0])]
            for row in pieces
        ]
    else:
        swapped = []
        for row in pieces:
            stack = jnp.stack(row)
            swapped.append(
                [
                    lax.dynamic_index_in_dim(stack, (to - patch + size) % size, 0, False)
                    for to in range(size)
                ]
            )
    first = [jnp.where(core == 0, a, b) for a, b in zip(swapped[0], swapped[1])]
    second = [jnp.where(core == 0, b, a) for a, b in zip(swapped[0], swapped[1])]
    return first + second


def relative(blocks, size):
    core, patch = lax.axis_index("core"), lax.axis_index("patch")
    return [
        [
            lax.dynamic_index_in_dim(
                blocks, (core + dc) % 2 * size + (patch + dx) % size, 0, False
            )
            for dx in range(size)
        ]
        for dc in range(2)
    ]


def per_device(
    tokens,
    cotangent,
    clip_embed,
    timesteps,
    frame_clip,
    ada_weight,
    ada_bias,
    qkv_weight,
    query_bias,
    value_bias,
    out_weight,
    out_bias,
    up_weight,
    up_bias,
    down_weight,
    down_bias,
):
    ring_size, patch_size = lax.axis_size("ring"), lax.axis_size("patch")
    sizes = (ring_size, 2, patch_size)
    group = 2 * patch_size
    device_count = ring_size * group
    ring, core, patch = (lax.axis_index(name) for name in ("ring", "core", "patch"))
    member = core * patch_size + patch
    device = ring * group + member
    rows, width = tokens.shape[1:]
    tokens, cotangent = tokens[0], cotangent[0]
    patches = patch_size * rows
    clips = clip_embed.shape[0]
    hidden = up_weight.shape[1]
    share = width // device_count
    heads = HEADS // group
    head_width = heads * HEAD_DIM
    units = hidden // group
    mine = jnp.arange(group) == member
    mine_of_all = jnp.arange(device_count) == device

    tokens_all = group_gather(tokens, patch_size)

    qkv_cols = jnp.transpose(qkv_weight.reshape(share, 3, group, head_width), (2, 0, 1, 3)).reshape(
        group, share, 3 * head_width
    )
    up_cols = jnp.transpose(
        up_weight.reshape(share, ring_size, group, hidden // device_count), (2, 0, 1, 3)
    ).reshape(group, share, units)
    packed = jnp.concatenate(
        [qkv_cols, up_cols, jnp.broadcast_to(out_weight, (group,) + out_weight.shape)], axis=2
    )
    received = jnp.concatenate(
        natural(group_swap(relative(packed, patch_size), patch_size), patch_size), axis=0
    )
    qkv_block = received[:, : 3 * head_width]
    up_block = received[:, 3 * head_width : 3 * head_width + units]
    out_block = received[:, 3 * head_width + units :]
    (w_qkv,) = ring_gather([qkv_block], ring_size, 1)
    w_out, w_up, w_down = ring_gather([out_block, up_block, down_weight], ring_size, 2)
    w_qkv = w_qkv.reshape(width, 3 * head_width)
    w_out = w_out.reshape(width, width)
    w_up = w_up.reshape(width, units)
    w_down = w_down.reshape(units, width)

    condition = clip_embed + sinusoid(timesteps, width)
    silu_cond, silu_back = jax.vjp(jax.nn.silu, condition)
    silu_low = silu_cond.astype(BF16)
    silu_part = lax.dynamic_slice_in_dim(silu_low, device * share, share, 1)
    mod_part = jnp.dot(silu_part, ada_weight, preferred_element_type=F32)

    def placed(shard):
        return jnp.where(mine_of_all[:, None], shard.astype(F32)[None, :], 0.0).reshape(-1)

    mod_part = mod_part + placed(ada_bias)[None, :]
    frame_count = 2 * ring_size
    own_frame = 2 * ring + core
    clip_part = jnp.where(
        (jnp.arange(frame_count) == own_frame) & (patch == 0), frame_clip[0].astype(F32), 0.0
    )
    sent = [
        mod_part.reshape(-1),
        placed(query_bias),
        placed(value_bias),
        placed(out_bias),
        placed(down_bias),
        placed(up_bias),
        clip_part,
    ]
    summed = all_sum(jnp.concatenate(sent), sizes, 3)
    got, at = [], 0
    for item in sent:
        got.append(summed[at : at + item.shape[0]])
        at += item.shape[0]
    modulation = got[0].reshape(clips, 6 * width)
    b_query = lax.dynamic_slice_in_dim(got[1], member * head_width, head_width, 0)
    b_value = lax.dynamic_slice_in_dim(got[2], member * head_width, head_width, 0)
    b_out, b_down = got[3], got[4]
    b_up = lax.dynamic_index_in_dim(
        got[5].reshape(ring_size, group, hidden // device_count), member, 1, False
    ).reshape(units)
    own_clip = frame_clip[0]
    other_clip = lax.dynamic_index_in_dim(got[6], 2 * ring + 1 - core, 0, False).astype(jnp.int32)
    own_mod = lax.dynamic_index_in_dim(modulation, own_clip, 0, False)
    other_mod = lax.dynamic_index_in_dim(modulation, other_clip, 0, False)
    shift_one, scale_one, gate_one, shift_two, scale_two, gate_two = (
        own_mod[at * width : (at + 1) * width] for at in range(6)
    )
    both = jnp.stack([own_mod[: 2 * width], other_mod[: 2 * width]])[:, None, :]

    normed_all, _ = layer_norm(tokens_all.astype(F32).reshape(2, patches, width))
    hidden_one = (
        (normed_all * (1.0 + both[:, :, width:]) + both[:, :, :width])
        .astype(BF16)
        .reshape(2 * patches, width)
    )
    qkv_bias = jnp.concatenate([b_query, jnp.zeros_like(b_query), b_value])
    projected = (
        lax.dot_general(w_qkv, hidden_one, (((0,), (1,)), ((), ())), preferred_element_type=F32)
        + qkv_bias[:, None]
    ).astype(BF16)
    qkv = projected.reshape(3 * heads, HEAD_DIM, 2 * patches)
    attended_t, lse = attention(qkv, patches)
    attended_t = attended_t.reshape(head_width, 2 * patches)

    def token_pieces(array):
        return [
            [
                array[:, (dc * patch_size + dx) * rows : (dc * patch_size + dx + 1) * rows]
                for dx in range(patch_size)
            ]
            for dc in range(2)
        ]

    attended = jnp.concatenate(
        natural(group_swap(token_pieces(attended_t), patch_size), patch_size), axis=0
    )

    input_rows = tokens.astype(F32)
    branch_one = (
        lax.dot_general(attended, w_out, (((0,), (0,)), ((), ())), preferred_element_type=F32)
        + b_out
    )
    midway = input_rows + gate_one * branch_one
    normed_two, inv_two = layer_norm(midway)
    hidden_two = (normed_two * (1.0 + scale_two) + shift_two).astype(BF16)
    grad_out = cotangent.astype(F32)
    grad_branch_two = (gate_two * grad_out).astype(BF16)

    gb_two_all = group_gather(grad_branch_two, patch_size)
    hidden_two_all = group_gather(hidden_two, patch_size)
    pre_act = jnp.dot(hidden_two_all, w_up, preferred_element_type=F32) + b_up
    act_full, gelu_back = jax.vjp(gelu_tanh, pre_act)
    act_low = act_full.astype(BF16)
    branch_two = group_sum(jnp.dot(act_low, w_down, preferred_element_type=F32), patch_size) + b_down
    output = (midway + gate_two * branch_two).astype(BF16)

    grad_act = lax.dot_general(
        gb_two_all, w_down, (((1,), (1,)), ((), ())), preferred_element_type=F32
    )
    grad_pre = gelu_back(grad_act)[0].astype(BF16)
    grad_hidden_two = group_sum(
        lax.dot_general(grad_pre, w_up, (((1,), (1,)), ((), ())), preferred_element_type=F32),
        patch_size,
    )
    over_tokens = (((0,), (0,)), ((), ()))
    g_down = lax.dot_general(act_low, gb_two_all, over_tokens, preferred_element_type=F32).astype(
        BF16
    )
    g_up = lax.dot_general(
        hidden_two_all, grad_pre, over_tokens, preferred_element_type=F32
    ).astype(BF16)
    g_up_b = jnp.sum(grad_pre.astype(F32), axis=0)
    g_down_b = jnp.sum(grad_branch_two.astype(F32), axis=0)
    block_rows = width // ring_size
    share_down, sum_up = ring_sum(
        [
            g_down.reshape(ring_size, units // ring_size, width),
            g_up.reshape(ring_size, block_rows, units),
        ],
        [F32, BF16],
        ring_size,
        4,
    )

    grad_gate_two = jnp.sum(grad_out * branch_two, axis=0)
    grad_shift_two = jnp.sum(grad_hidden_two, axis=0)
    grad_scale_two = jnp.sum(grad_hidden_two * normed_two, axis=0)
    grad_midway = grad_out + norm_back(grad_hidden_two * (1.0 + scale_two), normed_two, inv_two)
    grad_gate_one = jnp.sum(grad_midway * branch_one, axis=0)
    grad_branch_one = (gate_one * grad_midway).astype(BF16)
    g_out_b = jnp.sum(grad_branch_one.astype(F32), axis=0)
    grad_attended = lax.dot_general(
        w_out, grad_branch_one, (((1,), (1,)), ((), ())), preferred_element_type=F32
    ).astype(BF16)
    g_out = jnp.dot(attended, grad_branch_one, preferred_element_type=F32).astype(BF16)
    swapped = group_swap(
        relative(grad_attended.reshape(group, head_width, rows), patch_size), patch_size
    )
    grad_mix = jnp.concatenate([piece for row in swapped for piece in row], axis=1)
    grad_projected = attention_back(
        qkv, grad_mix.reshape(heads, HEAD_DIM, 2 * patches), lse, patches
    ).reshape(3 * head_width, 2 * patches)

    g_qkv = lax.dot_general(
        hidden_one, grad_projected, (((0,), (1,)), ((), ())), preferred_element_type=F32
    ).astype(BF16)
    g_query_b = jnp.sum(grad_projected[:head_width].astype(F32), axis=1)
    g_value_b = jnp.sum(grad_projected[2 * head_width :].astype(F32), axis=1)
    grad_hidden_one = group_sum(
        lax.dot_general(
            grad_projected, w_qkv, (((0,), (1,)), ((), ())), preferred_element_type=F32
        ),
        patch_size,
    )
    sum_out, sum_qkv = ring_sum(
        [g_out.reshape(ring_size, block_rows, width), g_qkv.reshape(ring_size, block_rows, -1)],
        [BF16, BF16],
        ring_size,
        5,
    )

    normed_one, inv_one = layer_norm(input_rows)
    grad_shift_one = jnp.sum(grad_hidden_one, axis=0)
    grad_scale_one = jnp.sum(grad_hidden_one * normed_one, axis=0)
    tokens_grad = (
        grad_midway + norm_back(grad_hidden_one * (1.0 + scale_one), normed_one, inv_one)
    ).astype(BF16)

    pieces = jnp.concatenate([sum_qkv, sum_up, sum_out], axis=1).reshape(group, share, -1)
    got_w = natural(group_swap(relative(pieces, patch_size), patch_size), patch_size)
    stacked = jnp.stack(got_w).astype(F32)
    share_qkv = jnp.transpose(
        stacked[:, :, : 3 * head_width].reshape(group, share, 3, head_width), (1, 2, 0, 3)
    ).reshape(share, 3 * width)
    share_up = jnp.transpose(
        stacked[:, :, 3 * head_width : 3 * head_width + units].reshape(
            group, share, ring_size, hidden // device_count
        ),
        (1, 2, 0, 3),
    ).reshape(share, hidden)
    share_out = jnp.sum(stacked[:, :, 3 * head_width + units :], axis=0)

    frame_grads = jnp.concatenate(
        [
            grad_shift_one,
            grad_scale_one,
            grad_gate_one,
            grad_shift_two,
            grad_scale_two,
            grad_gate_two,
        ]
    )
    clip_terms = jnp.where(
        (jnp.arange(clips) == own_clip)[:, None], frame_grads[None, :], 0.0
    ).reshape(-1)
    terms = [
        clip_terms,
        jnp.where(mine[:, None], g_query_b[None, :], 0.0).reshape(-1),
        jnp.where(mine[:, None], g_value_b[None, :], 0.0).reshape(-1),
        g_out_b,
        g_down_b,
        jnp.where(mine[None, :, None], g_up_b.reshape(ring_size, 1, -1), 0.0).reshape(-1),
    ]
    summed = all_sum(jnp.concatenate(terms), sizes, 6)
    got, at = [], 0
    for item in terms:
        got.append(summed[at : at + item.shape[0]])
        at += item.shape[0]
    mod_low = got[0].reshape(clips, 6 * width).astype(BF16)

    def own(vector):
        length = vector.shape[0] // device_count
        return lax.dynamic_slice_in_dim(vector, device * length, length, 0)

    ada_bias_grad = own(jnp.sum(mod_low.astype(F32), axis=0))
    ada_weight_grad = lax.dot_general(
        silu_part, mod_low, (((0,), (0,)), ((), ())), preferred_element_type=F32
    )
    grad_silu_part = lax.dot_general(
        mod_low, ada_weight, (((1,), (1,)), ((), ())), preferred_element_type=F32
    )
    grad_silu = all_sum(
        jnp.where(mine_of_all[None, :, None], grad_silu_part[:, None, :], 0.0).reshape(-1),
        sizes,
        7,
    ).reshape(clips, width)
    clip_grad = silu_back(grad_silu)[0]
    return (
        output[None],
        tokens_grad[None],
        clip_grad,
        ada_weight_grad,
        ada_bias_grad,
        share_qkv,
        own(got[1]),
        own(got[2]),
        share_out,
        own(got[3]),
        share_up,
        own(got[5]),
        share_down,
        own(got[4]),
    )


def solution(mesh):
    frames, patch = mesh.shape["frames"], mesh.shape["patch"]
    inner = Mesh(mesh.devices.reshape(frames // 2, 2, patch), ("ring", "core", "patch"))
    every = ("ring", "core", "patch")
    tokens = P(("ring", "core"), "patch", None)
    matrix = P(every, None)
    vector = P(every)
    return jax.shard_map(
        per_device,
        mesh=inner,
        in_specs=(
            tokens,
            tokens,
            P(),
            P(),
            P(("ring", "core")),
            matrix,
            vector,
            matrix,
            vector,
            vector,
            matrix,
            vector,
            matrix,
            vector,
            matrix,
            vector,
        ),
        out_specs=(
            tokens,
            tokens,
            P(),
            matrix,
            vector,
            matrix,
            vector,
            vector,
            matrix,
            vector,
            matrix,
            vector,
            matrix,
            vector,
        ),
        check_vma=False,
    )
```

time: 2160 us -> 740 us (0.34)
  blocking collectives: 1200 us -> 0 us
  Pallas kernels: 0 us -> 349 us
  waiting for transfers between devices: 406 us -> 108 us
  matrix products: 213 us -> 103 us
  starting transfers between devices: 99.3 us -> 17.5 us
  local copies, waits for them, and re-layouts: 169 us -> 89.9 us
  other arithmetic: 38 us -> 63.5 us
    unnamed x2 -> x0, blocking collectives: 1150 us -> none
    pallas_call x0 -> x9, Pallas kernels: none -> 349 us  [the longest x2 123 us: ring_gather(): pl.pallas_call(functools.partial(ring_gather_kernel, size, count), out_sh...]
    all_gather x7 -> x0, waiting for transfers between devices: 327 us -> none  [the longest x1 108 us: per_device(): lax.all_gather(ada_weight, ('frames', 'patch'), axis=0, tiled=True)]
    unnamed x166 -> x216, local copies, waits for them, and re-layouts: 139 us -> 23.5 us
    dot_general x38 -> x15, matrix products: 213 us -> 103 us  [the longest x1 19.2 us: per_device(): lax.dot_general(gb_two_all, w_down, (((1,), (1,)), ((), ())), preferred_e...]
    ppermute x0 -> x28, waiting for transfers between devices: none -> 108 us  [the longest x14 107 us: from_patch(): lax.ppermute(array, 'patch', [((to + hops) % size, to) for to in range(si...]
    unnamed x20 -> x0, starting transfers between devices: 98.9 us -> none
    psum x1 -> x0, blocking collectives: 51 us -> none  [per_device(): mod_total = lax.psum(clip_terms, ('frames', 'patch'))]
  transfers between devices with their start and end apart: 30 -> 28, of which waited for: 10 -> 9; matrix products, arithmetic and copies ran while one was open for 65% -> 21% of each run, Pallas kernels for 0% -> 35%
where the time goes in v1:
time: 740 us; the launch traced here: 735 us
  Pallas kernels  349 us (47%)
  waiting for transfers between devices  108 us (15%)
  matrix products  103 us (14%)
  local copies, waits for them, and re-layouts  89.9 us (12%)
  other arithmetic  63.5 us (9%)
  starting transfers between devices  17.5 us (2%)
    pallas_call x2, Pallas kernels, ring_gather(): pl.pallas_call(functools.partial(ring_gather_kernel, size, count), out_sh...  123 us
    pallas_call x2, Pallas kernels, ring_sum(): pl.pallas_call(functools.partial(ring_sum_kernel, size, count), out_shape...  110 us
    ppermute x14, waiting for transfers between devices, from_patch(): lax.ppermute(array, 'patch', [((to + hops) % size, to) for to in range(si...  107 us
    pallas_call x3, Pallas kernels, all_sum(): pl.pallas_call(functools.partial(all_sum_kernel, bits), out_shape=jax.Sha...  58.8 us
    pallas_call x1, Pallas kernels, attention_back(): pl.pallas_call(functools.partial(attention_back_kernel, factor, min(256,...  33.2 us
    pallas_call x1, Pallas kernels, attention(): pl.pallas_call(functools.partial(attention_kernel, factor, min(256, patch...  23.5 us
    unnamed x216, local copies, waits for them, and re-layouts  23.5 us
    dot_general x1, matrix products, per_device(): lax.dot_general(gb_two_all, w_down, (((1,), (1,)), ((), ())), preferred_e...  19.2 us
  transfers between devices with their start and end apart: 28, of which 9 were waited for; matrix products, arithmetic and copies ran while one was open for 21% of the time, Pallas kernels for 35%

profile of v1, /device:TPU:0, one launch (start us, length us, event | category | flops | bytes accessed | tf_op | source)
XLA Modules:
  0.0 735.5 jit_solution(4908822372236882463)
XLA Ops:
  40.3 23.2 %all_sum_3.1 = f32[184,128]{1,0:T(8,128)} custom-call(f32[184,128]{1,0:T(8,128)} %pad_bitcast_fusion.1.in_ref), custom_call_target="tpu_custom_call" | custom-call | tf_op jit(solution)/shard_map/all_sum_3/pallas_call | solution.py:243
  76.9 36.2 %ring_gather_1.1 = bf16[8,144,864]{2,1,0:T(8,128)(2,1)} custom-call(bf16[144,864]{1,0:T(8,128)(2,1)} %pad_maximum_fusion.21.refs_0_), custom_call_target="tpu_custom_call" | custom-call | bytes 23887872 | tf_op jit(solution)/shard_map/ring_gather_1/pallas_call | solution.py:123
  128.8 23.5 %attention.1 = (bf16[4,72,2048]{2,1,0:T(8,128)(2,1)S(1)}, f32[4,1,2048]{2,1,0:T(1,128)S(1)}) custom-call(bf16[12,72,2048]{2,1,0:T(8,128)(2,1)S(1)} %bitcast.173, bf16[12,72,2048]{2,1,0:T(8,128)(2,1)S(1)} %bitcast.174, bf16[12,72,2048]{2,1,0:T(8,128)(2,1)S(1)} %bitcast.175), custom_call_target="tpu_custom_call" | custom-call | flops 8589934592 | bytes 4718592 | tf_op jit(solution)/shard_map/attention/pallas_call | solution.py:280
  164.4 87.2 %ring_gather_2.1 = (bf16[8,144,1152]{2,1,0:T(8,128)(2,1)}, bf16[8,144,1152]{2,1,0:T(8,128)(2,1)}, bf16[8,144,1152]{2,1,0:T(8,128)(2,1)}) custom-call(bf16[144,1152]{1,0:T(8,128)(2,1)} %get-tuple-element.91.refs_0_, bf16[144,1152]{1,0:T(8,128)(2,1)} %get-tuple-element.90.refs_1_, bf16[144,1152]{1,0:T(8,128)(2,1)} %refs_2_.1), custom_call_target="tpu_custom_call" | custom-call | bytes 95551488 | tf_op jit(solution)/shard_map/ring_gather_2/pallas_call | solution.py:123
  253.0 5.9 fusion.47
  263.2 25.9 %collective-permute-done.10 = bf16[512,1152]{1,0:T(8,128)(2,1)S(1)} collective-permute-done((bf16[512,1152]{1,0:T(8,128)(2,1)S(1)}, bf16[512,1152]{1,0:T(8,128)(2,1)S(1)}, u32[]{:S(2)}, u32[]{:S(2)}) %collective-permute-start.10) | collective-permute-done | bytes 1179680 | tf_op jit(solution)/shard_map/ppermute | solution.py:374
  291.0 22.2 %collective-permute-done.14 = bf16[512,1152]{1,0:T(8,128)(2,1)S(1)} collective-permute-done((bf16[512,1152]{1,0:T(8,128)(2,1)S(1)}, bf16[512,1152]{1,0:T(8,128)(2,1)S(1)}, u32[]{:S(2)}, u32[]{:S(2)}) %collective-permute-start.14) | collective-permute-done | bytes 1179680 | tf_op jit(solution)/shard_map/ppermute | solution.py:374
  315.3 13.3 %convolution_add_fusion = f32[2048,1152]{1,0:T(8,128)} fusion(bf16[1152,1152]{1,0:T(8,128)(2,1)} %bitcast.208, f32[1152]{0:T(1024)S(1)} %add.352, bf16[1024,1152]{1,0:T(8,128)(2,1)} %collective-permute-done.11, bf16[512,1152]{1,0:T(8,128)(2,1)} %copy-done.34, bf16[512,1152]{1,0:T(8,128)(2,1)} %copy-done.23), kind=kOutput, calls=%fused_computation.15 | convolution fusion | flops 5452333056 | bytes 16814592 | tf_op jit(solution)/shard_map/dot_general | solution.py:591
  328.6 19.2 %convert_reduce_fusion = (f32[1152]{0:T(1024)S(1)}, bf16[2048,1152]{1,0:T(8,128)(2,1)}) fusion(f32[2048,1152]{1,0:T(8,128)} %convolution_add_fusion, bf16[1152,1152]{1,0:T(8,128)(2,1)S(1)} %bitcast.206, bf16[1024,1152]{1,0:T(8,128)(2,1)} %collective-permute-done.15, bf16[512,1152]{1,0:T(8,128)(2,1)S(1)} %copy-done.37, ...), kind=kOutput, calls=%fused_computation.10 | convolution fusion | flops 5511314432 | bytes 21533184 | tf_op jit(solution)/shard_map/dot_general | solution.py:597
  347.7 8.8 %fusion.49 = f32[2048,1152]{1,0:T(8,128)S(1)} fusion(bf16[2048,1152]{1,0:T(8,128)(2,1)} %get-tuple-element.118, bf16[1152,1152]{1,0:T(8,128)(2,1)S(1)} %bitcast.209), kind=kOutput, calls=%fused_computation.231 | convolution fusion | flops 5435817984 | bytes 16809984 | tf_op jit(solution)/shard_map/dot_general | solution.py:602
  357.3 10.9 %fusion.44 = f32[2048,1152]{1,0:T(8,128)S(1)} fusion(bf16[1152,1152]{1,0:T(8,128)(2,1)S(1)} %bitcast.207, f32[2048,1152]{1,0:T(8,128)} %convolution_add_fusion), kind=kOutput, calls=%fused_computation.228 | convolution fusion | flops 5457051648 | bytes 21528576 | tf_op jit(solution)/shard_map/dot_general | solution.py:594
  380.6 20.5 %collective-permute-done.17 = bf16[512,1152]{1,0:T(8,128)(2,1)S(1)} collective-permute-done((bf16[512,1152]{1,0:T(8,128)(2,1)}, bf16[512,1152]{1,0:T(8,128)(2,1)S(1)}, u32[]{:S(2)}, u32[]{:S(2)}) %collective-permute-start.17) | collective-permute-done | bytes 1179680 | tf_op jit(solution)/shard_map/ppermute | solution.py:374
  405.2 20.8 %collective-permute-done.13 = bf16[512,1152]{1,0:T(8,128)(2,1)} collective-permute-done((bf16[512,1152]{1,0:T(8,128)(2,1)}, bf16[512,1152]{1,0:T(8,128)(2,1)}, u32[]{:S(2)}, u32[]{:S(2)}) %collective-permute-start.13) | collective-permute-done | bytes 1179680 | tf_op jit(solution)/shard_map/ppermute | solution.py:374
  426.1 6.7 fusion.21
  436.2 12.4 %convolution_convert_fusion.2 = bf16[1152,1152]{1,0:T(8,128)(2,1)S(1)} fusion(bf16[1024,1152]{1,0:T(8,128)(2,1)} %collective-permute-done.15, bf16[512,1152]{1,0:T(8,128)(2,1)S(1)} %copy-done.38, bf16[512,1152]{1,0:T(8,128)(2,1)S(1)} %copy-done.21, f32[2048,1152]{1,0:T(8,128)} %convolution_add_fusion), kind=kOutput, calls=%fused_computation.19 | convolution fusion | flops 5472534528 | bytes 16809984 | tf_op jit(solution)/shard_map/dot_general | solution.py:606
  449.9 8.3 %convolution_convert_fusion.1 = bf16[1152,1152]{1,0:T(8,128)(2,1)S(1)} fusion(bf16[2048,1152]{1,0:T(8,128)(2,1)S(1)} %bitcast.211, bf16[1024,1152]{1,0:T(8,128)(2,1)} %collective-permute-done.11, bf16[512,1152]{1,0:T(8,128)(2,1)S(1)} %copy-done.35, bf16[512,1152]{1,0:T(8,128)(2,1)S(1)} %copy-done.24), kind=kOutput, calls=%fused_computation.18 | convolution fusion | flops 5451300864 | bytes 12091392 | tf_op jit(solution)/shard_map/dot_general | solution.py:609
  458.2 58.7 %ring_sum_4.1 = (f32[144,1152]{1,0:T(8,128)S(1)}, bf16[144,1152]{1,0:T(8,128)(2,1)S(1)}) custom-call(bf16[8,144,1152]{2,1,0:T(8,128)(2,1)S(1)} %bitcast.169, bf16[8,144,1152]{2,1,0:T(8,128)(2,1)S(1)} %bitcast.170), custom_call_target="tpu_custom_call" | custom-call | bytes 63700992 | tf_op jit(solution)/shard_map/ring_sum_4/pallas_call | solution.py:178
  520.2 33.2 %attention_back.1 = (bf16[4,72,2048]{2,1,0:T(8,128)(2,1)S(1)}, bf16[4,72,2048]{2,1,0:T(8,128)(2,1)S(1)}, bf16[4,72,2048]{2,1,0:T(8,128)(2,1)S(1)}) custom-call(bf16[12,72,2048]{2,1,0:T(8,128)(2,1)S(1)} %bitcast.176, bf16[12,72,2048]{2,1,0:T(8,128)(2,1)S(1)} %bitcast.177, bf16[12,72,2048]{2,1,0:T(8,128)(2,1)S(1)} %bitcast.178, ...), custom_call_target="tpu_custom_call" | custom-call | flops 21474836480 | bytes 9437184 | tf_op jit(solution)/shard_map/attention_back/pallas_call | solution.py:347
  568.1 5.9 convolution_convert_fusion.3
  578.7 51.7 %ring_sum_5.1 = (bf16[144,1152]{1,0:T(8,128)(2,1)S(1)}, bf16[144,864]{1,0:T(8,128)(2,1)S(1)}) custom-call(bf16[8,144,1152]{2,1,0:T(8,128)(2,1)S(1)} %bitcast.168, bf16[8,144,864]{2,1,0:T(8,128)(2,1)S(1)} %bitcast.167), custom_call_target="tpu_custom_call" | custom-call | bytes 55738368 | tf_op jit(solution)/shard_map/ring_sum_5/pallas_call | solution.py:178
  641.1 6.4 collective-permute-done.26
  673.9 7.0 collective-permute-done.23
  688.8 21.1 %all_sum_6.1 = f32[184,128]{1,0:T(8,128)} custom-call(f32[184,128]{1,0:T(8,128)} %pad_bitcast_fusion.in_ref), custom_call_target="tpu_custom_call" | custom-call | tf_op jit(solution)/shard_map/all_sum_6/pallas_call | solution.py:243
  714.9 14.5 %all_sum_7.1 = f32[24,128]{1,0:T(8,128)} custom-call(f32[24,128]{1,0:T(8,128)} %pad_bitcast_fusion.2.in_ref), custom_call_target="tpu_custom_call" | custom-call | tf_op jit(solution)/shard_map/all_sum_7/pallas_call | solution.py:243
  (419 shorter events, 188.1 us)
Async XLA Ops:
  0.7 66.3 %collective-permute-start.4 = (bf16[512,1152]{1,0:T(8,128)(2,1)}, bf16[512,1152]{1,0:T(8,128)(2,1)S(1)}, u32[]{:S(2)}, u32[]{:S(2)}) collective-permute-start(bf16[512,1152]{1,0:T(8,128)(2,1)} %bitcast.179), channel_id=1, source_target_pairs={{1,0},{0,1},{3,2},{2,3},{5,4},{4,5},{7,6},{6,7},{9,8},{8,9},{11,10... | collective-permute-start | bytes 3538952 | tf_op jit(solution)/shard_map/ppermute | solution.py:374
  15.8 55.5 %collective-permute-start.2 = (bf16[36,3168]{1,0:T(8,128)(2,1)}, bf16[36,3168]{1,0:T(8,128)(2,1)}, u32[]{:S(2)}, u32[]{:S(2)}) collective-permute-start(bf16[36,3168]{1,0:T(8,128)(2,1)} %bitcast.158), channel_id=1, source_target_pairs={{1,0},{0,1},{3,2},{2,3},{5,4},{4,5},{7,6},{6,7},{9,8},{8,9},{11,10... | collective-permute-start | bytes 684296 | tf_op jit(solution)/shard_map/ppermute | solution.py:374
  16.6 56.6 %collective-permute-start = (bf16[36,3168]{1,0:T(8,128)(2,1)}, bf16[36,3168]{1,0:T(8,128)(2,1)S(1)}, u32[]{:S(2)}, u32[]{:S(2)}) collective-permute-start(bf16[36,3168]{1,0:T(8,128)(2,1)} %bitcast.160), channel_id=1, source_target_pairs={{1,0},{0,1},{3,2},{2,3},{5,4},{4,5},{7,6},{6,7},{9,8},{8,9},{11,10... | collective-permute-start | bytes 684296 | tf_op jit(solution)/shard_map/ppermute | solution.py:374
  19.3 53.9 %collective-permute-start.1 = (bf16[36,3168]{1,0:T(8,128)(2,1)}, bf16[36,3168]{1,0:T(8,128)(2,1)S(1)}, u32[]{:S(2)}, u32[]{:S(2)}) collective-permute-start(bf16[36,3168]{1,0:T(8,128)(2,1)} %bitcast.159), channel_id=1, source_target_pairs={{0,2},{2,0},{1,3},{3,1},{4,6},{6,4},{5,7},{7,5},{8,10},{10,8},{9,1... | collective-permute-start | bytes 684296 | tf_op jit(solution)/shard_map/ppermute | solution.py:378
  68.5 44.6 %collective-permute-start.5 = (bf16[1024,1152]{1,0:T(8,128)(2,1)}, bf16[1024,1152]{1,0:T(8,128)(2,1)}, u32[]{:S(2)}, u32[]{:S(2)}) collective-permute-start(bf16[1024,1152]{1,0:T(8,128)(2,1)} %pad_maximum_fusion.3), channel_id=1, source_target_pairs={{0,2},{2,0},{1,3},{3,1},{4,6},{6,4},{5,7},{7,5},{8,10},{10,8},{9,1... | collective-permute-start | bytes 7077896 | tf_op jit(solution)/shard_map/ppermute | solution.py:378
  153.5 98.2 %collective-permute-start.6 = (bf16[288,512]{1,0:T(8,128)(2,1)}, bf16[288,512]{1,0:T(8,128)(2,1)}, u32[]{:S(2)}, u32[]{:S(2)}) collective-permute-start(bf16[288,512]{1,0:T(8,128)(2,1)} %get-tuple-element.84), channel_id=1, source_target_pairs={{1,0},{0,1},{3,2},{2,3},{5,4},{4,5},{7,6},{6,7},{9,8},{8,9},{11,10... | collective-permute-start | bytes 884744 | tf_op jit(solution)/shard_map/ppermute | solution.py:374
  155.5 96.1 %collective-permute-start.7 = (bf16[288,512]{1,0:T(8,128)(2,1)}, bf16[288,512]{1,0:T(8,128)(2,1)}, u32[]{:S(2)}, u32[]{:S(2)}) collective-permute-start(bf16[288,512]{1,0:T(8,128)(2,1)} %get-tuple-element.86), channel_id=1, source_target_pairs={{0,2},{2,0},{1,3},{3,1},{4,6},{6,4},{5,7},{7,5},{8,10},{10,8},{9,1... | collective-permute-start | bytes 884744 | tf_op jit(solution)/shard_map/ppermute | solution.py:378
  160.1 91.6 %collective-permute-start.9 = (bf16[288,512]{1,0:T(8,128)(2,1)}, bf16[288,512]{1,0:T(8,128)(2,1)}, u32[]{:S(2)}, u32[]{:S(2)}) collective-permute-start(bf16[288,512]{1,0:T(8,128)(2,1)} %collective-permute-done.8), channel_id=1, source_target_pairs={{0,2},{2,0},{1,3},{3,1},{4,6},{6,4},{5,7},{7,5},{8,10},{10,8},{9,1... | collective-permute-start | bytes 884744 | tf_op jit(solution)/shard_map/ppermute | solution.py:378
  260.3 28.9 %collective-permute-start.10 = (bf16[512,1152]{1,0:T(8,128)(2,1)S(1)}, bf16[512,1152]{1,0:T(8,128)(2,1)S(1)}, u32[]{:S(2)}, u32[]{:S(2)}) collective-permute-start(bf16[512,1152]{1,0:T(8,128)(2,1)S(1)} %add_convert_fusion.3), channel_id=1, source_target_pairs={{1,0},{0,1},{3,2},{2,3},{5,4},{4,5},{7,6},{6,7},{9,8},{8,9},{11,10... | collective-permute-start | bytes 3538952 | tf_op jit(solution)/shard_map/ppermute | solution.py:374
  262.0 51.2 %collective-permute-start.14 = (bf16[512,1152]{1,0:T(8,128)(2,1)S(1)}, bf16[512,1152]{1,0:T(8,128)(2,1)S(1)}, u32[]{:S(2)}, u32[]{:S(2)}) collective-permute-start(bf16[512,1152]{1,0:T(8,128)(2,1)S(1)} %get-tuple-element.52), channel_id=1, source_target_pairs={{1,0},{0,1},{3,2},{2,3},{5,4},{4,5},{7,6},{6,7},{9,8},{8,9},{11,10... | collective-permute-start | bytes 3538952 | tf_op jit(solution)/shard_map/ppermute | solution.py:374
  291.0 24.3 %collective-permute-start.11 = (bf16[1024,1152]{1,0:T(8,128)(2,1)}, bf16[1024,1152]{1,0:T(8,128)(2,1)}, u32[]{:S(2)}, u32[]{:S(2)}) collective-permute-start(bf16[1024,1152]{1,0:T(8,128)(2,1)} %pad_maximum_fusion.4), channel_id=1, source_target_pairs={{0,2},{2,0},{1,3},{3,1},{4,6},{6,4},{5,7},{7,5},{8,10},{10,8},{9,1... | collective-permute-start | bytes 7077896 | tf_op jit(solution)/shard_map/ppermute | solution.py:378
  315.0 13.6 %collective-permute-start.15 = (bf16[1024,1152]{1,0:T(8,128)(2,1)}, bf16[1024,1152]{1,0:T(8,128)(2,1)}, u32[]{:S(2)}, u32[]{:S(2)}) collective-permute-start(bf16[1024,1152]{1,0:T(8,128)(2,1)} %pad_maximum_fusion.5), channel_id=1, source_target_pairs={{0,2},{2,0},{1,3},{3,1},{4,6},{6,4},{5,7},{7,5},{8,10},{10,8},{9,1... | collective-permute-start | bytes 7077896 | tf_op jit(solution)/shard_map/ppermute | solution.py:378
  356.8 11.9 %collective-permute-start.16 = (bf16[1024,1152]{1,0:T(8,128)(2,1)S(1)}, bf16[1024,1152]{1,0:T(8,128)(2,1)}, u32[]{:S(2)}, u32[]{:S(2)}) collective-permute-start(bf16[1024,1152]{1,0:T(8,128)(2,1)S(1)} %slice.333), channel_id=1, source_target_pairs={{0,2},{2,0},{1,3},{3,1},{4,6},{6,4},{5,7},{7,5},{8,10},{10,8},{9,1... | collective-permute-start | bytes 7077896 | tf_op jit(solution)/shard_map/ppermute | solution.py:378
  372.1 29.0 %collective-permute-start.17 = (bf16[512,1152]{1,0:T(8,128)(2,1)}, bf16[512,1152]{1,0:T(8,128)(2,1)S(1)}, u32[]{:S(2)}, u32[]{:S(2)}) collective-permute-start(bf16[512,1152]{1,0:T(8,128)(2,1)} %slice.336), channel_id=1, source_target_pairs={{1,0},{0,1},{3,2},{2,3},{5,4},{4,5},{7,6},{6,7},{9,8},{8,9},{11,10... | collective-permute-start | bytes 3538952 | tf_op jit(solution)/shard_map/ppermute | solution.py:374
  378.5 47.6 %collective-permute-start.13 = (bf16[512,1152]{1,0:T(8,128)(2,1)}, bf16[512,1152]{1,0:T(8,128)(2,1)}, u32[]{:S(2)}, u32[]{:S(2)}) collective-permute-start(bf16[512,1152]{1,0:T(8,128)(2,1)} %slice.337), channel_id=1, source_target_pairs={{1,0},{0,1},{3,2},{2,3},{5,4},{4,5},{7,6},{6,7},{9,8},{8,9},{11,10... | collective-permute-start | bytes 3538952 | tf_op jit(solution)/shard_map/ppermute | solution.py:374
  434.7 14.6 %collective-permute-start.20 = (bf16[288,512]{1,0:T(8,128)(2,1)S(1)}, bf16[288,512]{1,0:T(8,128)(2,1)}, u32[]{:S(2)}, u32[]{:S(2)}) collective-permute-start(bf16[288,512]{1,0:T(8,128)(2,1)S(1)} %get-tuple-element.80), channel_id=1, source_target_pairs={{1,0},{0,1},{3,2},{2,3},{5,4},{4,5},{7,6},{6,7},{9,8},{8,9},{11,10... | collective-permute-start | bytes 884744 | tf_op jit(solution)/shard_map/ppermute | solution.py:374
  448.6 69.4 %collective-permute-start.18 = (bf16[288,512]{1,0:T(8,128)(2,1)S(1)}, bf16[288,512]{1,0:T(8,128)(2,1)S(1)}, u32[]{:S(2)}, u32[]{:S(2)}) collective-permute-start(bf16[288,512]{1,0:T(8,128)(2,1)S(1)} %get-tuple-element.82), channel_id=1, source_target_pairs={{1,0},{0,1},{3,2},{2,3},{5,4},{4,5},{7,6},{6,7},{9,8},{8,9},{11,10... | collective-permute-start | bytes 884744 | tf_op jit(solution)/shard_map/ppermute | solution.py:374
  449.4 68.6 %collective-permute-start.19 = (bf16[288,512]{1,0:T(8,128)(2,1)S(1)}, bf16[288,512]{1,0:T(8,128)(2,1)S(1)}, u32[]{:S(2)}, u32[]{:S(2)}) collective-permute-start(bf16[288,512]{1,0:T(8,128)(2,1)S(1)} %get-tuple-element.81), channel_id=1, source_target_pairs={{0,2},{2,0},{1,3},{3,1},{4,6},{6,4},{5,7},{7,5},{8,10},{10,8},{9,1... | collective-permute-start | bytes 884744 | tf_op jit(solution)/shard_map/ppermute | solution.py:378
  449.4 68.6 %collective-permute-start.21 = (bf16[288,512]{1,0:T(8,128)(2,1)}, bf16[288,512]{1,0:T(8,128)(2,1)S(1)}, u32[]{:S(2)}, u32[]{:S(2)}) collective-permute-start(bf16[288,512]{1,0:T(8,128)(2,1)} %collective-permute-done.20), channel_id=1, source_target_pairs={{0,2},{2,0},{1,3},{3,1},{4,6},{6,4},{5,7},{7,5},{8,10},{10,8},{9,1... | collective-permute-start | bytes 884744 | tf_op jit(solution)/shard_map/ppermute | solution.py:378
  563.3 84.2 %collective-permute-start.22 = (bf16[1024,1152]{1,0:T(8,128)(2,1)}, bf16[1024,1152]{1,0:T(8,128)(2,1)}, u32[]{:S(2)}, u32[]{:S(2)}) collective-permute-start(bf16[1024,1152]{1,0:T(8,128)(2,1)} %slice.332), channel_id=1, source_target_pairs={{0,2},{2,0},{1,3},{3,1},{4,6},{6,4},{5,7},{7,5},{8,10},{10,8},{9,1... | collective-permute-start | bytes 7077896 | tf_op jit(solution)/shard_map/ppermute | solution.py:378
  638.1 9.4 %collective-permute-start.26 = (bf16[36,3168]{1,0:T(8,128)(2,1)}, bf16[36,3168]{1,0:T(8,128)(2,1)}, u32[]{:S(2)}, u32[]{:S(2)}) collective-permute-start(bf16[36,3168]{1,0:T(8,128)(2,1)} %get-tuple-element.88), channel_id=1, source_target_pairs={{1,0},{0,1},{3,2},{2,3},{5,4},{4,5},{7,6},{6,7},{9,8},{8,9},{11,10... | collective-permute-start | bytes 684296 | tf_op jit(solution)/shard_map/ppermute | solution.py:374
  640.0 13.7 %collective-permute-start.24 = (bf16[36,3168]{1,0:T(8,128)(2,1)S(1)}, bf16[36,3168]{1,0:T(8,128)(2,1)S(1)}, u32[]{:S(2)}, u32[]{:S(2)}) collective-permute-start(bf16[36,3168]{1,0:T(8,128)(2,1)S(1)} %get-tuple-element.87), channel_id=1, source_target_pairs={{1,0},{0,1},{3,2},{2,3},{5,4},{4,5},{7,6},{6,7},{9,8},{8,9},{11,10... | collective-permute-start | bytes 684296 | tf_op jit(solution)/shard_map/ppermute | solution.py:374
  640.7 12.9 %collective-permute-start.25 = (bf16[36,3168]{1,0:T(8,128)(2,1)S(1)}, bf16[36,3168]{1,0:T(8,128)(2,1)S(1)}, u32[]{:S(2)}, u32[]{:S(2)}) collective-permute-start(bf16[36,3168]{1,0:T(8,128)(2,1)S(1)} %get-tuple-element.89), channel_id=1, source_target_pairs={{0,2},{2,0},{1,3},{3,1},{4,6},{6,4},{5,7},{7,5},{8,10},{10,8},{9,1... | collective-permute-start | bytes 684296 | tf_op jit(solution)/shard_map/ppermute | solution.py:378
  652.3 28.6 %collective-permute-start.23 = (bf16[512,1152]{1,0:T(8,128)(2,1)}, bf16[512,1152]{1,0:T(8,128)(2,1)S(1)}, u32[]{:S(2)}, u32[]{:S(2)}) collective-permute-start(bf16[512,1152]{1,0:T(8,128)(2,1)} %slice.335), channel_id=1, source_target_pairs={{1,0},{0,1},{3,2},{2,3},{5,4},{4,5},{7,6},{6,7},{9,8},{8,9},{11,10... | collective-permute-start | bytes 3538952 | tf_op jit(solution)/shard_map/ppermute | solution.py:374
  (102 other events, 1324.7 us)

commit v2 on v1

v2 whole, which is shorter than its diff:
```python
import functools
import math

import jax
import jax.numpy as jnp
from jax import lax
from jax.experimental import pallas as pl
from jax.experimental.pallas import tpu as pltpu
from jax.sharding import Mesh
from jax.sharding import PartitionSpec as P

HEADS = 16
HEAD_DIM = 72
BF16 = jnp.bfloat16
F32 = jnp.float32
LOG2E = 1.4426950408889634
MESH_ID = pl.DeviceIdType.MESH
MIB = 2**20


def layer_norm(values_in):
    centre = values_in - jnp.mean(values_in, axis=-1, keepdims=True)
    spread = jnp.mean(centre * centre, axis=-1, keepdims=True)
    inv_std = lax.rsqrt(spread + 1e-06)
    return (centre * inv_std, inv_std)


def norm_back(grad_normed, normed, inv_std):
    mean_grad = jnp.mean(grad_normed, axis=-1, keepdims=True)
    mean_prod = jnp.mean(grad_normed * normed, axis=-1, keepdims=True)
    return (grad_normed - mean_grad - normed * mean_prod) * inv_std


def gelu_tanh(values_in):
    inner = 0.7978845608028654 * (values_in + 0.044715 * values_in * values_in * values_in)
    return 0.5 * values_in * (1.0 + jnp.tanh(inner))


def sinusoid(steps_in, width_in):
    half_width = width_in // 2
    freqs = jnp.exp(-math.log(10000.0) * jnp.arange(half_width, dtype=jnp.float32) / half_width)
    angles = steps_in.astype(jnp.float32)[:, None] * freqs[None, :]
    return jnp.concatenate([jnp.cos(angles), jnp.sin(angles)], axis=1)


class Where:
    def __init__(self, sizes):
        self.size, _, self.span = sizes
        self.ring, self.core, self.patch = (
            lax.axis_index(name) for name in ("ring", "core", "patch")
        )
        along, across = self.ring // 2, self.ring % 2
        self.place = (1 - across) * along + across * (self.size - 1 - along)
        self.member = self.core * self.span + self.patch

    def at_place(self, place):
        place = (place + 2 * self.size) % self.size
        back = place // (self.size // 2)
        return (1 - back) * 2 * place + back * (2 * (self.size - 1 - place) + 1)

    def neighbour(self, step):
        return (self.at_place(self.place + step), self.core, self.patch)

    def peer(self, dc, dx):
        core = 1 - self.core if dc else self.core
        return (self.ring, core, (self.patch + dx) % self.span)

    def peer_member(self, dc, dx):
        _, core, patch = self.peer(dc, dx)
        return core * self.span + patch

    def ring_peers(self):
        return [self.neighbour(1), self.neighbour(-1)]

    def group_peers(self):
        return [
            self.peer(dc, dx) for dc in range(2) for dx in range(self.span) if dc or dx
        ]


def greet(peers):
    barrier = pltpu.get_barrier_semaphore()
    for peer in peers:
        pl.semaphore_signal(barrier, inc=1, device_id=peer, device_id_type=MESH_ID)
    pl.semaphore_wait(barrier, len(peers))


def remote(source, target, send_sem, recv_sem, peer):
    return pltpu.make_async_remote_copy(
        src_ref=source,
        dst_ref=target,
        send_sem=send_sem,
        recv_sem=recv_sem,
        device_id=peer,
        device_id_type=MESH_ID,
    )


def halves(rows, columns):
    if rows % 16 == 0:
        cut = -(-rows // 32) * 16
        return (pl.ds(0, cut), slice(None)), (pl.ds(cut, rows - cut), slice(None))
    cut = -(-columns // 256) * 128
    return (slice(None), pl.ds(0, cut)), (slice(None), pl.ds(cut, columns - cut))


class RingGather:
    @staticmethod
    def scratch(size):
        dma = pltpu.SemaphoreType.DMA
        return [dma((2, size - 1)), dma((2, size - 1)), dma((1,))]

    def __init__(self, where, block, out, sems):
        self.where, self.block, self.out = where, block, out
        self.send, self.recv, self.own = sems
        self.steps = where.size

    def keep(self):
        return pltpu.make_async_copy(self.block, self.out.at[self.where.ring], self.own.at[0])

    def copy(self, way, step):
        where, sign = self.where, (-1, 1)[way]
        part = halves(*self.block.shape)[way]
        slot = where.at_place(where.place + sign * step)
        target = self.out.at[(slot,) + part]
        source = target if step else self.block.at[part]
        return remote(
            source, target, self.send.at[way, step], self.recv.at[way, step], where.neighbour(-sign)
        )

    def run(self, step):
        last = self.where.size - 2
        if step == 0:
            self.keep().start()
        for way in range(2):
            if step:
                self.copy(way, step - 1).wait_recv()
            if step <= last:
                self.copy(way, step).start()
        if step > last:
            for way in range(2):
                for past in range(last + 1):
                    self.copy(way, past).wait_send()
            self.keep().wait()


class RingGatherSplit:
    @staticmethod
    def scratch(size):
        dma, half = pltpu.SemaphoreType.DMA, size // 2
        return [dma((half,)), dma((half,)), dma((half,)), dma((half,)), dma((1,))]

    def __init__(self, where, block, out, sems):
        self.where, self.block, self.out = where, block, out
        self.send, self.recv, self.send_core, self.recv_core, self.own = sems
        self.half = where.size // 2
        self.steps = self.half + 2

    def keep(self):
        return pltpu.make_async_copy(self.block, self.out.at[self.where.ring], self.own.at[0])

    def slot(self, step):
        where = self.where
        return self.out.at[where.at_place(where.place + (2 * where.core - 1) * step)]

    def copy(self, step):
        where = self.where
        target = self.slot(step)
        source = target if step else self.block
        peer = where.neighbour(1 - 2 * where.core)
        return remote(source, target, self.send.at[step], self.recv.at[step], peer)

    def hand(self, step):
        target = self.slot(step + 1)
        return remote(
            target, target, self.send_core.at[step], self.recv_core.at[step], self.where.peer(1, 0)
        )

    def run(self, step):
        half = self.half
        if step == 0:
            self.keep().start()
        if 0 < step <= half:
            self.copy(step - 1).wait_recv()
        if step < half:
            self.copy(step).start()
        if 0 < step < half:
            self.hand(step - 1).start()
        if step == half + 1:
            for past in range(half):
                self.copy(past).wait_send()
            for past in range(half - 1):
                self.hand(past).wait()
            self.keep().wait()


class RingSum:
    @staticmethod
    def scratch(size, rows, columns):
        dma = pltpu.SemaphoreType.DMA
        slots = pltpu.VMEM((size - 1, rows, columns), BF16)
        return [slots, slots, dma((2, size - 1)), dma((2, size - 1))]

    def __init__(self, where, terms, out, scratch):
        self.where, self.terms, self.out = where, terms, out
        self.held, self.landed, self.send, self.recv = scratch
        self.steps = where.size

    def copy(self, way, step):
        part = (step,) + halves(*self.terms.shape[1:])[way]
        return remote(
            self.held.at[part],
            self.landed.at[part],
            self.send.at[way, step],
            self.recv.at[way, step],
            self.where.neighbour((1, -1)[way]),
        )

    def run(self, step):
        where, last = self.where, self.where.size - 2
        for way, part in enumerate(halves(*self.terms.shape[1:])):
            slot = where.at_place(where.place + (-1, 1)[way] * (step + 1))
            total = self.terms[(slot,) + part]
            if step:
                self.copy(way, step - 1).wait_recv()
                total = total.astype(F32) + self.landed[(step - 1,) + part].astype(F32)
            if step <= last:
                self.held[(step,) + part] = total.astype(BF16)
                self.copy(way, step).start()
            else:
                self.out[part] = total.astype(self.out.dtype)
        if step > last:
            for way in range(2):
                for past in range(last + 1):
                    self.copy(way, past).wait_send()


class GroupGather:
    @staticmethod
    def scratch(span, parts=1):
        dma = pltpu.SemaphoreType.DMA
        return [dma((2, span, parts)), dma((2, span, parts)), dma((1,))]

    def __init__(self, where, block, out, sems, parts=1):
        self.where, self.block, self.out, self.parts = where, block, out, parts
        self.send, self.recv, self.own = sems
        self.steps = 3

    def rows(self, part):
        size = self.block.shape[0] // self.parts
        return pl.ds(part * size, size)

    def hop(self, dx, part):
        where, rows = self.where, self.rows(part)
        at = (0, dx, part)
        return remote(
            self.block.at[rows],
            self.out.at[0, dx, rows],
            self.send.at[at],
            self.recv.at[at],
            where.peer(0, where.span - dx),
        )

    def cross(self, dx, part):
        rows = self.rows(part)
        source = self.out.at[0, dx, rows] if dx else self.block.at[rows]
        at = (1, dx, part)
        return remote(
            source,
            self.out.at[1, dx, rows],
            self.send.at[at],
            self.recv.at[at],
            self.where.peer(1, 0),
        )

    def start(self, part):
        for dx in range(1, self.where.span):
            self.hop(dx, part).start()
        self.cross(0, part).start()

    def pass_on(self, part):
        for dx in range(1, self.where.span):
            self.hop(dx, part).wait_recv()
            self.cross(dx, part).start()

    def finish(self):
        for part in range(self.parts):
            for dx in range(self.where.span):
                if dx:
                    self.hop(dx, part).wait_send()
                self.cross(dx, part).wait()

    def keep(self):
        return pltpu.make_async_copy(self.block, self.out.at[0, 0], self.own.at[0])

    def run(self, step):
        if step == 0:
            self.keep().start()
            for part in range(self.parts):
                self.start(part)
        elif step == 1:
            for part in range(self.parts):
                self.pass_on(part)
        else:
            self.finish()
            self.keep().wait()


class GroupSwap:
    @staticmethod
    def scratch(span):
        dma = pltpu.SemaphoreType.DMA
        return [dma((2, span)), dma((2, span)), dma((1,))]

    def __init__(self, where, source, target, sems):
        self.where, self.source, self.target = where, source, target
        self.send, self.recv, self.own = sems
        self.steps = 2

    def run(self, step):
        where = self.where
        keep = pltpu.make_async_copy(self.source(0, 0), self.target(0, 0), self.own.at[0])
        copies = [
            remote(
                self.source(dc, dx),
                self.target(dc, dx),
                self.send.at[dc, dx],
                self.recv.at[dc, dx],
                where.peer(dc, dx),
            )
            for dx in reversed(range(where.span))
            for dc in range(2)
            if dc or dx
        ]
        if step == 0:
            for copy in copies:
                copy.start()
            keep.start()
        else:
            for copy in copies:
                copy.wait()
            keep.wait()


class GroupSum:
    @staticmethod
    def scratch(span, rows, columns):
        dma = pltpu.SemaphoreType.DMA
        slots = pltpu.VMEM((span, rows, columns), BF16)
        return [slots, slots, dma((span,)), dma((span,)), dma((span,)), dma((span,))]

    def __init__(self, where, terms, out, scratch):
        self.where, self.terms, self.out = where, terms, out
        self.crossed, self.landed, *sems = scratch
        self.send_core, self.recv_core, self.send, self.recv = sems
        self.steps = 3

    def cross(self, dx):
        return remote(
            self.terms.at[1, dx],
            self.crossed.at[dx],
            self.send_core.at[dx],
            self.recv_core.at[dx],
            self.where.peer(1, 0),
        )

    def hop(self, dx):
        return remote(
            self.crossed.at[dx],
            self.landed.at[dx],
            self.send.at[dx],
            self.recv.at[dx],
            self.where.peer(0, dx),
        )

    def fold(self, dx):
        self.cross(dx).wait_recv()
        total = self.terms[0, dx].astype(F32) + self.crossed[dx].astype(F32)
        self.crossed[dx] = total.astype(BF16)
        self.hop(dx).start()

    def finish(self):
        self.cross(0).wait_recv()
        total = self.terms[0, 0].astype(F32) + self.crossed[0].astype(F32)
        for dx in range(1, self.where.span):
            self.hop(dx).wait_recv()
            total = total + self.landed[dx].astype(F32)
        self.out[...] = total.astype(self.out.dtype)
        for dx in range(self.where.span):
            self.cross(dx).wait_send()
            if dx:
                self.hop(dx).wait_send()

    def run(self, step):
        later = list(reversed(range(self.where.span)))
        if step == 0:
            for dx in later:
                self.cross(dx).start()
        elif step == 1:
            for dx in later[:-1]:
                self.fold(dx)
        else:
            self.finish()


class CoreSum:
    @staticmethod
    def scratch(span, rows, columns):
        dma = pltpu.SemaphoreType.DMA
        return [pltpu.VMEM((span, rows, columns), BF16), dma((span,)), dma((span,))]

    def __init__(self, where, terms, out, scratch):
        self.where, self.terms, self.out = where, terms, out
        self.crossed, self.send_core, self.recv_core = scratch

    cross = GroupSum.cross

    def fold(self, dx):
        self.cross(dx).wait_recv()
        total = self.terms[0, dx].astype(F32) + self.crossed[dx].astype(F32)
        self.out[dx] = total.astype(BF16)

    def finish(self):
        for dx in range(self.where.span):
            self.cross(dx).wait_send()


class PatchSum:
    @staticmethod
    def scratch(span, rows, columns):
        dma = pltpu.SemaphoreType.DMA
        return [pltpu.VMEM((span, rows, columns), BF16), dma((span,)), dma((span,))]

    def __init__(self, where, terms, out, scratch):
        self.where, self.crossed, self.out = where, terms, out
        self.landed, self.send, self.recv = scratch
        self.steps = 2

    hop = GroupSum.hop

    def run(self, step):
        span = self.where.span
        if step == 0:
            for dx in range(1, span):
                self.hop(dx).start()
        else:
            total = self.crossed[0].astype(F32)
            for dx in range(1, span):
                self.hop(dx).wait_recv()
                total = total + self.landed[dx].astype(F32)
            self.out[...] = total
            for dx in range(1, span):
                self.hop(dx).wait_send()


class AllSum:
    @staticmethod
    def bits(sizes):
        found = []
        for axis in (2, 0, 1):
            bit = 1
            while bit < sizes[axis]:
                found.append((axis, bit))
                bit *= 2
        return found

    @staticmethod
    def scratch(sizes, rows):
        count = len(AllSum.bits(sizes))
        dma = pltpu.SemaphoreType.DMA
        slots = pltpu.VMEM((count, rows, 128), F32)
        return [slots, slots, dma((count,)), dma((count,))]

    def __init__(self, where, sizes, block, out, scratch):
        self.block, self.out = block, out
        self.held, self.landed, self.send, self.recv = scratch
        here = (where.ring, where.core, where.patch)
        self.peers = []
        for axis, bit in AllSum.bits(sizes):
            peer = list(here)
            peer[axis] = here[axis] + (1 - 2 * ((here[axis] // bit) % 2)) * bit
            self.peers.append(tuple(peer))
        self.steps = len(self.peers) + 1

    def copy(self, step):
        return remote(
            self.held.at[step],
            self.landed.at[step],
            self.send.at[step],
            self.recv.at[step],
            self.peers[step],
        )

    def run(self, step):
        if step == 0:
            total = self.block[...]
        else:
            self.copy(step - 1).wait()
            total = self.held[step - 1] + self.landed[step - 1]
        if step < len(self.peers):
            self.held[step] = total
            self.copy(step).start()
        else:
            self.out[...] = total


HBM = pl.BlockSpec(memory_space=pl.ANY)
CORE = pl.BlockSpec(memory_space=pltpu.VMEM)


def take(refs, counts):
    found, at = [], 0
    for count in counts:
        found.append(list(refs[at : at + count]))
        at += count
    return found


def flat_block(vector):
    rows = -(-vector.shape[0] // 1024) * 8
    return jnp.pad(vector, (0, rows * 128 - vector.shape[0])).reshape(rows, 128)


def entry_kernel(sizes, share, *refs):
    where = Where(sizes)
    size, group = where.size, 2 * where.span
    ins, outs, scratch = take(refs, (5, 5, len(refs) - 10))
    tokens, qkv_cols, up_cols, out_rows, vector = ins
    tokens_all, w_qkv, w_out, up_block, summed = outs
    lands, rest = scratch[:3], scratch[3:]
    wide, blocks = rest[:3], rest[3:5]
    sems = take(rest[5:], (3, 3, 3, 3, 3, 5, 4))
    greet(
        where.ring_peers() + where.group_peers() + AllSum(where, sizes, None, None, [0] * 4).peers
    )
    member = where.member

    def swap(source, land, job_sems):
        return GroupSwap(where, source, lambda dc, dx: land.at[member], job_sems)

    swaps = [
        swap(lambda dc, dx: qkv_cols.at[where.peer_member(dc, dx)], lands[0], sems[0]),
        swap(lambda dc, dx: out_rows, lands[1], sems[1]),
        swap(lambda dc, dx: up_cols.at[where.peer_member(dc, dx)], lands[2], sems[2]),
    ]
    gather = GroupGather(where, tokens, tokens_all, sems[3])
    ring_qkv = RingGather(where, blocks[0], w_qkv, sems[4])
    ring_out = RingGatherSplit(where, blocks[1], w_out, sems[5])
    sums = AllSum(where, sizes, vector, summed, sems[6])

    def join(at, block):
        for piece in range(group):
            wide[at][piece * share : (piece + 1) * share, :] = lands[at][piece].astype(F32)
        block[...] = wide[at][...].astype(BF16)

    swaps[0].run(0)
    sums.run(0)
    swaps[1].run(0)
    swaps[2].run(0)
    gather.run(0)
    swaps[0].run(1)
    join(0, blocks[0])
    ring_qkv.run(0)
    sums.run(1)
    swaps[1].run(1)
    join(1, blocks[1])
    ring_out.run(0)
    swaps[2].run(1)
    join(2, up_block)
    steps = max(ring_qkv.steps, ring_out.steps, sums.steps - 1)
    for step in range(1, steps):
        for job, at in ((ring_qkv, step), (ring_out, step), (sums, step + 1)):
            if at < job.steps:
                job.run(at)
        if step == steps - 2:
            gather.run(1)
    gather.run(2)


def entry(tokens, qkv_cols, up_cols, out_rows, vector, sizes, call_id):
    size, _, span = sizes
    group = 2 * span
    share = out_rows.shape[0]
    rows, width = tokens.shape
    block_rows = group * share
    columns = [qkv_cols.shape[2], width, up_cols.shape[2]]
    shape = jax.ShapeDtypeStruct
    scratch = [pltpu.VMEM((group, share, n), BF16) for n in columns]
    scratch += [pltpu.VMEM((block_rows, n), F32) for n in columns]
    scratch += [pltpu.VMEM((block_rows, n), BF16) for n in columns[:2]]
    scratch += GroupSwap.scratch(span) * 3
    scratch += GroupGather.scratch(span)
    scratch += RingGather.scratch(size)
    scratch += RingGatherSplit.scratch(size)
    scratch += AllSum.scratch(sizes, vector.shape[0])
    return pl.pallas_call(
        functools.partial(entry_kernel, sizes, share),
        out_shape=[
            shape((2, span, rows, width), BF16),
            shape((size, block_rows, columns[0]), BF16),
            shape((size, block_rows, width), BF16),
            shape((block_rows, columns[2]), BF16),
            shape(vector.shape, F32),
        ],
        in_specs=[HBM, HBM, HBM, HBM, CORE],
        out_specs=[HBM, HBM, HBM, CORE, CORE],
        scratch_shapes=scratch,
        compiler_params=pltpu.CompilerParams(
            collective_id=call_id, has_side_effects=True, vmem_limit_bytes=32 * MIB
        ),
        name="entry",
    )(tokens, qkv_cols, up_cols, out_rows, vector)


def exchange_kernel(sizes, kinds, counts, order, *refs):
    where = Where(sizes)
    ins, outs, scratch = take(refs, (len(kinds), len(kinds), len(refs) - 2 * len(kinds)))
    scratch = take(scratch, counts)
    jobs, peers = [], []
    for kind, source, out, own in zip(kinds, ins, outs, scratch):
        if kind is AllSum:
            jobs.append(AllSum(where, sizes, source, out, own))
            peers += jobs[-1].peers
        else:
            jobs.append(kind(where, source, out, own))
    if any(kind in (RingGather, RingSum, RingGatherSplit) for kind in kinds):
        peers += where.ring_peers()
    if any(kind in (GroupGather, GroupSum, RingGatherSplit) for kind in kinds):
        peers += where.group_peers()
    greet(peers)
    for step in range(max(job.steps for job in jobs)):
        for job in jobs:
            if step < job.steps:
                job.run(step)


def exchange(jobs, sizes, call_id):
    size, _, span = sizes
    kinds, arrays, outs, scratch, counts, spaces = [], [], [], [], [], []
    shape = jax.ShapeDtypeStruct
    for kind, array, *dtype in jobs:
        kinds.append(kind)
        arrays.append(array)
        inside = True
        if kind is RingSum:
            outs.append(shape(array.shape[1:], dtype[0]))
            own = RingSum.scratch(size, *array.shape[1:])
        elif kind is GroupSum:
            outs.append(shape(array.shape[2:], dtype[0]))
            own = GroupSum.scratch(span, *array.shape[2:])
        elif kind is AllSum:
            outs.append(shape(array.shape, F32))
            own = AllSum.scratch(sizes, array.shape[0])
        elif kind is GroupGather:
            outs.append(shape((2, span) + array.shape, array.dtype))
            own, inside = GroupGather.scratch(span), False
        else:
            outs.append(shape((size,) + array.shape, array.dtype))
            own, inside = kind.scratch(size), False
        scratch += own
        counts.append(len(own))
        spaces.append(CORE if inside else HBM)
    return pl.pallas_call(
        functools.partial(exchange_kernel, sizes, tuple(kinds), tuple(counts), None),
        out_shape=outs,
        in_specs=spaces,
        out_specs=spaces,
        scratch_shapes=scratch,
        compiler_params=pltpu.CompilerParams(
            collective_id=call_id, has_side_effects=True, vmem_limit_bytes=48 * MIB
        ),
        name=f"exchange_{call_id}",
    )(*arrays)


def along_grid(jobs, total, before):
    at = pl.program_id(0) * pl.num_programs(1) + pl.program_id(1)
    if before:
        for grid in range(total):
            todo = [(job, grid) for job in jobs if grid < job.steps - 1]
            if todo:

                @pl.when(at == grid)
                def _():
                    for job, step in todo:
                        job.run(step)

    else:

        @pl.when(at == total - 1)
        def _():
            for job in jobs:
                for step in range(min(total, job.steps - 1), job.steps):
                    job.run(step)


def attention_kernel(sizes, factor, chunk, total, *refs):
    where = Where(sizes)
    ins, outs, scratch = take(refs, (5, 4, len(refs) - 9))
    q_ref, k_ref, v_ref, up_block, grad_block = ins
    out_ref, lse_ref, w_up, grad_all = outs
    sems = take(scratch, (3, 3))
    jobs = [
        RingGather(where, up_block, w_up, sems[0]),
        GroupGather(where, grad_block, grad_all, sems[1]),
    ]
    at = pl.program_id(0) * pl.num_programs(1) + pl.program_id(1)

    @pl.when(at == 0)
    def _():
        greet(where.ring_peers() + where.group_peers())

    along_grid(jobs[:1], total, True)

    @pl.when(at == 0)
    def _():
        jobs[1].run(0)

    keys = k_ref[0].T
    values_t = v_ref[0]
    for start in range(0, q_ref.shape[2], chunk):
        span = slice(start, start + chunk)
        scores = jnp.dot(keys, q_ref[0, :, span], preferred_element_type=F32) * factor
        top = jnp.max(scores, axis=0, keepdims=True)
        probs = jnp.exp2(scores - top)
        row_sum = jnp.sum(probs, axis=0, keepdims=True)
        mixed = jnp.dot(values_t, probs.astype(BF16), preferred_element_type=F32)
        out_ref[0, :, span] = (mixed / row_sum).astype(BF16)
        lse_ref[0, :, span] = top + jnp.log2(row_sum)

    along_grid(jobs[:1], total, False)

    @pl.when(at == total - 1)
    def _():
        jobs[1].run(1)
        jobs[1].run(2)


def attention(qkv, up_block, grad_block, patches, sizes, call_id):
    size, _, span = sizes
    triple, dim, tokens = qkv.shape
    heads = triple // 3
    frames = tokens // patches
    block = (1, dim, patches)
    factor = LOG2E / math.sqrt(HEAD_DIM)
    shape = jax.ShapeDtypeStruct
    return pl.pallas_call(
        functools.partial(attention_kernel, sizes, factor, min(256, patches), frames * heads),
        out_shape=[
            shape((heads, dim, tokens), BF16),
            shape((heads, 1, tokens), F32),
            shape((size,) + up_block.shape, BF16),
            shape((2, span) + grad_block.shape, BF16),
        ],
        grid=(frames, heads),
        in_specs=[
            pl.BlockSpec(block, lambda f, h: (h, 0, f)),
            pl.BlockSpec(block, lambda f, h: (heads + h, 0, f)),
            pl.BlockSpec(block, lambda f, h: (2 * heads + h, 0, f)),
            HBM,
            HBM,
        ],
        out_specs=[
            pl.BlockSpec(block, lambda f, h: (h, 0, f)),
            pl.BlockSpec((1, 1, patches), lambda f, h: (h, 0, f)),
            HBM,
            HBM,
        ],
        scratch_shapes=RingGather.scratch(size) + GroupGather.scratch(span),
        compiler_params=pltpu.CompilerParams(
            collective_id=call_id, has_side_effects=True, vmem_limit_bytes=32 * MIB
        ),
        cost_estimate=pl.CostEstimate(
            flops=4 * heads * patches * tokens * 256,
            bytes_accessed=4 * heads * dim * tokens * 2,
            transcendentals=heads * patches * tokens,
        ),
        name="attention",
    )(qkv, qkv, qkv, up_block, grad_block)


def attention_back_kernel(sizes, factor, chunk, total, *refs):
    where = Where(sizes)
    ins, outs, scratch = take(refs, (7, 5, len(refs) - 12))
    q_ref, k_ref, v_ref, g_ref, lse_ref, up_terms, half_terms = ins
    dq_ref, dk_ref, dv_ref, up_sum, half_sum = outs
    dk_sum, dv_sum = scratch[:2]
    own = take(scratch[2:], (4, 3))
    ring_up = RingSum(where, up_terms, up_sum, own[0])
    half = PatchSum(where, half_terms, half_sum, own[1])
    at = pl.program_id(0) * pl.num_programs(1) + pl.program_id(1)

    @pl.when(at == 0)
    def _():
        greet(where.ring_peers() + where.group_peers())
        half.run(0)

    along_grid([ring_up], total, True)

    keys_t = k_ref[0]
    keys = keys_t.T
    values = v_ref[0].T
    scale = factor / LOG2E
    patches = q_ref.shape[2]
    for start in range(0, patches, chunk):
        span = slice(start, start + chunk)
        queries_t = q_ref[0, :, span]
        grad_t = g_ref[0, :, span]
        scores = jnp.dot(keys, queries_t, preferred_element_type=F32) * factor
        probs = jnp.exp2(scores - lse_ref[0, :, span])
        grad_probs = jnp.dot(values, grad_t, preferred_element_type=F32)
        row_dot = jnp.sum(probs * grad_probs, axis=0, keepdims=True)
        grad_scores = (probs * (grad_probs - row_dot)).astype(BF16)
        probs_low = probs.astype(BF16)
        dq = jnp.dot(keys_t, grad_scores, preferred_element_type=F32)
        dq_ref[0, :, span] = (dq * scale).astype(BF16)
        dims = (((1,), (1,)), ((), ()))
        dk = lax.dot_general(queries_t, grad_scores, dims, preferred_element_type=F32)
        dv = lax.dot_general(grad_t, probs_low, dims, preferred_element_type=F32)
        if start == 0:
            dk_sum[...] = dk
            dv_sum[...] = dv
        else:
            dk_sum[...] += dk
            dv_sum[...] += dv
    dk_ref[0] = (dk_sum[...] * scale).astype(BF16)
    dv_ref[0] = dv_sum[...].astype(BF16)

    along_grid([ring_up], total, False)

    @pl.when(at == total - 1)
    def _():
        half.run(1)


def attention_back(qkv, grad, lse, up_terms, half_terms, patches, sizes, call_id):
    size, _, span = sizes
    triple, dim, tokens = qkv.shape
    heads = triple // 3
    frames = tokens // patches
    block = (1, dim, patches)
    factor = LOG2E / math.sqrt(HEAD_DIM)
    spec = pl.BlockSpec(block, lambda f, h: (h, 0, f))
    shape = jax.ShapeDtypeStruct
    grads = shape((heads, dim, tokens), BF16)
    *parts, up_sum, half_sum = pl.pallas_call(
        functools.partial(attention_back_kernel, sizes, factor, min(256, patches), frames * heads),
        out_shape=[grads] * 3
        + [shape(up_terms.shape[1:], BF16), shape(half_terms.shape[1:], F32)],
        grid=(frames, heads),
        in_specs=[
            spec,
            pl.BlockSpec(block, lambda f, h: (heads + h, 0, f)),
            pl.BlockSpec(block, lambda f, h: (2 * heads + h, 0, f)),
            spec,
            pl.BlockSpec((1, 1, patches), lambda f, h: (h, 0, f)),
            CORE,
            CORE,
        ],
        out_specs=[spec] * 3 + [CORE, CORE],
        scratch_shapes=[pltpu.VMEM((dim, patches), F32)] * 2
        + RingSum.scratch(size, *up_terms.shape[1:])
        + PatchSum.scratch(span, *half_terms.shape[1:]),
        compiler_params=pltpu.CompilerParams(
            collective_id=call_id, has_side_effects=True, vmem_limit_bytes=48 * MIB
        ),
        cost_estimate=pl.CostEstimate(
            flops=10 * heads * patches * tokens * 256,
            bytes_accessed=8 * heads * dim * tokens * 2,
            transcendentals=heads * patches * tokens,
        ),
        name="attention_back",
    )(qkv, qkv, qkv, grad, lse, up_terms, half_terms)
    return jnp.concatenate(parts, axis=0), up_sum, half_sum


def joined(array):
    group, features, count = array.shape
    if features % 16:
        return array.astype(F32).reshape(group * features, count).astype(BF16)
    return array.reshape(group * features, count)


def middle_kernel(sizes, parts, *refs):
    where = Where(sizes)
    ins, outs, scratch = take(refs, (5, 5, len(refs) - 10))
    heads_t, w_out, tokens, vectors, down_block = ins
    attended, branch, midway, hidden_all, w_down = outs
    hidden = scratch[0]
    sems = take(scratch[1:], (3, 3, 3))
    greet(where.ring_peers() + where.group_peers())
    rows, width = tokens.shape
    span = where.span

    swap = GroupSwap(
        where,
        lambda dc, dx: heads_t.at[:, pl.ds((dc * span + dx) * rows, rows)],
        lambda dc, dx: attended.at[where.member],
        sems[0],
    )
    ring = RingGather(where, down_block, w_down, sems[1])
    gather = GroupGather(where, hidden, hidden_all, sems[2], parts)
    swap.run(0)
    for step in range(4):
        ring.run(step)
    swap.run(1)
    size = rows // parts
    for part in range(parts):
        span_rows = slice(part * size, (part + 1) * size)
        mixed = joined(attended[:, :, span_rows])
        one = lax.dot_general(
            mixed, w_out[...], (((0,), (0,)), ((), ())), preferred_element_type=F32
        )
        one = one + vectors[0:1, :]
        branch[span_rows, :] = one
        mid = tokens[span_rows, :].astype(F32) + vectors[1:2, :] * one
        midway[span_rows, :] = mid
        normed, _ = layer_norm(mid)
        hidden[span_rows, :] = (normed * (1.0 + vectors[2:3, :]) + vectors[3:4, :]).astype(BF16)
        gather.start(part)
    for step in range(4, ring.steps):
        ring.run(step)
    for part in range(parts):
        gather.pass_on(part)
    gather.finish()
    gather.keep().start()
    gather.keep().wait()


def middle(heads_t, w_out, tokens, vectors, down_block, sizes, call_id):
    size, _, span = sizes
    rows, width = tokens.shape
    parts = rows // 128
    shape = jax.ShapeDtypeStruct
    return pl.pallas_call(
        functools.partial(middle_kernel, sizes, parts),
        out_shape=[
            shape((2 * span, heads_t.shape[0], rows), BF16),
            shape((rows, width), F32),
            shape((rows, width), F32),
            shape((2, span, rows, width), BF16),
            shape((size,) + down_block.shape, BF16),
        ],
        in_specs=[CORE, CORE, CORE, CORE, HBM],
        out_specs=[CORE, CORE, CORE, HBM, HBM],
        scratch_shapes=[pltpu.VMEM((rows, width), BF16)]
        + GroupSwap.scratch(span)
        + RingGather.scratch(size)
        + GroupGather.scratch(span, parts),
        compiler_params=pltpu.CompilerParams(
            collective_id=call_id, has_side_effects=True, vmem_limit_bytes=40 * MIB
        ),
        name="middle",
    )(heads_t, w_out, tokens, vectors, down_block)


def gelu_both(values_in):
    square = values_in * values_in
    inner = 0.7978845608028654 * values_in * (1.0 + 0.044715 * square)
    bent = jnp.tanh(inner)
    outer = 0.5 * (1.0 + bent)
    slope = 0.7978845608028654 * (1.0 + 3.0 * 0.044715 * square)
    return values_in * outer, outer + 0.5 * values_in * (1.0 - bent * bent) * slope


def feed_kernel(sizes, chunk, tile, *refs):
    where = Where(sizes)
    ins, outs, scratch = take(refs, (5, 5, len(refs) - 10))
    hidden, grad, w_up, w_down, bias = ins
    half, grad_hidden, g_up, g_down, g_bias = outs
    act, grad_pre, branch, back = scratch[:4]
    own = take(scratch[4:], (3, 6))
    span = where.span
    rows, width = grad_hidden.shape
    units = bias.shape[1]
    sum_half = CoreSum(where, branch, half, own[0])
    sum_back = GroupSum(where, back, grad_hidden, own[1])
    greet(where.group_peers())
    each = rows // chunk
    across = (((1,), (1,)), ((), ()))

    def body(step, total):
        at = step // each
        dx, dc = span - 1 - at // 2, 1 - at % 2
        inside = pl.ds(pl.multiple_of(step % each * chunk, chunk), chunk)
        first = pl.multiple_of((dc * span + dx) * rows + step % each * chunk, chunk)
        here = pl.ds(first, chunk)
        pre = jnp.dot(hidden[here, :], w_up[...], preferred_element_type=F32) + bias[...]
        value, slope = gelu_both(pre)
        value = value.astype(BF16)
        act[here, :] = value
        grad_act = lax.dot_general(grad[here, :], w_down[...], across, preferred_element_type=F32)
        low = (grad_act * slope).astype(BF16)
        grad_pre[here, :] = low
        back[dc, dx, inside, :] = lax.dot_general(
            low, w_up[...], across, preferred_element_type=F32
        ).astype(BF16)
        branch[dc, dx, inside, :] = jnp.dot(
            value, w_down[...], preferred_element_type=F32
        ).astype(BF16)
        for place in range(2 * span):
            done_dx, done_dc = span - 1 - place // 2, 1 - place % 2

            @pl.when(step == (place + 1) * each - 1)
            def _():
                if done_dc:
                    sum_back.cross(done_dx).start()
                    sum_half.cross(done_dx).start()
                elif done_dx:
                    sum_back.fold(done_dx)
                    sum_half.fold(done_dx)

        return total + jnp.sum(low.astype(F32), axis=0, keepdims=True)

    zero = jnp.zeros((1, units), F32)
    g_bias[...] = lax.fori_loop(0, 2 * span * each, body, zero)
    sum_half.fold(0)
    over = (((0,), (0,)), ((), ()))
    for low in range(0, units, tile):
        cut = slice(low, low + tile)
        g_down[cut, :] = lax.dot_general(
            act[:, cut], grad[...], over, preferred_element_type=F32
        ).astype(BF16)
        g_up[:, cut] = lax.dot_general(
            hidden[...], grad_pre[:, cut], over, preferred_element_type=F32
        ).astype(BF16)
    sum_half.finish()
    sum_back.finish()


def feed(hidden, grad, w_up, w_down, bias, sizes, call_id):
    _, _, span = sizes
    tokens, width = hidden.shape
    units = w_up.shape[1]
    rows = tokens // (2 * span)
    shape = jax.ShapeDtypeStruct
    terms = pltpu.VMEM((2, span, rows, width), BF16)
    return pl.pallas_call(
        functools.partial(feed_kernel, sizes, min(256, rows), 384 if units % 384 == 0 else units),
        out_shape=[
            shape((span, rows, width), BF16),
            shape((rows, width), F32),
            shape((width, units), BF16),
            shape((units, width), BF16),
            shape((1, units), F32),
        ],
        in_specs=[CORE] * 5,
        out_specs=[CORE] * 5,
        scratch_shapes=[pltpu.VMEM((tokens, units), BF16)] * 2
        + [terms] * 2
        + CoreSum.scratch(span, rows, width)
        + GroupSum.scratch(span, rows, width),
        compiler_params=pltpu.CompilerParams(
            collective_id=call_id, has_side_effects=True, vmem_limit_bytes=60 * MIB
        ),
        name="feed",
    )(hidden, grad, w_up, w_down, bias)


def from_patch(array, hops, size):
    if hops == 0:
        return array
    return lax.ppermute(array, "patch", [((to + hops) % size, to) for to in range(size)])


def from_core(array):
    return lax.ppermute(array, "core", [(0, 1), (1, 0)])


def group_swap(pieces, size):
    out = []
    for dc in range(2):
        row = []
        for dx in range(size):
            piece = pieces[dc][(size - dx) % size]
            piece = from_patch(piece, dx, size)
            row.append(from_core(piece) if dc else piece)
        out.append(row)
    return out


def natural(pieces, size):
    core, patch = lax.axis_index("core"), lax.axis_index("patch")
    if size == 2:
        swapped = [
            [jnp.where(patch == 0, row[0], row[1]), jnp.where(patch == 0, row[1], row[0])]
            for row in pieces
        ]
    else:
        swapped = []
        for row in pieces:
            stack = jnp.stack(row)
            swapped.append(
                [
                    lax.dynamic_index_in_dim(stack, (to - patch + size) % size, 0, False)
                    for to in range(size)
                ]
            )
    first = [jnp.where(core == 0, a, b) for a, b in zip(swapped[0], swapped[1])]
    second = [jnp.where(core == 0, b, a) for a, b in zip(swapped[0], swapped[1])]
    return first + second


def relative(blocks, size):
    core, patch = lax.axis_index("core"), lax.axis_index("patch")
    return [
        [
            lax.dynamic_index_in_dim(
                blocks, (core + dc) % 2 * size + (patch + dx) % size, 0, False
            )
            for dx in range(size)
        ]
        for dc in range(2)
    ]


def per_device(
    tokens,
    cotangent,
    clip_embed,
    timesteps,
    frame_clip,
    ada_weight,
    ada_bias,
    qkv_weight,
    query_bias,
    value_bias,
    out_weight,
    out_bias,
    up_weight,
    up_bias,
    down_weight,
    down_bias,
):
    ring_size, patch_size = lax.axis_size("ring"), lax.axis_size("patch")
    sizes = (ring_size, 2, patch_size)
    group = 2 * patch_size
    device_count = ring_size * group
    ring, core, patch = (lax.axis_index(name) for name in ("ring", "core", "patch"))
    member = core * patch_size + patch
    device = ring * group + member
    rows, width = tokens.shape[1:]
    tokens, cotangent = tokens[0], cotangent[0]
    patches = patch_size * rows
    clips = clip_embed.shape[0]
    hidden = up_weight.shape[1]
    share = width // device_count
    heads = HEADS // group
    head_width = heads * HEAD_DIM
    units = hidden // group
    mine = jnp.arange(group) == member
    mine_of_all = jnp.arange(device_count) == device

    qkv_cols = jnp.transpose(qkv_weight.reshape(share, 3, group, head_width), (2, 0, 1, 3)).reshape(
        group, share, 3 * head_width
    )
    up_cols = jnp.transpose(
        up_weight.reshape(share, ring_size, group, hidden // device_count), (2, 0, 1, 3)
    ).reshape(group, share, units)

    condition = clip_embed + sinusoid(timesteps, width)
    silu_cond, silu_back = jax.vjp(jax.nn.silu, condition)
    silu_low = silu_cond.astype(BF16)
    silu_part = lax.dynamic_slice_in_dim(silu_low, device * share, share, 1)
    mod_part = jnp.dot(silu_part, ada_weight, preferred_element_type=F32)
    shards = [ada_bias, query_bias, value_bias, out_bias, down_bias, up_bias]
    lengths = [shard.shape[0] for shard in shards]
    shards = jnp.concatenate(shards).astype(F32)
    placed = jnp.where(mine_of_all[:, None], shards[None, :], 0.0).reshape(-1)
    frame_count = 2 * ring_size
    own_frame = 2 * ring + core
    clip_part = jnp.where(
        (jnp.arange(frame_count) == own_frame) & (patch == 0), frame_clip[0].astype(F32), 0.0
    )
    vector = jnp.concatenate([mod_part.reshape(-1), placed, clip_part])

    tokens_all, w_qkv, w_out, up_block, summed = entry(
        tokens, qkv_cols, up_cols, out_weight, flat_block(vector), sizes, 1
    )
    w_qkv = w_qkv.reshape(width, 3 * head_width)
    w_out = w_out.reshape(width, width)
    summed = summed.reshape(-1)
    split = clips * 6 * width
    full = summed[split : split + placed.shape[0]].reshape(device_count, -1)
    found, at = [], 0
    for length in lengths:
        found.append(full[:, at : at + length].reshape(-1))
        at += length
    ada_full, query_full, value_full, b_out, b_down, up_full = found
    modulation = summed[:split].reshape(clips, 6 * width) + ada_full[None, :]
    clips_of = summed[split + placed.shape[0] :][:frame_count]
    b_query = lax.dynamic_slice_in_dim(query_full, member * head_width, head_width, 0)
    b_value = lax.dynamic_slice_in_dim(value_full, member * head_width, head_width, 0)
    b_up = lax.dynamic_index_in_dim(
        up_full.reshape(ring_size, group, hidden // device_count), member, 1, False
    ).reshape(units)
    own_clip = frame_clip[0]
    other_clip = lax.dynamic_index_in_dim(clips_of, 2 * ring + 1 - core, 0, False).astype(jnp.int32)
    own_mod = lax.dynamic_index_in_dim(modulation, own_clip, 0, False)
    other_mod = lax.dynamic_index_in_dim(modulation, other_clip, 0, False)
    shift_one, scale_one, gate_one, shift_two, scale_two, gate_two = (
        own_mod[at * width : (at + 1) * width] for at in range(6)
    )
    both = jnp.stack([own_mod[: 2 * width], other_mod[: 2 * width]])[:, None, :]

    normed_all, _ = layer_norm(tokens_all.astype(F32).reshape(2, patches, width))
    hidden_one = (
        (normed_all * (1.0 + both[:, :, width:]) + both[:, :, :width])
        .astype(BF16)
        .reshape(2 * patches, width)
    )
    qkv_bias = jnp.concatenate([b_query, jnp.zeros_like(b_query), b_value])
    projected = (
        lax.dot_general(w_qkv, hidden_one, (((0,), (1,)), ((), ())), preferred_element_type=F32)
        + qkv_bias[:, None]
    ).astype(BF16)
    qkv = projected.reshape(3 * heads, HEAD_DIM, 2 * patches)
    grad_out = cotangent.astype(F32)
    grad_branch_two = (gate_two * grad_out).astype(BF16)
    attended_t, lse, w_up, gb_two_all = attention(
        qkv, up_block, grad_branch_two, patches, sizes, 2
    )
    w_up = w_up.reshape(width, units)

    vectors = jnp.stack([b_out, gate_one, scale_two, shift_two] + [b_out] * 4)
    attended, branch_one, midway, hidden_two_all, w_down = middle(
        attended_t.reshape(head_width, 2 * patches), w_out, tokens, vectors, down_weight, sizes, 3
    )
    attended = attended.reshape(width, rows)
    w_down = w_down.reshape(units, width)

    branch_half, grad_hidden_two, g_up, g_down, g_up_b = feed(
        hidden_two_all.reshape(2 * patches, width),
        gb_two_all.reshape(2 * patches, width),
        w_up,
        w_down,
        b_up[None, :],
        sizes,
        4,
    )
    g_up_b = g_up_b[0]
    g_down_b = jnp.sum(grad_branch_two.astype(F32), axis=0)
    block_rows = width // ring_size
    (share_down,) = exchange(
        [(RingSum, g_down.reshape(ring_size, units // ring_size, width), F32)], sizes, 5
    )

    input_rows = tokens.astype(F32)
    normed_two, inv_two = layer_norm(midway)
    grad_shift_two = jnp.sum(grad_hidden_two, axis=0)
    grad_scale_two = jnp.sum(grad_hidden_two * normed_two, axis=0)
    grad_midway = grad_out + norm_back(grad_hidden_two * (1.0 + scale_two), normed_two, inv_two)
    grad_gate_one = jnp.sum(grad_midway * branch_one, axis=0)
    grad_branch_one = (gate_one * grad_midway).astype(BF16)
    g_out_b = jnp.sum(grad_branch_one.astype(F32), axis=0)
    grad_attended = lax.dot_general(
        w_out, grad_branch_one, (((1,), (1,)), ((), ())), preferred_element_type=F32
    ).astype(BF16)
    g_out = jnp.dot(attended, grad_branch_one, preferred_element_type=F32).astype(BF16)
    swapped = group_swap(
        relative(grad_attended.reshape(group, head_width, rows), patch_size), patch_size
    )
    grad_mix = jnp.concatenate([piece for row in swapped for piece in row], axis=1)
    grad_projected, sum_up, branch_two = attention_back(
        qkv,
        grad_mix.reshape(heads, HEAD_DIM, 2 * patches),
        lse,
        g_up.reshape(ring_size, block_rows, units),
        branch_half,
        patches,
        sizes,
        6,
    )
    grad_projected = grad_projected.reshape(3 * head_width, 2 * patches)
    branch_two = branch_two + b_down
    output = (midway + gate_two * branch_two).astype(BF16)
    grad_gate_two = jnp.sum(grad_out * branch_two, axis=0)

    g_qkv = lax.dot_general(
        hidden_one, grad_projected, (((0,), (1,)), ((), ())), preferred_element_type=F32
    ).astype(BF16)
    g_query_b = jnp.sum(grad_projected[:head_width].astype(F32), axis=1)
    g_value_b = jnp.sum(grad_projected[2 * head_width :].astype(F32), axis=1)
    grad_hidden_terms = lax.dot_general(
        grad_projected, w_qkv, (((0,), (1,)), ((), ())), preferred_element_type=F32
    ).astype(BF16)
    grad_hidden_one, sum_qkv, sum_out = exchange(
        [
            (GroupSum, grad_hidden_terms.reshape(2, patch_size, rows, width), F32),
            (RingSum, g_qkv.reshape(ring_size, block_rows, -1), BF16),
            (RingSum, g_out.reshape(ring_size, block_rows, width), BF16),
        ],
        sizes,
        7,
    )

    normed_one, inv_one = layer_norm(input_rows)
    grad_shift_one = jnp.sum(grad_hidden_one, axis=0)
    grad_scale_one = jnp.sum(grad_hidden_one * normed_one, axis=0)
    tokens_grad = (
        grad_midway + norm_back(grad_hidden_one * (1.0 + scale_one), normed_one, inv_one)
    ).astype(BF16)

    pieces = jnp.concatenate([sum_qkv, sum_up, sum_out], axis=1).reshape(group, share, -1)
    got_w = natural(group_swap(relative(pieces, patch_size), patch_size), patch_size)
    stacked = jnp.stack(got_w).astype(F32)
    share_qkv = jnp.transpose(
        stacked[:, :, : 3 * head_width].reshape(group, share, 3, head_width), (1, 2, 0, 3)
    ).reshape(share, 3 * width)
    share_up = jnp.transpose(
        stacked[:, :, 3 * head_width : 3 * head_width + units].reshape(
            group, share, ring_size, hidden // device_count
        ),
        (1, 2, 0, 3),
    ).reshape(share, hidden)
    share_out = jnp.sum(stacked[:, :, 3 * head_width + units :], axis=0)

    frame_grads = jnp.concatenate(
        [
            grad_shift_one,
            grad_scale_one,
            grad_gate_one,
            grad_shift_two,
            grad_scale_two,
            grad_gate_two,
        ]
    )
    clip_terms = jnp.where(
        (jnp.arange(clips) == own_clip)[:, None], frame_grads[None, :], 0.0
    ).reshape(-1)
    terms = [
        clip_terms,
        jnp.where(mine[:, None], g_query_b[None, :], 0.0).reshape(-1),
        jnp.where(mine[:, None], g_value_b[None, :], 0.0).reshape(-1),
        g_out_b,
        g_down_b,
        jnp.where(mine[None, :, None], g_up_b.reshape(ring_size, 1, -1), 0.0).reshape(-1),
    ]
    (summed,) = exchange([(AllSum, flat_block(jnp.concatenate(terms)))], sizes, 8)
    summed = summed.reshape(-1)
    got, at = [], 0
    for item in terms:
        got.append(summed[at : at + item.shape[0]])
        at += item.shape[0]
    mod_low = got[0].reshape(clips, 6 * width).astype(BF16)

    def own(vector):
        length = vector.shape[0] // device_count
        return lax.dynamic_slice_in_dim(vector, device * length, length, 0)

    ada_bias_grad = own(jnp.sum(mod_low.astype(F32), axis=0))
    ada_weight_grad = lax.dot_general(
        silu_part, mod_low, (((0,), (0,)), ((), ())), preferred_element_type=F32
    )
    grad_silu_part = lax.dot_general(
        mod_low, ada_weight, (((1,), (1,)), ((), ())), preferred_element_type=F32
    )
    spread = jnp.where(mine_of_all[None, :, None], grad_silu_part[:, None, :], 0.0).reshape(-1)
    (grad_silu,) = exchange([(AllSum, flat_block(spread))], sizes, 9)
    grad_silu = grad_silu.reshape(-1)[: clips * width].reshape(clips, width)
    clip_grad = silu_back(grad_silu)[0]
    return (
        output[None],
        tokens_grad[None],
        clip_grad,
        ada_weight_grad,
        ada_bias_grad,
        share_qkv,
        own(got[1]),
        own(got[2]),
        share_out,
        own(got[3]),
        share_up,
        own(got[5]),
        share_down,
        own(got[4]),
    )


def solution(mesh):
    frames, patch = mesh.shape["frames"], mesh.shape["patch"]
    inner = Mesh(mesh.devices.reshape(frames // 2, 2, patch), ("ring", "core", "patch"))
    every = ("ring", "core", "patch")
    tokens = P(("ring", "core"), "patch", None)
    matrix = P(every, None)
    vector = P(every)
    return jax.shard_map(
        per_device,
        mesh=inner,
        in_specs=(
            tokens,
            tokens,
            P(),
            P(),
            P(("ring", "core")),
            matrix,
            vector,
            matrix,
            vector,
            vector,
            matrix,
            vector,
            matrix,
            vector,
            matrix,
            vector,
        ),
        out_specs=(
            tokens,
            tokens,
            P(),
            matrix,
            vector,
            matrix,
            vector,
            vector,
            matrix,
            vector,
            matrix,
            vector,
            matrix,
            vector,
        ),
        check_vma=False,
    )
```

time: 740 us -> 541 us (0.73)
  waiting for transfers between devices: 108 us -> 6.14 us
  matrix products: 103 us -> 27.8 us
  Pallas kernels: 349 us -> 402 us
  local copies, waits for them, and re-layouts: 89.9 us -> 58.2 us
  other arithmetic: 63.5 us -> 34.7 us
  starting transfers between devices: 17.5 us -> 4.47 us
    ppermute x14 -> x4, waiting for transfers between devices: 107 us -> 6.13 us  [from_patch(): lax.ppermute(array, 'patch', [((to + hops) % size, to) for to in range(si...]
    dot_general x7 -> x0, matrix products: 78.7 us -> none  [the longest x1 19.2 us: per_device(): lax.dot_general(gb_two_all, w_down, (((1,), (1,)), ((), ())), preferred_e...]
    pallas_call x9, Pallas kernels: 349 us -> 402 us  [the longest x4 146 us: exchange(): pl.pallas_call(functools.partial(exchange_kernel, sizes, tuple(kinds), tu...]
    ppermute x14 -> x4, starting transfers between devices: 15.8 us -> 4.05 us  [from_patch(): lax.ppermute(array, 'patch', [((to + hops) % size, to) for to in range(si...]
    add x4 -> x2, other arithmetic: 9.72 us -> 0.73 us  [the longest x1 0.7 us: per_device(): 1.0 + scale_two]
    concatenate x6 -> x1, other arithmetic: 9.32 us -> 0.43 us  [attention_back(): return (jnp.concatenate(parts, axis=0), up_sum, half_sum)]
    slice x7, local copies, waits for them, and re-layouts: 8.37 us -> 0.18 us  [the longest x3 0.16 us: per_device(): found.append(full[:, at:at + length].reshape(-1))]
    unnamed x216 -> x161, local copies, waits for them, and re-layouts: 23.5 us -> 28.9 us
  transfers between devices with their start and end apart: 28 -> 8, of which waited for: 9 -> 2; matrix products, arithmetic and copies ran while one was open for 21% -> 4% of each run, Pallas kernels for 35% -> 7%
where the time goes in v2:
time: 541 us; the launch traced here: 537 us
  Pallas kernels  402 us (74%)
  local copies, waits for them, and re-layouts  58.2 us (11%)
  other arithmetic  34.7 us (6%)
  matrix products  27.8 us (5%)
  waiting for transfers between devices  6.14 us (1%)
    pallas_call x4, Pallas kernels, exchange(): pl.pallas_call(functools.partial(exchange_kernel, sizes, tuple(kinds), tu...  146 us
    pallas_call x1, Pallas kernels, entry(): pl.pallas_call(functools.partial(entry_kernel, sizes, share), out_shape=[...  63.7 us
    pallas_call x1, Pallas kernels, feed(): pl.pallas_call(functools.partial(feed_kernel, sizes, min(256, rows), 384...  57.3 us
    pallas_call x1, Pallas kernels, middle(): pl.pallas_call(functools.partial(middle_kernel, sizes, parts), out_shape=...  48.5 us
    pallas_call x1, Pallas kernels, attention_back(): pl.pallas_call(functools.partial(attention_back_kernel, sizes, factor, mi...  44.2 us
    pallas_call x1, Pallas kernels, attention(): pl.pallas_call(functools.partial(attention_kernel, sizes, factor, min(256...  42.4 us
    unnamed x161, local copies, waits for them, and re-layouts  28.9 us
  transfers between devices with their start and end apart: 8, of which 2 were waited for; matrix products, arithmetic and copies ran while one was open for 4% of the time, Pallas kernels for 7%

profile of v2, /device:TPU:0, one launch (start us, length us, event | category | flops | bytes accessed | tf_op | source)
XLA Modules:
  0.0 536.8 jit_solution(18330550437828630449)
XLA Ops:
  9.1 63.7 %entry.1 = (bf16[2,2,512,1152]{3,2,1,0:T(8,128)(2,1)S(1)}, bf16[8,144,864]{2,1,0:T(8,128)(2,1)S(1)}, bf16[8,144,1152]{2,1,0:T(8,128)(2,1)S(1)}, bf16[144,1152]{1,0:T(8,128)(2,1)S(1)}, f32[240,128]{1,0:T(8,128)S(1)}) custom-call(bf16[512,1152]{1,0:T(8,128)(2,1)S(1)} %bitcast.151, bf16[4,36,864]{2,1,0:T(8,128)(2,1)S(1)} %copy.43.refs_1_, ...), custom_call_target="tpu_custom_call" | custom-call | tf_op jit(solution)/shard_map/entry/pallas_call | solution.py:596
  79.5 3.2 convert_reduce_fusion
  87.7 3.7 fusion.3
  91.4 5.2 add_convert_fusion
  96.6 42.4 %attention.1 = (bf16[4,72,2048]{2,1,0:T(8,128)(2,1)S(1)}, f32[4,1,2048]{2,1,0:T(1,128)S(1)}, bf16[8,144,1152]{2,1,0:T(8,128)(2,1)S(1)}, bf16[2,2,512,1152]{3,2,1,0:T(8,128)(2,1)S(1)}) custom-call(bf16[12,72,2048]{2,1,0:T(8,128)(2,1)S(1)} %bitcast.165, bf16[12,72,2048]{2,1,0:T(8,128)(2,1)S(1)} %bitcast.166, bf16[12,72,2048]{2,1,0:T(8,128)(2,1)S(1)} %bitcast.167, ...), custom_call_target="tpu_custom_call" | custom-call | flops 8589934592 | bytes 4718592 | tf_op jit(solution)/shard_map/attention/pallas_call | solution.py:747
  148.2 48.5 %middle.1 = (bf16[4,288,512]{2,1,0:T(8,128)(2,1)S(1)}, f32[512,1152]{1,0:T(8,128)S(1)}, f32[512,1152]{1,0:T(8,128)S(1)}, bf16[2,2,512,1152]{3,2,1,0:T(8,128)(2,1)}, bf16[8,144,1152]{2,1,0:T(8,128)(2,1)S(1)}) custom-call(bf16[288,2048]{1,0:T(8,128)(2,1)S(1)} %bitcast.160, bf16[1152,1152]{1,0:T(8,128)(2,1)S(1)} %bitcast.158, bf16[512,1152]{1,0:T(8,128)(2,1)S(1)} %bitcast.152, ...), custom_call_target="tpu_custom_call" | custom-call | tf_op jit(solution)/shard_map/middle/pallas_call | solution.py:935
  201.2 57.3 %feed.1 = (bf16[2,512,1152]{2,1,0:T(8,128)(2,1)}, f32[512,1152]{1,0:T(8,128)}, bf16[1152,1152]{1,0:T(8,128)(2,1)}, bf16[1152,1152]{1,0:T(8,128)(2,1)}, f32[1,1152]{1,0:T(1,128)}) custom-call(bf16[2048,1152]{1,0:T(8,128)(2,1)} %bitcast.171, bf16[2048,1152]{1,0:T(8,128)(2,1)} %bitcast.154, bf16[1152,1152]{1,0:T(8,128)(2,1)} %bitcast.155, ...), custom_call_target="tpu_custom_call" | custom-call | tf_op jit(solution)/shard_map/feed/pallas_call | solution.py:1038
  258.5 3.4 multiply_reduce_fusion.1
  261.9 3.1 convert_reduce_fusion.3
  266.1 2.7 convolution_convert_fusion.3
  268.9 2.3 constant_dynamic-slice_fusion.2
  274.6 2.3 fusion.15
  281.7 40.0 %exchange_5.1 = f32[144,1152]{1,0:T(8,128)S(1)} custom-call(bf16[8,144,1152]{2,1,0:T(8,128)(2,1)S(1)} %bitcast.157), custom_call_target="tpu_custom_call" | custom-call | tf_op jit(solution)/shard_map/exchange_5/pallas_call | solution.py:663
  324.3 4.8 convolution_convert_fusion.1
  330.2 44.2 %attention_back.1 = (bf16[4,72,2048]{2,1,0:T(8,128)(2,1)S(1)}, bf16[4,72,2048]{2,1,0:T(8,128)(2,1)S(1)}, bf16[4,72,2048]{2,1,0:T(8,128)(2,1)S(1)}, bf16[144,1152]{1,0:T(8,128)(2,1)S(1)}, f32[512,1152]{1,0:T(8,128)}) custom-call(bf16[12,72,2048]{2,1,0:T(8,128)(2,1)} %bitcast.168, bf16[12,72,2048]{2,1,0:T(8,128)(2,1)} %bitcast.169, ...), custom_call_target="tpu_custom_call" | custom-call | flops 21474836480 | bytes 9437184 | tf_op jit(solution)/shard_map/attention_back/pallas_call | solution.py:846
  376.1 7.4 %convolution_convert_fusion = bf16[2048,1152]{1,0:T(8,128)(2,1)} fusion(bf16[864,2048]{1,0:T(8,128)(2,1)S(1)} %bitcast.178, bf16[1152,864]{1,0:T(8,128)(2,1)S(1)} %bitcast.163), kind=kOutput, calls=%fused_computation.6 | convolution fusion | flops 4079222784 | bytes 10248192 | tf_op jit(solution)/shard_map/dot_general | solution.py:1284
  383.4 5.9 %convolution_convert_fusion.2 = bf16[1152,864]{0,1:T(8,128)(2,1)} fusion(bf16[864,2048]{1,0:T(8,128)(2,1)S(1)} %bitcast.179, bf16[2048,1152]{1,0:T(8,128)(2,1)S(1)} %bitcast.177), kind=kOutput, calls=%fused_computation.14 | convolution fusion | flops 4077858816 | bytes 10248192 | tf_op jit(solution)/shard_map/dot_general | solution.py:1279
  391.0 4.3 copy.45
  396.9 74.2 %exchange_7.1 = (f32[512,1152]{1,0:T(8,128)S(1)}, bf16[144,864]{1,0:T(8,128)(2,1)S(1)}, bf16[144,1152]{1,0:T(8,128)(2,1)S(1)}) custom-call(bf16[2,2,512,1152]{3,2,1,0:T(8,128)(2,1)} %bitcast.173, bf16[8,144,864]{2,1,0:T(8,128)(2,1)S(1)} %bitcast.153, bf16[8,144,1152]{2,1,0:T(8,128)(2,1)} %bitcast.181), custom_call_target="tpu_custom_call" | custom-call | tf_op jit(solution)/shard_map/exchange_7/pallas_call | solution.py:663
  479.2 17.0 %exchange_8.1 = f32[184,128]{1,0:T(8,128)S(1)} custom-call(f32[184,128]{1,0:T(8,128)S(1)} %pad_bitcast_fusion.refs_0_), custom_call_target="tpu_custom_call" | custom-call | tf_op jit(solution)/shard_map/exchange_8/pallas_call | solution.py:663
  496.9 14.5 %exchange_9.1 = f32[24,128]{1,0:T(8,128)S(1)} custom-call(f32[24,128]{1,0:T(8,128)S(1)} %pad_bitcast_fusion.1.refs_0_), custom_call_target="tpu_custom_call" | custom-call | tf_op jit(solution)/shard_map/exchange_9/pallas_call | solution.py:663
  519.1 2.8 collective-permute-done.6
  523.3 3.4 collective-permute-done.4
  532.4 3.2 reshape.509
  (297 shorter events, 73.7 us)
Async XLA Ops:
  0.6 7.8 %copy-start = (bf16[36,6912]{1,0:T(8,128)(2,1)S(1)}, bf16[36,6912]{1,0:T(8,128)(2,1)}, u32[]{:S(2)}) copy-start(bf16[36,6912]{1,0:T(8,128)(2,1)} %param.21) | copy-start | bytes 1492996
  2.7 6.4 %copy-start.3 = (bf16[1,512,1152]{2,1,0:T(8,128)(2,1)S(1)}, bf16[1,512,1152]{2,1,0:T(8,128)(2,1)}, u32[]{:S(2)}) copy-start(bf16[1,512,1152]{2,1,0:T(8,128)(2,1)} %param.16) | copy-start | bytes 3538948
  7.3 75.4 %copy-start.61 = (pred[32]{0:T(512)(128)(4,1)}, pred[32]{0:T(512)(128)(4,1)S(1)}, u32[]{:S(2)}) copy-start(pred[32]{0:T(512)(128)(4,1)S(1)} %iota_compare_fusion.3) | copy-start | bytes 100
  96.6 42.5 %copy-start.29 = (bf16[864,2048]{1,0:T(8,128)(2,1)}, bf16[864,2048]{1,0:T(8,128)(2,1)S(1)}, u32[]{:S(2)}) copy-start(bf16[864,2048]{1,0:T(8,128)(2,1)S(1)} %add_convert_fusion) | copy-start | bytes 10616836
  96.6 47.3 %copy-start.23 = (bf16[144,1152]{1,0:T(8,128)(2,1)S(1)}, bf16[144,1152]{1,0:T(8,128)(2,1)}, u32[]{:S(2)}) copy-start(bf16[144,1152]{1,0:T(8,128)(2,1)} %refs_4_.1) | copy-start | bytes 995332
  271.1 53.2 %collective-permute-start.2 = (bf16[288,512]{1,0:T(8,128)(2,1)}, bf16[288,512]{1,0:T(8,128)(2,1)}, u32[]{:S(2)}, u32[]{:S(2)}) collective-permute-start(bf16[288,512]{1,0:T(8,128)(2,1)} %get-tuple-element.98), channel_id=1, source_target_pairs={{1,0},{0,1},{3,2},{2,3},{5,4},{4,5},{7,6},{6,7},{9,8},{8,9},{11,10... | collective-permute-start | bytes 884744 | tf_op jit(solution)/shard_map/ppermute | solution.py:1063
  271.9 57.3 %collective-permute-start.1 = (bf16[288,512]{1,0:T(8,128)(2,1)}, bf16[288,512]{1,0:T(8,128)(2,1)S(1)}, u32[]{:S(2)}, u32[]{:S(2)}) collective-permute-start(bf16[288,512]{1,0:T(8,128)(2,1)} %get-tuple-element.99), channel_id=1, source_target_pairs={{0,2},{2,0},{1,3},{3,1},{4,6},{6,4},{5,7},{7,5},{8,10},{10,8},{9,1... | collective-permute-start | bytes 884744 | tf_op jit(solution)/shard_map/ppermute | solution.py:1067
  271.9 57.3 %collective-permute-start = (bf16[288,512]{1,0:T(8,128)(2,1)}, bf16[288,512]{1,0:T(8,128)(2,1)}, u32[]{:S(2)}, u32[]{:S(2)}) collective-permute-start(bf16[288,512]{1,0:T(8,128)(2,1)} %get-tuple-element.100), channel_id=1, source_target_pairs={{1,0},{0,1},{3,2},{2,3},{5,4},{4,5},{7,6},{6,7},{9,8},{8,9},{11,10... | collective-permute-start | bytes 884744 | tf_op jit(solution)/shard_map/ppermute | solution.py:1063
  324.3 4.8 collective-permute-start.3
  374.5 8.9 %slice-start = ((s8[4718592]{0:T(1024)(128)(4,1)}), s8[4194304]{0:T(1024)(128)(4,1)S(1)}, s32[]{:S(2)}) async-start(s8[4718592]{0:T(1024)(128)(4,1)} %bitcast.175), calls=%async_computation | async-start | bytes 8388608
  376.1 7.4 %slice-start.1 = ((s8[4718592]{0:T(1024)(128)(4,1)}), s8[524288]{0:T(1024)(128)(4,1)S(1)}, s32[]{:S(2)}) async-start(s8[4718592]{0:T(1024)(128)(4,1)} %bitcast.175), calls=%async_computation.1 | async-start | bytes 1048576
  396.9 74.3 %copy-start.6 = (bf16[1,512,1152]{2,1,0:T(8,128)(2,1)S(1)}, bf16[1,512,1152]{2,1,0:T(8,128)(2,1)}, u32[]{:S(2)}) copy-start(bf16[1,512,1152]{2,1,0:T(8,128)(2,1)} %param.16) | copy-start | bytes 3538948
  396.9 74.3 %copy-start.40 = (f32[1152]{0:T(1024)S(1)}, f32[1152]{0:T(1024)}, u32[]{:S(2)}) copy-start(f32[1152]{0:T(1024)} %get-tuple-element.116) | copy-start | bytes 13828
  396.9 74.3 %copy-start.52 = (f32[512]{0:T(512)S(1)}, f32[512]{0:T(512)}, u32[]{:S(2)}) copy-start(f32[512]{0:T(512)} %copy-done.51) | copy-start | bytes 6148
  396.9 74.3 %copy-start.55 = (f32[512]{0:T(512)S(1)}, f32[512]{0:T(512)}, u32[]{:S(2)}) copy-start(f32[512]{0:T(512)} %add_rsqrt_fusion) | copy-start | bytes 6148
  476.2 20.4 %copy-start.62 = (pred[32]{0:T(512)(128)(4,1)S(1)}, pred[32]{0:T(512)(128)(4,1)}, u32[]{:S(2)}) copy-start(pred[32]{0:T(512)(128)(4,1)} %copy-done.61) | copy-start | bytes 100
  476.2 35.2 %copy-start.22 = (bf16[144,1152]{1,0:T(8,128)(2,1)S(1)}, bf16[144,1152]{1,0:T(8,128)(2,1)}, u32[]{:S(2)}) copy-start(bf16[144,1152]{1,0:T(8,128)(2,1)} %copy-done.21) | copy-start | bytes 995332
  511.4 7.1 %copy-start.44 = (f32[2,1152]{1,0:T(2,128)S(1)}, f32[2,1152]{1,0:T(2,128)}, u32[]{:S(2)}) copy-start(f32[2,1152]{1,0:T(2,128)} %copy-done.43) | copy-start | bytes 27652
  511.4 7.1 %copy-start.46 = (f32[2,1152]{1,0:T(2,128)S(1)}, f32[2,1152]{1,0:T(2,128)}, u32[]{:S(2)}) copy-start(f32[2,1152]{1,0:T(2,128)} %copy-done.45) | copy-start | bytes 27652
  511.4 10.5 %copy-start.60 = (bf16[2,36]{1,0:T(2,128)(2,1)S(1)}, bf16[2,36]{1,0:T(2,128)(2,1)}, u32[]{:S(2)}) copy-start(bf16[2,36]{1,0:T(2,128)(2,1)} %copy-done.59) | copy-start | bytes 436
  512.5 10.8 %collective-permute-start.5 = (bf16[36,3168]{1,0:T(8,128)(2,1)S(1)}, bf16[36,3168]{1,0:T(8,128)(2,1)S(1)}, u32[]{:S(2)}, u32[]{:S(2)}) collective-permute-start(bf16[36,3168]{1,0:T(8,128)(2,1)S(1)} %get-tuple-element.103), channel_id=1, source_target_pairs={{0,2},{2,0},{1,3},{3,1},{4,6},{6,4},{5,7},{7,5},{8,10},{10,8},{9,1... | collective-permute-start | bytes 684296 | tf_op jit(solution)/shard_map/ppermute | solution.py:1067
  512.9 9.0 %collective-permute-start.6 = (bf16[36,3168]{1,0:T(8,128)(2,1)S(1)}, bf16[36,3168]{1,0:T(8,128)(2,1)S(1)}, u32[]{:S(2)}, u32[]{:S(2)}) collective-permute-start(bf16[36,3168]{1,0:T(8,128)(2,1)S(1)} %get-tuple-element.102), channel_id=1, source_target_pairs={{1,0},{0,1},{3,2},{2,3},{5,4},{4,5},{7,6},{6,7},{9,8},{8,9},{11,10... | collective-permute-start | bytes 684296 | tf_op jit(solution)/shard_map/ppermute | solution.py:1063
  514.2 12.4 %collective-permute-start.4 = (bf16[36,3168]{1,0:T(8,128)(2,1)S(1)}, bf16[36,3168]{1,0:T(8,128)(2,1)S(1)}, u32[]{:S(2)}, u32[]{:S(2)}) collective-permute-start(bf16[36,3168]{1,0:T(8,128)(2,1)S(1)} %get-tuple-element.101), channel_id=1, source_target_pairs={{1,0},{0,1},{3,2},{2,3},{5,4},{4,5},{7,6},{6,7},{9,8},{8,9},{11,10... | collective-permute-start | bytes 684296 | tf_op jit(solution)/shard_map/ppermute | solution.py:1063
  521.9 4.7 collective-permute-start.7
  (58 other events, 157.0 us)

commit v3 on v2

v3 whole, which is shorter than its diff:
```python
import functools
import math

import jax
import jax.numpy as jnp
from jax import lax
from jax.experimental import pallas as pl
from jax.experimental.pallas import tpu as pltpu
from jax.sharding import Mesh
from jax.sharding import PartitionSpec as P

HEADS = 16
HEAD_DIM = 72
BF16 = jnp.bfloat16
F32 = jnp.float32
LOG2E = 1.4426950408889634
MESH_ID = pl.DeviceIdType.MESH
MIB = 2**20


def layer_norm(values_in):
    centre = values_in - jnp.mean(values_in, axis=-1, keepdims=True)
    spread = jnp.mean(centre * centre, axis=-1, keepdims=True)
    inv_std = lax.rsqrt(spread + 1e-06)
    return (centre * inv_std, inv_std)


def norm_back(grad_normed, normed, inv_std):
    mean_grad = jnp.mean(grad_normed, axis=-1, keepdims=True)
    mean_prod = jnp.mean(grad_normed * normed, axis=-1, keepdims=True)
    return (grad_normed - mean_grad - normed * mean_prod) * inv_std


def gelu_tanh(values_in):
    inner = 0.7978845608028654 * (values_in + 0.044715 * values_in * values_in * values_in)
    return 0.5 * values_in * (1.0 + jnp.tanh(inner))


def sinusoid(steps_in, width_in):
    half_width = width_in // 2
    freqs = jnp.exp(-math.log(10000.0) * jnp.arange(half_width, dtype=jnp.float32) / half_width)
    angles = steps_in.astype(jnp.float32)[:, None] * freqs[None, :]
    return jnp.concatenate([jnp.cos(angles), jnp.sin(angles)], axis=1)


class Where:
    def __init__(self, sizes):
        self.size, _, self.span = sizes
        self.ring, self.core, self.patch = (
            lax.axis_index(name) for name in ("ring", "core", "patch")
        )
        along, across = self.ring // 2, self.ring % 2
        self.place = (1 - across) * along + across * (self.size - 1 - along)
        self.member = self.core * self.span + self.patch

    def at_place(self, place):
        place = (place + 2 * self.size) % self.size
        back = place // (self.size // 2)
        return (1 - back) * 2 * place + back * (2 * (self.size - 1 - place) + 1)

    def neighbour(self, step):
        return (self.at_place(self.place + step), self.core, self.patch)

    def peer(self, dc, dx):
        core = 1 - self.core if dc else self.core
        return (self.ring, core, (self.patch + dx) % self.span)

    def peer_member(self, dc, dx):
        _, core, patch = self.peer(dc, dx)
        return core * self.span + patch

    def ring_peers(self):
        return [self.neighbour(1), self.neighbour(-1)]

    def group_peers(self):
        return [
            self.peer(dc, dx) for dc in range(2) for dx in range(self.span) if dc or dx
        ]


def greet(peers):
    barrier = pltpu.get_barrier_semaphore()
    for peer in peers:
        pl.semaphore_signal(barrier, inc=1, device_id=peer, device_id_type=MESH_ID)
    pl.semaphore_wait(barrier, len(peers))


def remote(source, target, send_sem, recv_sem, peer):
    return pltpu.make_async_remote_copy(
        src_ref=source,
        dst_ref=target,
        send_sem=send_sem,
        recv_sem=recv_sem,
        device_id=peer,
        device_id_type=MESH_ID,
    )


def strands(rows, columns):
    by_rows = rows % 16 == 0
    tile = 16 if by_rows else 128
    tiles = (rows if by_rows else columns) // tile
    sizes = [tiles // 4 + (at < tiles % 4) for at in range(4)]
    found, low = [], 0
    for at, count in enumerate(sizes):
        cut = pl.ds(low * tile, count * tile)
        found.append((at // 2, (cut, slice(None)) if by_rows else (slice(None), cut)))
        low += count
    return found


class RingGather:
    @staticmethod
    def scratch(size):
        dma = pltpu.SemaphoreType.DMA
        return [dma((4, size - 1)), dma((4, size - 1)), dma((1,))]

    def __init__(self, where, block, out, sems):
        self.where, self.block, self.out = where, block, out
        self.send, self.recv, self.own = sems
        self.parts = strands(*block.shape)
        self.events = 2 * (where.size - 1) + 1

    def keep(self):
        return pltpu.make_async_copy(self.block, self.out.at[self.where.ring], self.own.at[0])

    def copy(self, at, step):
        where = self.where
        way, part = self.parts[at]
        sign = (-1, 1)[way]
        slot = where.at_place(where.place + sign * step)
        target = self.out.at[(slot,) + part]
        source = target if step else self.block.at[part]
        return remote(
            source, target, self.send.at[at, step], self.recv.at[at, step], where.neighbour(-sign)
        )

    def run(self, event):
        step, piece = event // 2, event % 2
        if event == 0:
            self.keep().start()
        if event < self.events - 1:
            for at in (piece, piece + 2):
                if step:
                    self.copy(at, step - 1).wait_recv()
                self.copy(at, step).start()
        else:
            for at in range(4):
                self.copy(at, step - 1).wait_recv()
                for past in range(step):
                    self.copy(at, past).wait_send()
            self.keep().wait()


class RingGatherSplit:
    @staticmethod
    def scratch(size):
        dma, half = pltpu.SemaphoreType.DMA, size // 2
        return [dma((2, half))] * 4 + [dma((1,))]

    def __init__(self, where, block, out, sems):
        self.where, self.block, self.out = where, block, out
        self.send, self.recv, self.send_core, self.recv_core, self.own = sems
        self.half = where.size // 2
        self.events = self.half + 2
        cut = -(-block.shape[0] // 32) * 16
        self.parts = (pl.ds(0, cut), pl.ds(cut, block.shape[0] - cut))

    def keep(self):
        return pltpu.make_async_copy(self.block, self.out.at[self.where.ring], self.own.at[0])

    def slot(self, step, at):
        where = self.where
        place = where.at_place(where.place + (2 * where.core - 1) * step)
        return self.out.at[place, self.parts[at]]

    def copy(self, step, at):
        where = self.where
        target = self.slot(step, at)
        source = target if step else self.block.at[self.parts[at]]
        peer = where.neighbour(1 - 2 * where.core)
        return remote(source, target, self.send.at[at, step], self.recv.at[at, step], peer)

    def hand(self, step, at):
        target = self.slot(step + 1, at)
        return remote(
            target,
            target,
            self.send_core.at[at, step],
            self.recv_core.at[at, step],
            self.where.peer(1, 0),
        )

    def run(self, step):
        half = self.half
        if step == 0:
            self.keep().start()
        for at in range(2):
            if 0 < step <= half:
                self.copy(step - 1, at).wait_recv()
            if step < half:
                self.copy(step, at).start()
            if 0 < step < half:
                self.hand(step - 1, at).start()
            if step == half + 1:
                for past in range(half):
                    self.copy(past, at).wait_send()
                for past in range(half - 1):
                    self.hand(past, at).wait()
        if step == half + 1:
            self.keep().wait()


class RingSum:
    @staticmethod
    def scratch(size, rows, columns):
        dma = pltpu.SemaphoreType.DMA
        slots = pltpu.VMEM((size - 1, rows, columns), BF16)
        return [slots, slots, dma((4, size - 1)), dma((4, size - 1))]

    def __init__(self, where, terms, out, scratch):
        self.where, self.terms, self.out = where, terms, out
        self.held, self.landed, self.send, self.recv = scratch
        self.parts = strands(*out.shape)
        self.events = 2 * where.size

    def copy(self, at, step):
        way, part = self.parts[at]
        part = (step,) + part
        return remote(
            self.held.at[part],
            self.landed.at[part],
            self.send.at[at, step],
            self.recv.at[at, step],
            self.where.neighbour((1, -1)[way]),
        )

    def term(self, slot, part):
        if len(self.terms.shape) == 3:
            return self.terms[(slot,) + part]
        rows = self.out.shape[0]
        first = pl.multiple_of(slot * rows + part[0].start, 16)
        return self.terms[(pl.ds(first, part[0].size), part[1])]

    def run(self, event):
        step, piece = event // 2, event % 2
        where, last = self.where, self.where.size - 2
        for at in (piece, piece + 2):
            way, part = self.parts[at]
            slot = where.at_place(where.place + (-1, 1)[way] * (step + 1))
            total = self.term(slot, part)
            if step:
                self.copy(at, step - 1).wait_recv()
                total = total.astype(F32) + self.landed[(step - 1,) + part].astype(F32)
            if step <= last:
                self.held[(step,) + part] = total.astype(BF16)
                self.copy(at, step).start()
            else:
                self.out[part] = total.astype(self.out.dtype)
        if event == self.events - 1:
            for at in range(4):
                for past in range(last + 1):
                    self.copy(at, past).wait_send()


class RingSumSplit:
    @staticmethod
    def scratch(size, rows, columns):
        dma, half = pltpu.SemaphoreType.DMA, size // 2
        slots = pltpu.VMEM((half, rows, columns), BF16)
        return [slots] * 3 + [dma((half,)), dma((half,)), dma((2, half)), dma((2, half))]

    def __init__(self, where, terms, out, scratch):
        self.where, self.terms, self.out = where, terms, out
        self.given, self.held, self.landed, *sems = scratch
        self.send_core, self.recv_core, self.send, self.recv = sems
        self.half = where.size // 2
        self.events = self.half + 1
        rows = out.shape[0]
        cut = -(-rows // 32) * 16
        self.parts = (pl.ds(0, cut), pl.ds(cut, rows - cut))

    def slot(self, step, side):
        return self.where.at_place(self.where.place + side * (self.half - step))

    def give(self, step):
        side = 2 * self.where.core - 1
        return remote(
            self.terms.at[self.slot(step, side)],
            self.given.at[step],
            self.send_core.at[step],
            self.recv_core.at[step],
            self.where.peer(1, 0),
        )

    def copy(self, step, at):
        return remote(
            self.held.at[step, self.parts[at]],
            self.landed.at[step, self.parts[at]],
            self.send.at[at, step],
            self.recv.at[at, step],
            self.where.neighbour(1 - 2 * self.where.core),
        )

    def run(self, step):
        half, core = self.half, self.where.core
        if step == 0:
            for at in range(half):
                self.give(at).start()
        if step < half:
            self.give(step).wait_recv()
            slot = self.slot(step, 1 - 2 * core)
        for at, rows in enumerate(self.parts):
            if step < half:
                total = self.terms[slot, rows].astype(F32) + self.given[step, rows].astype(F32)
                if step == 0:
                    total = total * (1 - core).astype(F32)
            else:
                total = self.terms[self.where.ring, rows].astype(F32)
            if step:
                self.copy(step - 1, at).wait_recv()
                total = total + self.landed[step - 1, rows].astype(F32)
            if step < half:
                self.held[step, rows] = total.astype(BF16)
                self.copy(step, at).start()
            else:
                self.out[rows] = total.astype(self.out.dtype)
        if step == half:
            for past in range(half):
                self.give(past).wait_send()
                for at in range(2):
                    self.copy(past, at).wait_send()


class GroupGather:
    @staticmethod
    def scratch(span, parts=1):
        dma = pltpu.SemaphoreType.DMA
        return [dma((2, span, parts)), dma((2, span, parts)), dma((1,))]

    def __init__(self, where, block, out, sems, parts=1):
        self.where, self.block, self.out, self.parts = where, block, out, parts
        self.send, self.recv, self.own = sems

    def rows(self, part):
        size = self.block.shape[0] // self.parts
        return pl.ds(part * size, size)

    def hop(self, dx, part):
        where, rows = self.where, self.rows(part)
        at = (0, dx, part)
        return remote(
            self.block.at[rows],
            self.out.at[0, dx, rows],
            self.send.at[at],
            self.recv.at[at],
            where.peer(0, where.span - dx),
        )

    def cross(self, dx, part):
        rows = self.rows(part)
        source = self.out.at[0, dx, rows] if dx else self.block.at[rows]
        at = (1, dx, part)
        return remote(
            source,
            self.out.at[1, dx, rows],
            self.send.at[at],
            self.recv.at[at],
            self.where.peer(1, 0),
        )

    def start(self, part):
        for dx in range(1, self.where.span):
            self.hop(dx, part).start()
        self.cross(0, part).start()

    def pass_on(self, part):
        for dx in range(1, self.where.span):
            self.hop(dx, part).wait_recv()
            self.cross(dx, part).start()

    def arrived(self, dx):
        for part in range(self.parts):
            self.cross(dx, part).wait_recv()

    def sent(self):
        for part in range(self.parts):
            for dx in range(self.where.span):
                if dx:
                    self.hop(dx, part).wait_send()
                self.cross(dx, part).wait_send()

    def finish(self):
        for dx in range(self.where.span):
            self.arrived(dx)
        self.sent()

    def keep(self):
        return pltpu.make_async_copy(self.block, self.out.at[0, 0], self.own.at[0])

    def run(self, step):
        if step == 0:
            self.keep().start()
            for part in range(self.parts):
                self.start(part)
        elif step == 1:
            for part in range(self.parts):
                self.pass_on(part)
        else:
            self.finish()
            self.keep().wait()


class GroupSwap:
    @staticmethod
    def scratch(span):
        dma = pltpu.SemaphoreType.DMA
        return [dma((2, span)), dma((2, span)), dma((1,))]

    def __init__(self, where, source, target, sems):
        self.where, self.source, self.target = where, source, target
        self.send, self.recv, self.own = sems

    def run(self, step):
        where = self.where
        keep = pltpu.make_async_copy(self.source(0, 0), self.target(0, 0), self.own.at[0])
        copies = [
            remote(
                self.source(dc, dx),
                self.target(dc, dx),
                self.send.at[dc, dx],
                self.recv.at[dc, dx],
                where.peer(dc, dx),
            )
            for dx in reversed(range(where.span))
            for dc in range(2)
            if dc or dx
        ]
        if step == 0:
            for copy in copies:
                copy.start()
            keep.start()
        else:
            for copy in copies:
                copy.wait()
            keep.wait()


class GroupSum:
    @staticmethod
    def scratch(span, rows, columns):
        dma = pltpu.SemaphoreType.DMA
        slots = pltpu.VMEM((span, rows, columns), BF16)
        return [slots, slots, dma((span,)), dma((span,)), dma((span,)), dma((span,))]

    def __init__(self, where, terms, out, scratch):
        self.where, self.terms, self.out = where, terms, out
        self.crossed, self.landed, *sems = scratch
        self.send_core, self.recv_core, self.send, self.recv = sems

    def cross(self, dx):
        return remote(
            self.terms.at[1, dx],
            self.crossed.at[dx],
            self.send_core.at[dx],
            self.recv_core.at[dx],
            self.where.peer(1, 0),
        )

    def hop(self, dx):
        return remote(
            self.crossed.at[dx],
            self.landed.at[dx],
            self.send.at[dx],
            self.recv.at[dx],
            self.where.peer(0, dx),
        )

    def fold(self, dx):
        self.cross(dx).wait_recv()
        total = self.terms[0, dx].astype(F32) + self.crossed[dx].astype(F32)
        self.crossed[dx] = total.astype(BF16)
        self.hop(dx).start()

    def finish(self):
        self.cross(0).wait_recv()
        total = self.terms[0, 0].astype(F32) + self.crossed[0].astype(F32)
        for dx in range(1, self.where.span):
            self.hop(dx).wait_recv()
            total = total + self.landed[dx].astype(F32)
        self.out[...] = total.astype(self.out.dtype)
        for dx in range(self.where.span):
            self.cross(dx).wait_send()
            if dx:
                self.hop(dx).wait_send()

    def run(self, step):
        later = list(reversed(range(self.where.span)))
        if step == 0:
            for dx in later:
                self.cross(dx).start()
        elif step == 1:
            for dx in later[:-1]:
                self.fold(dx)
        else:
            self.finish()


class CoreSum:
    @staticmethod
    def scratch(span, rows, columns):
        dma = pltpu.SemaphoreType.DMA
        return [pltpu.VMEM((span, rows, columns), BF16), dma((span,)), dma((span,))]

    def __init__(self, where, terms, out, scratch):
        self.where, self.terms, self.out = where, terms, out
        self.crossed, self.send_core, self.recv_core = scratch

    cross = GroupSum.cross

    def fold(self, dx):
        self.cross(dx).wait_recv()
        total = self.terms[0, dx].astype(F32) + self.crossed[dx].astype(F32)
        self.out[dx] = total.astype(BF16)

    def finish(self):
        for dx in range(self.where.span):
            self.cross(dx).wait_send()


class PatchSum:
    @staticmethod
    def scratch(span, rows, columns):
        dma = pltpu.SemaphoreType.DMA
        return [pltpu.VMEM((span, rows, columns), BF16), dma((span,)), dma((span,))]

    def __init__(self, where, terms, out, scratch):
        self.where, self.crossed, self.out = where, terms, out
        self.landed, self.send, self.recv = scratch

    hop = GroupSum.hop

    def run(self, step):
        span = self.where.span
        if step == 0:
            for dx in range(1, span):
                self.hop(dx).start()
        else:
            total = self.crossed[0].astype(F32)
            for dx in range(1, span):
                self.hop(dx).wait_recv()
                total = total + self.landed[dx].astype(F32)
            self.out[...] = total
            for dx in range(1, span):
                self.hop(dx).wait_send()


class AllSum:
    @staticmethod
    def bits(sizes, axes=(2, 0, 1)):
        found = []
        for axis in axes:
            bit = 1
            while bit < sizes[axis]:
                found.append((axis, bit))
                bit *= 2
        return found

    @staticmethod
    def scratch(sizes, shape):
        count = len(AllSum.bits(sizes))
        dma = pltpu.SemaphoreType.DMA
        slots = pltpu.VMEM((count,) + tuple(shape), F32)
        return [slots, slots, dma((count,)), dma((count,))]

    def __init__(self, where, sizes, block, out, scratch, axes=(2, 0, 1)):
        self.block, self.out = block, out
        self.held, self.landed, self.send, self.recv = scratch
        here = (where.ring, where.core, where.patch)
        self.peers = []
        for axis, bit in AllSum.bits(sizes, axes):
            peer = list(here)
            peer[axis] = here[axis] + (1 - 2 * ((here[axis] // bit) % 2)) * bit
            self.peers.append(tuple(peer))
        self.events = len(self.peers) + 1

    def copy(self, step):
        return remote(
            self.held.at[step],
            self.landed.at[step],
            self.send.at[step],
            self.recv.at[step],
            self.peers[step],
        )

    def run(self, step):
        if step == 0:
            total = self.block[...]
        else:
            self.copy(step - 1).wait()
            total = self.held[step - 1] + self.landed[step - 1]
        if step < len(self.peers):
            self.held[step] = total
            self.copy(step).start()
        else:
            self.out[...] = total


HBM = pl.BlockSpec(memory_space=pl.ANY)
CORE = pl.BlockSpec(memory_space=pltpu.VMEM)


def take(refs, counts):
    found, at = [], 0
    for count in counts:
        found.append(list(refs[at : at + count]))
        at += count
    return found


def flat_block(vector):
    rows = -(-vector.shape[0] // 1024) * 8
    return jnp.pad(vector, (0, rows * 128 - vector.shape[0])).reshape(rows, 128)


def join(pieces, wide, block):
    group, share, _ = pieces.shape
    for at in range(group):
        wide[at * share : (at + 1) * share, :] = pieces[at].astype(F32)
    block[...] = wide[...].astype(BF16)


def entry_kernel(sizes, clips, chunk, *refs):
    where = Where(sizes)
    ins, outs, scratch = take(refs, (8, 8, len(refs) - 16))
    tokens, qkv_weight, up_weight, out_rows, silu_part, ada_weight, small, frame_clip = ins
    tokens_all, w_qkv, w_out, up_block, summed, hidden, projected, own_rows = outs
    cols, lands, wide, blocks, (w_qkv_t, vector, spread), *sems = take(
        scratch, (2, 3, 3, 2, 3, 3, 3, 3, 3, 3, 5, 4)
    )
    sums = AllSum(where, sizes, vector, summed, sems[6])
    member, span, group = where.member, where.span, 2 * where.span
    rows, width = tokens.shape
    share = out_rows.shape[0]
    device = where.ring * group + member

    def swap(source, land, job_sems):
        return GroupSwap(where, source, lambda dc, dx: land.at[member], job_sems)

    swap_qkv = swap(lambda dc, dx: cols[0].at[where.peer_member(dc, dx)], lands[0], sems[0])
    swap_up = swap(lambda dc, dx: cols[1].at[where.peer_member(dc, dx)], lands[1], sems[1])
    swap_out = swap(lambda dc, dx: out_rows, lands[2], sems[2])
    gather = GroupGather(where, tokens, tokens_all, sems[3], max(1, rows // 128))
    ring = RingGather(where, blocks[0], w_qkv, sems[4])
    ring_out = RingGatherSplit(where, blocks[1], w_out, sems[5])

    features = qkv_weight.shape[1] // (3 * group)
    wide_rows = qkv_weight[...].astype(F32)
    for at in range(group):
        for part in range(3):
            low = (part * group + at) * features
            cols[0][at, :, part * features : (part + 1) * features] = wide_rows[
                :, low : low + features
            ].astype(BF16)

    units = up_weight.shape[1] // (group * where.size)
    spread[...] = jnp.zeros_like(spread)
    lengths = [share] * 4 + [units, 6 * share]
    low = 0
    for at, length in enumerate(lengths):
        spread[at : at + 1, :length] = small[0:1, low : low + length]
        low += length
    lanes = lax.broadcasted_iota(jnp.int32, (1, width), 1)
    vector[...] = jnp.zeros_like(vector)
    vector[0:4, :] = pltpu.roll(spread[...], device * share, 1)[0:4]
    start = device * units
    moved = pltpu.roll(spread[...], start % width, 1)[4:5]
    for at in range(4):
        vector[4 + at : 5 + at, :] = jnp.where(start // width == at, moved, 0.0)
    start = device * 6 * share
    moved = pltpu.roll(spread[...], start % width, 1)[5:6]
    lies = start // width + jnp.where(lanes < start % width, 1, 0)
    terms = jnp.dot(silu_part[...], ada_weight[...], preferred_element_type=F32)
    for part in range(6):
        bias = jnp.where(lies == part, moved, 0.0)
        for clip in range(clips):
            at = 8 + 6 * clip + part
            vector[at : at + 1, :] = (
                terms[clip : clip + 1, part * width : (part + 1) * width] + bias
            )
    own_clip = frame_clip[0].astype(F32)
    own_frame = 2 * where.ring + where.core
    at = 8 + 6 * clips
    vector[at : at + 1, :] = jnp.where((lanes == own_frame) & (where.patch == 0), own_clip, 0.0)

    greet(where.ring_peers() + where.group_peers() + sums.peers)
    swap_qkv.run(0)
    sums.run(0)
    swap_qkv.run(1)
    join(lands[0], wide[0], blocks[0])
    ring.run(0)
    ring.run(1)
    swap_out.run(0)
    gather.run(0)
    wide_rows = up_weight[...].astype(F32)
    for at in range(group):
        for ring_at in range(where.size):
            low = (ring_at * group + at) * units
            cols[1][at, :, ring_at * units : (ring_at + 1) * units] = wide_rows[
                :, low : low + units
            ].astype(BF16)
    swap_up.run(0)
    ring.run(2)
    sums.run(1)
    ring.run(3)
    swap_out.run(1)
    join(lands[2], wide[2], blocks[1])
    ring_out.run(0)
    ring.run(4)
    turns(ring, 5, [(sums, 2), (ring_out, 1)], 2)
    swap_up.run(1)
    join(lands[1], wide[1], up_block)

    at = 8 + 6 * clips
    other_frame = 2 * where.ring + 1 - where.core
    other_clip = jnp.sum(
        jnp.where(lanes == other_frame, summed[at : at + 1, :], 0.0), axis=1, keepdims=True
    )
    own, other = [0.0] * 6, [0.0] * 2
    for clip in range(clips):
        is_own = jnp.maximum(1.0 - jnp.abs(own_clip - clip), 0.0)
        is_other = jnp.maximum(1.0 - jnp.abs(other_clip - clip), 0.0)
        for part in range(6):
            row = summed[8 + 6 * clip + part : 9 + 6 * clip + part, :]
            own[part] = own[part] + is_own * row
            if part < 2:
                other[part] = other[part] + is_other * row
        own_rows[8 + clip : 9 + clip, :] = jnp.zeros((1, width), F32) + is_own
        own_rows[8 + clips + clip : 9 + clips + clip, :] = jnp.zeros((1, width), F32) + is_other
    for part in range(6):
        own_rows[part : part + 1, :] = own[part]
    own_rows[6:8, :] = summed[2:4, :]

    features = blocks[0].shape[1] // 3
    lead = pltpu.roll(summed[0:8, :], (width - member * features) % width, 1).T
    bias_q, bias_v = lead[:features, 0:1], lead[:features, 1:2]
    w_qkv_t[...] = w_qkv[...].reshape(width, 3 * features).T

    def project(dc, dx, at):
        here = slice(at, at + chunk)
        normed, _ = layer_norm(tokens_all[dc, dx, here, :].astype(F32))
        shift, scale = (other if dc else own)[:2]
        low = (normed * (1.0 + scale) + shift).astype(BF16)
        first = (dc * span + dx) * rows + at
        hidden[first : first + chunk, :] = low
        found = lax.dot_general(
            w_qkv_t[...], low, (((1,), (1,)), ((), ())), preferred_element_type=F32
        )
        there = slice(first, first + chunk)
        projected[:features, there] = (found[:features] + bias_q).astype(BF16)
        projected[features : 2 * features, there] = found[features : 2 * features].astype(BF16)
        projected[2 * features :, there] = (found[2 * features :] + bias_v).astype(BF16)

    gather.keep().wait()
    for dx in range(span):
        if dx == 1:
            gather.run(1)
        for dc in range(2):
            if dc:
                gather.arrived(dx)
            for at in range(0, rows, chunk):
                project(dc, dx, at)
    gather.sent()


def turns(ring, event, others, every):
    count = 0
    others = [list(item) for item in others]
    while event < ring.events or any(at < job.events for job, at in others):
        if event < ring.events:
            ring.run(event)
            event += 1
        count += 1
        if count % every == 0 or event >= ring.events:
            for item in others:
                if item[1] < item[0].events:
                    item[0].run(item[1])
                    item[1] += 1


def entry(
    tokens, qkv_weight, up_weight, out_rows, silu_part, ada_weight, small, clip, sizes, call_id
):
    size, _, span = sizes
    group, share = 2 * span, out_rows.shape[0]
    rows, width = tokens.shape
    clips = silu_part.shape[0]
    block_rows = group * share
    columns = [qkv_weight.shape[1] // group, up_weight.shape[1] // group, width]
    count = 9 + 6 * clips
    vector = (count + -count % 8, width)
    shape = jax.ShapeDtypeStruct
    scratch = [pltpu.VMEM((group, share, n), BF16) for n in columns[:2]]
    scratch += [pltpu.VMEM((group, share, n), BF16) for n in columns]
    scratch += [pltpu.VMEM((block_rows, n), F32) for n in columns]
    scratch += [pltpu.VMEM((block_rows, n), BF16) for n in (columns[0], width)]
    scratch += [pltpu.VMEM((columns[0], width), BF16)]
    scratch += [pltpu.VMEM(vector, F32), pltpu.VMEM((8, width), F32)]
    scratch += GroupSwap.scratch(span) * 3
    scratch += GroupGather.scratch(span, max(1, rows // 128))
    scratch += RingGather.scratch(size)
    scratch += RingGatherSplit.scratch(size)
    scratch += AllSum.scratch(sizes, vector)
    return pl.pallas_call(
        functools.partial(entry_kernel, sizes, clips, min(256, rows)),
        out_shape=[
            shape((2, span, rows, width), BF16),
            shape((size, block_rows, columns[0]), BF16),
            shape((size, block_rows, width), BF16),
            shape((block_rows, columns[1]), BF16),
            shape(vector, F32),
            shape((group * rows, width), BF16),
            shape((columns[0], group * rows), BF16),
            shape((8 + 2 * clips + -2 * clips % 8, width), F32),
        ],
        in_specs=[HBM, CORE, CORE, HBM, CORE, CORE, CORE, pl.BlockSpec(memory_space=pltpu.SMEM)],
        out_specs=[CORE, CORE, HBM, CORE, CORE, CORE, CORE, CORE],
        scratch_shapes=scratch,
        compiler_params=pltpu.CompilerParams(
            collective_id=call_id, has_side_effects=True, vmem_limit_bytes=48 * MIB
        ),
        name="entry",
    )(tokens, qkv_weight, up_weight, out_rows, silu_part, ada_weight, small, clip)


def beside(job, total, places, count, first=0, stride=1):
    at = pl.program_id(0) * pl.num_programs(1) + pl.program_id(1)
    slots, event = {}, 0
    for place in range(first, total * places, stride):
        todo = list(range(event, min(event + count, job.events - 1)))
        if todo:
            slots[place] = todo
            event += len(todo)

    def ahead(place):
        for grid in range(total):
            todo = slots.get(grid * places + place)
            if todo:

                @pl.when(at == grid)
                def _():
                    for event in todo:
                        job.run(event)

    def finish():
        for late in range(event, job.events):
            job.run(late)

    return ahead, finish


def attention_kernel(sizes, factor, chunk, total, *refs):
    where = Where(sizes)
    ins, outs, scratch = take(refs, (5, 4, len(refs) - 9))
    q_ref, k_ref, v_ref, up_block, grad_block = ins
    out_ref, lse_ref, w_up, grad_all = outs
    sems = take(scratch, (3, 3))
    chunks = q_ref.shape[2] // chunk
    places = max(chunks // 2, 1)
    ahead, finish = beside(RingGather(where, up_block, w_up, sems[0]), total, places, 1)
    gather = GroupGather(where, grad_block, grad_all, sems[1], 2)
    at = pl.program_id(0) * pl.num_programs(1) + pl.program_id(1)

    @pl.when(at == 0)
    def _():
        greet(where.ring_peers() + where.group_peers())
        gather.run(0)

    keys = k_ref[0].T
    values_t = v_ref[0]
    for number in range(chunks):
        if number % 2 == 0:
            ahead(number // 2)
        span = slice(number * chunk, (number + 1) * chunk)
        scores = jnp.dot(keys, q_ref[0, :, span], preferred_element_type=F32) * factor
        top = jnp.max(scores, axis=0, keepdims=True)
        probs = jnp.exp2(scores - top)
        row_sum = jnp.sum(probs, axis=0, keepdims=True)
        mixed = jnp.dot(values_t, probs.astype(BF16), preferred_element_type=F32)
        out_ref[0, :, span] = (mixed / row_sum).astype(BF16)
        lse_ref[0, :, span] = top + jnp.log2(row_sum)

    @pl.when(at == total - 1)
    def _():
        gather.run(1)
        finish()
        gather.run(2)


def attention(qkv, up_block, grad_block, patches, sizes, call_id):
    size, _, span = sizes
    triple, dim, tokens = qkv.shape
    heads = triple // 3
    frames = tokens // patches
    block = (1, dim, patches)
    factor = LOG2E / math.sqrt(HEAD_DIM)
    shape = jax.ShapeDtypeStruct
    return pl.pallas_call(
        functools.partial(attention_kernel, sizes, factor, min(256, patches), frames * heads),
        out_shape=[
            shape((heads, dim, tokens), BF16),
            shape((heads, 1, tokens), F32),
            shape((size,) + up_block.shape, BF16),
            shape((2, span) + grad_block.shape, BF16),
        ],
        grid=(frames, heads),
        in_specs=[
            pl.BlockSpec(block, lambda f, h: (h, 0, f)),
            pl.BlockSpec(block, lambda f, h: (heads + h, 0, f)),
            pl.BlockSpec(block, lambda f, h: (2 * heads + h, 0, f)),
            HBM,
            HBM,
        ],
        out_specs=[
            pl.BlockSpec(block, lambda f, h: (h, 0, f)),
            pl.BlockSpec((1, 1, patches), lambda f, h: (h, 0, f)),
            HBM,
            HBM,
        ],
        scratch_shapes=RingGather.scratch(size) + GroupGather.scratch(span, 2),
        compiler_params=pltpu.CompilerParams(
            collective_id=call_id, has_side_effects=True, vmem_limit_bytes=32 * MIB
        ),
        cost_estimate=pl.CostEstimate(
            flops=4 * heads * patches * tokens * 256,
            bytes_accessed=4 * heads * dim * tokens * 2,
            transcendentals=heads * patches * tokens,
        ),
        name="attention",
    )(qkv, qkv, qkv, up_block, grad_block)


def attention_back_kernel(sizes, factor, chunk, total, *refs):
    where = Where(sizes)
    ins, outs, scratch = take(refs, (7, 3, len(refs) - 10))
    q_ref, k_ref, v_ref, g_ref, lse_ref, up_terms, half_terms = ins
    grads_ref, up_sum, half_sum = outs
    dk_sum, dv_sum = scratch[:2]
    own = take(scratch[2:], (4, 3))
    patches = q_ref.shape[2]
    chunks = patches // chunk
    ahead, finish = beside(RingSum(where, up_terms, up_sum, own[0]), total, 1, 2)
    half = PatchSum(where, half_terms, half_sum, own[1])
    at = pl.program_id(0) * pl.num_programs(1) + pl.program_id(1)

    @pl.when(at == 0)
    def _():
        greet(where.ring_peers() + where.group_peers())
        half.run(0)

    keys_t = k_ref[0]
    keys = keys_t.T
    values = v_ref[0].T
    scale = factor / LOG2E
    ahead(0)
    for number in range(chunks):
        span = slice(number * chunk, (number + 1) * chunk)
        queries_t = q_ref[0, :, span]
        grad_t = g_ref[0, :, span]
        scores = jnp.dot(keys, queries_t, preferred_element_type=F32) * factor
        probs = jnp.exp2(scores - lse_ref[0, :, span])
        grad_probs = jnp.dot(values, grad_t, preferred_element_type=F32)
        row_dot = jnp.sum(probs * grad_probs, axis=0, keepdims=True)
        grad_scores = (probs * (grad_probs - row_dot)).astype(BF16)
        probs_low = probs.astype(BF16)
        dq = jnp.dot(keys_t, grad_scores, preferred_element_type=F32)
        grads_ref[0, 0, :, span] = (dq * scale).astype(BF16)
        dims = (((1,), (1,)), ((), ()))
        dk = lax.dot_general(queries_t, grad_scores, dims, preferred_element_type=F32)
        dv = lax.dot_general(grad_t, probs_low, dims, preferred_element_type=F32)
        if number == 0:
            dk_sum[...] = dk
            dv_sum[...] = dv
        else:
            dk_sum[...] += dk
            dv_sum[...] += dv
    grads_ref[1, 0] = (dk_sum[...] * scale).astype(BF16)
    grads_ref[2, 0] = dv_sum[...].astype(BF16)

    @pl.when(at == total - 1)
    def _():
        finish()
        half.run(1)


def attention_back(qkv, grad, lse, up_terms, half_terms, patches, sizes, call_id):
    size, _, span = sizes
    triple, dim, tokens = qkv.shape
    heads = triple // 3
    frames = tokens // patches
    block = (1, dim, patches)
    factor = LOG2E / math.sqrt(HEAD_DIM)
    spec = pl.BlockSpec(block, lambda f, h: (h, 0, f))
    shape = jax.ShapeDtypeStruct
    return pl.pallas_call(
        functools.partial(attention_back_kernel, sizes, factor, min(256, patches), frames * heads),
        out_shape=[
            shape((3, heads, dim, tokens), BF16),
            shape(up_terms.shape[1:], BF16),
            shape(half_terms.shape[1:], F32),
        ],
        grid=(frames, heads),
        in_specs=[
            spec,
            pl.BlockSpec(block, lambda f, h: (heads + h, 0, f)),
            pl.BlockSpec(block, lambda f, h: (2 * heads + h, 0, f)),
            spec,
            pl.BlockSpec((1, 1, patches), lambda f, h: (h, 0, f)),
            CORE,
            CORE,
        ],
        out_specs=[pl.BlockSpec((3,) + block, lambda f, h: (0, h, 0, f)), CORE, CORE],
        scratch_shapes=[pltpu.VMEM((dim, patches), F32)] * 2
        + RingSum.scratch(size, *up_terms.shape[1:])
        + PatchSum.scratch(span, *half_terms.shape[1:]),
        compiler_params=pltpu.CompilerParams(
            collective_id=call_id, has_side_effects=True, vmem_limit_bytes=48 * MIB
        ),
        cost_estimate=pl.CostEstimate(
            flops=10 * heads * patches * tokens * 256,
            bytes_accessed=8 * heads * dim * tokens * 2,
            transcendentals=heads * patches * tokens,
        ),
        name="attention_back",
    )(qkv, qkv, qkv, grad, lse, up_terms, half_terms)


def joined(array):
    group, features, count = array.shape
    if features % 16:
        return array.astype(F32).reshape(group * features, count).astype(BF16)
    return array.reshape(group * features, count)


def middle_kernel(sizes, parts, *refs):
    where = Where(sizes)
    ins, outs, scratch = take(refs, (5, 5, len(refs) - 10))
    heads_t, w_out, tokens, vectors, down_block = ins
    attended, branch, midway, hidden_all, w_down = outs
    (hidden,), *sems = take(scratch, (1, 3, 3, 3))
    greet(where.ring_peers() + where.group_peers())
    rows, width = tokens.shape
    span = where.span

    swap = GroupSwap(
        where,
        lambda dc, dx: heads_t.at[:, pl.ds((dc * span + dx) * rows, rows)],
        lambda dc, dx: attended.at[where.member],
        sems[0],
    )
    ring = RingGather(where, down_block, w_down, sems[1])
    gather = GroupGather(where, hidden, hidden_all, sems[2], parts)
    swap.run(0)
    event = min(7, ring.events - 1)
    for early in range(event):
        ring.run(early)
    swap.run(1)
    size = rows // parts
    full = w_out[...]
    for part in range(parts):
        span_rows = slice(part * size, (part + 1) * size)
        mixed = joined(attended[:, :, span_rows])
        one = lax.dot_general(mixed, full, (((0,), (0,)), ((), ())), preferred_element_type=F32)
        one = one + vectors[6:7, :]
        branch[span_rows, :] = one
        mid = tokens[span_rows, :].astype(F32) + vectors[2:3, :] * one
        midway[span_rows, :] = mid
        normed, _ = layer_norm(mid)
        hidden[span_rows, :] = (normed * (1.0 + vectors[4:5, :]) + vectors[3:4, :]).astype(BF16)
        gather.start(part)
        if event < ring.events:
            ring.run(event)
            event += 1
    gather.keep().start()
    for event in range(event, ring.events):
        ring.run(event)
    for part in range(parts):
        gather.pass_on(part)
    gather.finish()
    gather.keep().wait()


def middle(heads_t, w_out, tokens, vectors, down_block, sizes, call_id):
    size, _, span = sizes
    rows, width = tokens.shape
    parts = rows // 128
    shape = jax.ShapeDtypeStruct
    return pl.pallas_call(
        functools.partial(middle_kernel, sizes, parts),
        out_shape=[
            shape((2 * span, heads_t.shape[0], rows), BF16),
            shape((rows, width), F32),
            shape((rows, width), F32),
            shape((2, span, rows, width), BF16),
            shape((size,) + down_block.shape, BF16),
        ],
        in_specs=[CORE, CORE, CORE, CORE, HBM],
        out_specs=[CORE, CORE, CORE, HBM, HBM],
        scratch_shapes=[pltpu.VMEM((rows, width), BF16)]
        + GroupSwap.scratch(span)
        + RingGather.scratch(size)
        + GroupGather.scratch(span, parts),
        compiler_params=pltpu.CompilerParams(
            collective_id=call_id, has_side_effects=True, vmem_limit_bytes=40 * MIB
        ),
        name="middle",
    )(heads_t, w_out, tokens, vectors, down_block)


def gelu_both(values_in):
    square = values_in * values_in
    inner = 0.7978845608028654 * values_in * (1.0 + 0.044715 * square)
    bent = jnp.tanh(inner)
    outer = 0.5 * (1.0 + bent)
    slope = 0.7978845608028654 * (1.0 + 3.0 * 0.044715 * square)
    return values_in * outer, outer + 0.5 * values_in * (1.0 - bent * bent) * slope


def feed_kernel(sizes, chunk, tile, *refs):
    where = Where(sizes)
    ins, outs, scratch = take(refs, (5, 5, len(refs) - 10))
    hidden, grad, w_up, w_down, bias = ins
    half, grad_hidden, g_up, g_down, g_bias = outs
    act, grad_pre, branch, back = scratch[:4]
    own = take(scratch[4:], (3, 6))
    span = where.span
    rows, width = grad_hidden.shape
    units = bias.shape[1]
    sum_half = CoreSum(where, branch, half, own[0])
    sum_back = GroupSum(where, back, grad_hidden, own[1])
    greet(where.group_peers())
    each = rows // chunk
    across = (((1,), (1,)), ((), ()))

    def body(step, total):
        at = step // each
        dx, dc = span - 1 - at // 2, 1 - at % 2
        inside = pl.ds(pl.multiple_of(step % each * chunk, chunk), chunk)
        first = pl.multiple_of((dc * span + dx) * rows + step % each * chunk, chunk)
        here = pl.ds(first, chunk)
        pre = jnp.dot(hidden[here, :], w_up[...], preferred_element_type=F32) + bias[...]
        value, slope = gelu_both(pre)
        value = value.astype(BF16)
        act[here, :] = value
        grad_act = lax.dot_general(grad[here, :], w_down[...], across, preferred_element_type=F32)
        low = (grad_act * slope).astype(BF16)
        grad_pre[here, :] = low
        back[dc, dx, inside, :] = lax.dot_general(
            low, w_up[...], across, preferred_element_type=F32
        ).astype(BF16)
        branch[dc, dx, inside, :] = jnp.dot(
            value, w_down[...], preferred_element_type=F32
        ).astype(BF16)
        for place in range(2 * span):
            done_dx, done_dc = span - 1 - place // 2, 1 - place % 2

            @pl.when(step == (place + 1) * each - 1)
            def _():
                if done_dc:
                    sum_back.cross(done_dx).start()
                    sum_half.cross(done_dx).start()
                elif done_dx:
                    sum_back.fold(done_dx)
                    sum_half.fold(done_dx)

        return total + jnp.sum(low.astype(F32), axis=0, keepdims=True)

    zero = jnp.zeros((1, units), F32)
    g_bias[...] = lax.fori_loop(0, 2 * span * each, body, zero)
    sum_half.fold(0)
    over = (((0,), (0,)), ((), ()))
    for low in range(0, units, tile):
        cut = slice(low, low + tile)
        g_down[cut, :] = lax.dot_general(
            act[:, cut], grad[...], over, preferred_element_type=F32
        ).astype(BF16)
        g_up[:, cut] = lax.dot_general(
            hidden[...], grad_pre[:, cut], over, preferred_element_type=F32
        ).astype(BF16)
    sum_half.finish()
    sum_back.finish()


def feed(hidden, grad, w_up, w_down, bias, sizes, call_id):
    _, _, span = sizes
    tokens, width = hidden.shape
    units = w_up.shape[1]
    rows = tokens // (2 * span)
    shape = jax.ShapeDtypeStruct
    terms = pltpu.VMEM((2, span, rows, width), BF16)
    return pl.pallas_call(
        functools.partial(feed_kernel, sizes, min(256, rows), 384 if units % 384 == 0 else units),
        out_shape=[
            shape((span, rows, width), BF16),
            shape((rows, width), F32),
            shape((width, units), BF16),
            shape((units, width), BF16),
            shape((1, units), F32),
        ],
        in_specs=[CORE] * 5,
        out_specs=[CORE] * 5,
        scratch_shapes=[pltpu.VMEM((tokens, units), BF16)] * 2
        + [terms] * 2
        + CoreSum.scratch(span, rows, width)
        + GroupSum.scratch(span, rows, width),
        compiler_params=pltpu.CompilerParams(
            collective_id=call_id, has_side_effects=True, vmem_limit_bytes=60 * MIB
        ),
        name="feed",
    )(hidden, grad, w_up, w_down, bias)


def return_kernel(sizes, parts, tile, *refs):
    where = Where(sizes)
    ins, outs, scratch = take(refs, (8, 5, len(refs) - 13))
    grad_hidden, midway, branch, grad_out, w_out, attended, vectors, down_terms = ins
    grad_mid, grad_mix, down_sum, g_out, sums = outs
    (grad_heads, grad_one), *own = take(scratch, (2, 4, 3 * parts))
    greet(where.ring_peers() + where.group_peers())
    rows, width = midway.shape
    span = where.span
    size = rows // parts
    features = grad_heads.shape[1]
    ring = RingSum(where, down_terms, down_sum, own[0])
    swaps = []
    for part in range(parts):
        cut = pl.ds(part * size, size)

        def source(dc, dx, cut=cut):
            return grad_heads.at[where.peer_member(dc, dx), :, cut]

        def target(dc, dx, part=part):
            block = dc * span + (span - dx) % span
            return grad_mix.at[:, pl.ds(block * rows + part * size, size)]

        swaps.append(GroupSwap(where, source, target, own[1][3 * part : 3 * part + 3]))
    ring.run(0)
    ring.run(1)
    full = w_out[...]
    totals = [jnp.zeros((1, width), F32)] * 4
    event = 2
    for part in range(parts):
        here = slice(part * size, (part + 1) * size)
        normed, inv_std = layer_norm(midway[here, :])
        grad = grad_hidden[here, :]
        mid = grad_out[here, :].astype(F32) + norm_back(
            grad * (1.0 + vectors[4:5, :]), normed, inv_std
        )
        grad_mid[here, :] = mid
        low = (vectors[2:3, :] * mid).astype(BF16)
        grad_one[here, :] = low
        heads_t = lax.dot_general(full, low, (((1,), (1,)), ((), ())), preferred_element_type=F32)
        grad_heads[:, :, here] = heads_t.reshape(2 * span, features, size).astype(BF16)
        swaps[part].run(0)
        found = [grad, grad * normed, mid * branch[here, :], low.astype(F32)]
        totals = [
            total + jnp.sum(item, axis=0, keepdims=True) for total, item in zip(totals, found)
        ]
        ring.run(event)
        event += 1
    for at, total in enumerate(totals):
        sums[at : at + 1, :] = total
    sums[4:8, :] = jnp.zeros((4, width), F32)
    for low in range(0, width, tile):
        cut = slice(low, low + tile)
        g_out[cut, :] = jnp.dot(
            attended[cut, :], grad_one[...], preferred_element_type=F32
        ).astype(BF16)
        if event < ring.events:
            ring.run(event)
            event += 1
    for event in range(event, ring.events):
        ring.run(event)
    for swap in swaps:
        swap.run(1)


def back_to_heads(
    grad_hidden, midway, branch, grad_out, w_out, attended, vectors, down_terms, sizes, call_id
):
    size, _, span = sizes
    rows, width = midway.shape
    group = 2 * span
    parts = rows // 128
    features = width // group
    shape = jax.ShapeDtypeStruct
    return pl.pallas_call(
        functools.partial(return_kernel, sizes, parts, 384),
        out_shape=[
            shape((rows, width), F32),
            shape((features, group * rows), BF16),
            shape(down_terms.shape[1:], F32),
            shape((width, width), BF16),
            shape((8, width), F32),
        ],
        in_specs=[CORE] * 8,
        out_specs=[CORE] * 5,
        scratch_shapes=[
            pltpu.VMEM((group, features, rows), BF16),
            pltpu.VMEM((rows, width), BF16),
        ]
        + RingSum.scratch(size, *down_terms.shape[1:])
        + GroupSwap.scratch(span) * parts,
        compiler_params=pltpu.CompilerParams(
            collective_id=call_id, has_side_effects=True, vmem_limit_bytes=48 * MIB
        ),
        name="back_to_heads",
    )(grad_hidden, midway, branch, grad_out, w_out, attended, vectors, down_terms)


def last_kernel(sizes, chunk, tile, clips, *refs):
    where = Where(sizes)
    ins, outs, scratch = take(refs, (7, 5, len(refs) - 12))
    grad_qkv, hidden, tokens, w_qkv, out_terms, early, chosen = ins
    grad_hidden, qkv_sum, out_sum, early_sum, late_sum = outs
    (back, g_qkv, late), *own = take(scratch, (3, 6, 4, 7, 4, 4))
    span = where.span
    rows, width = grad_hidden.shape
    sum_back = GroupSum(where, back, grad_hidden, own[0])
    ring = RingSum(where, g_qkv, qkv_sum, own[1])
    ring_out = RingSumSplit(where, out_terms, out_sum, own[2])
    first_sums = AllSum(where, sizes, early, early_sum, own[3])
    sums = AllSum(where, sizes, late, late_sum, own[4], (0, 1, 2))
    greet(where.ring_peers() + where.group_peers() + sums.peers)
    ring_out.run(0)
    first_sums.run(0)
    each = rows // chunk
    blocks = 2 * span
    far = 2 * (span - 1) * each
    planned = dict(zip(range(far, blocks * each), [(ring, at) for at in (2, 3, 4, 5)]))

    def body(step, totals):
        at = step // each
        dx, dc = span - 1 - at // 2, 1 - at % 2
        inside = pl.ds(pl.multiple_of(step % each * chunk, chunk), chunk)
        first = pl.multiple_of((dc * span + dx) * rows + step % each * chunk, chunk)
        here = pl.ds(first, chunk)
        term = lax.dot_general(
            grad_qkv[:, here], w_qkv[...], (((0,), (1,)), ((), ())), preferred_element_type=F32
        )
        back[dc, dx, inside, :] = term.astype(BF16)
        normed, _ = layer_norm(tokens[here, :].astype(F32))
        shift = jnp.sum(term, axis=0, keepdims=True)
        scale = jnp.sum(term * normed, axis=0, keepdims=True)
        other = dc.astype(F32)
        for place in range(blocks):
            done_dx, done_dc = span - 1 - place // 2, 1 - place % 2

            @pl.when(step == (place + 1) * each - 1)
            def _():
                if done_dc:
                    sum_back.cross(done_dx).start()
                elif done_dx:
                    sum_back.fold(done_dx)

        for when, (job, event) in planned.items():
            pl.when(step == when)(functools.partial(job.run, event))
        own_part, other_part = 1.0 - other, other
        return (
            totals[0] + own_part * shift,
            totals[1] + own_part * scale,
            totals[2] + other_part * shift,
            totals[3] + other_part * scale,
        )

    zero = jnp.zeros((1, width), F32)
    totals = lax.fori_loop(0, far, body, (zero,) * 4)
    event = 1
    for low in range(0, width, tile):
        ring_out.run(event)
        first_sums.run(event)
        event += 1
        cut = slice(low, low + tile)
        g_qkv[cut, :] = lax.dot_general(
            hidden[:, cut], grad_qkv[...], (((0,), (1,)), ((), ())), preferred_element_type=F32
        ).astype(BF16)
    ring.run(0)
    ring.run(1)
    totals = lax.fori_loop(far, blocks * each, body, totals)
    late[...] = jnp.zeros_like(late)
    for clip in range(clips):
        for part in range(2):
            at = 2 * clip + part
            late[at : at + 1, :] = (
                chosen[clip : clip + 1, :] * totals[part]
                + chosen[clips + clip : clips + clip + 1, :] * totals[2 + part]
            )
    sums.run(0)
    todo = [(ring_out, at) for at in range(event, ring_out.events)]
    todo += [(first_sums, at) for at in range(event, first_sums.events)]
    late_todo = list(range(1, sums.events - 1))
    for event in range(2 + len(planned), ring.events):
        ring.run(event)
        if todo:
            job, at = todo.pop(0)
            job.run(at)
        if event % 2 and late_todo:
            sums.run(late_todo.pop(0))
    for job, at in todo:
        job.run(at)
    for at in late_todo:
        sums.run(at)
    sum_back.finish()
    sums.run(sums.events - 1)


def back_to_tokens(
    grad_qkv, hidden, tokens, w_qkv, out_terms, early, chosen, clips, sizes, call_id
):
    size, _, span = sizes
    count, width = tokens.shape
    rows = count // (2 * span)
    features = grad_qkv.shape[0]
    block_rows = width // size
    late = (2 * clips + -2 * clips % 8, width)
    shape = jax.ShapeDtypeStruct
    return pl.pallas_call(
        functools.partial(last_kernel, sizes, min(256, rows), 384, clips),
        out_shape=[
            shape((rows, width), F32),
            shape((block_rows, features), BF16),
            shape((block_rows, width), BF16),
            shape(early.shape, F32),
            shape(late, F32),
        ],
        in_specs=[CORE] * 7,
        out_specs=[CORE] * 5,
        scratch_shapes=[
            pltpu.VMEM((2, span, rows, width), BF16),
            pltpu.VMEM((width, features), BF16),
            pltpu.VMEM(late, F32),
        ]
        + GroupSum.scratch(span, rows, width)
        + RingSum.scratch(size, block_rows, features)
        + RingSumSplit.scratch(size, block_rows, width)
        + AllSum.scratch(sizes, early.shape)
        + AllSum.scratch(sizes, late),
        compiler_params=pltpu.CompilerParams(
            collective_id=call_id, has_side_effects=True, vmem_limit_bytes=60 * MIB
        ),
        name="back_to_tokens",
    )(grad_qkv, hidden, tokens, w_qkv, out_terms, early, chosen)


def final_kernel(sizes, *refs):
    where = Where(sizes)
    ins, outs, scratch = take(refs, (4, 4, len(refs) - 8))
    summed, share_qkv, share_up, share_out = outs
    got, own = scratch[:3], take(scratch[3:], (4, 3, 3, 3))
    sums = AllSum(where, sizes, ins[0], summed, own[0])
    greet(where.group_peers() + sums.peers)
    swaps = [
        GroupSwap(
            where,
            lambda dc, dx, source=ins[at + 1]: source.at[where.peer_member(dc, dx)],
            lambda dc, dx, target=got[at]: target.at[where.member],
            own[at + 1],
        )
        for at in range(3)
    ]
    sums.run(0)
    for swap in swaps:
        swap.run(0)
    for event in range(1, sums.events):
        sums.run(event)
    group, _, three = got[0].shape
    features = three // 3
    swaps[0].run(1)
    for member in range(group):
        piece = got[0][member].astype(F32)
        for part in range(3):
            low = (part * group + member) * features
            share_qkv[:, low : low + features] = piece[:, part * features : (part + 1) * features]
    swaps[1].run(1)
    units = got[1].shape[2] // where.size
    for member in range(group):
        piece = got[1][member].astype(F32)
        for ring in range(where.size):
            low = (ring * group + member) * units
            share_up[:, low : low + units] = piece[:, ring * units : (ring + 1) * units]
    swaps[2].run(1)
    total = got[2][0].astype(F32)
    for member in range(1, group):
        total = total + got[2][member].astype(F32)
    share_out[...] = total


def final(block, pieces, sizes, call_id):
    group, share, _ = pieces[0].shape
    shape = jax.ShapeDtypeStruct
    return pl.pallas_call(
        functools.partial(final_kernel, sizes),
        out_shape=[
            shape(block.shape, F32),
            shape((share, group * pieces[0].shape[2]), F32),
            shape((share, group * pieces[1].shape[2]), F32),
            shape((share, pieces[2].shape[2]), F32),
        ],
        in_specs=[CORE] * 4,
        out_specs=[CORE] * 4,
        scratch_shapes=[pltpu.VMEM(item.shape, BF16) for item in pieces]
        + AllSum.scratch(sizes, block.shape)
        + GroupSwap.scratch(sizes[2]) * 3,
        compiler_params=pltpu.CompilerParams(
            collective_id=call_id, has_side_effects=True, vmem_limit_bytes=32 * MIB
        ),
        name="final",
    )(block, *pieces)


def per_device(
    tokens,
    cotangent,
    clip_embed,
    timesteps,
    frame_clip,
    ada_weight,
    ada_bias,
    qkv_weight,
    query_bias,
    value_bias,
    out_weight,
    out_bias,
    up_weight,
    up_bias,
    down_weight,
    down_bias,
):
    ring_size, patch_size = lax.axis_size("ring"), lax.axis_size("patch")
    sizes = (ring_size, 2, patch_size)
    group = 2 * patch_size
    device_count = ring_size * group
    ring, core, patch = (lax.axis_index(name) for name in ("ring", "core", "patch"))
    member = core * patch_size + patch
    device = ring * group + member
    rows, width = tokens.shape[1:]
    tokens, cotangent = tokens[0], cotangent[0]
    patches = patch_size * rows
    clips = clip_embed.shape[0]
    hidden = up_weight.shape[1]
    share = width // device_count
    heads = HEADS // group
    head_width = heads * HEAD_DIM
    units = hidden // group
    mine = jnp.arange(group) == member
    mine_of_all = jnp.arange(device_count) == device

    condition = clip_embed + sinusoid(timesteps, width)
    silu_cond, silu_back = jax.vjp(jax.nn.silu, condition)
    silu_low = silu_cond.astype(BF16)
    silu_part = lax.dynamic_slice_in_dim(silu_low, device * share, share, 1)
    small = jnp.concatenate(
        [query_bias, value_bias, out_bias, down_bias, up_bias, ada_bias]
    ).astype(F32)[None, :]

    tokens_all, w_qkv, w_out, up_block, summed, hidden_one, projected, own_rows = entry(
        tokens,
        qkv_weight,
        up_weight,
        out_weight,
        silu_part,
        ada_weight,
        small,
        frame_clip,
        sizes,
        1,
    )
    w_qkv = w_qkv.reshape(width, 3 * head_width)
    w_out = w_out.reshape(width, width)
    scale_one, gate_one, scale_two, gate_two, b_down = (own_rows[at] for at in (1, 2, 4, 5, 7))
    b_up = lax.dynamic_index_in_dim(
        summed[4 : 4 + hidden // width].reshape(ring_size, group, hidden // device_count),
        member,
        1,
        False,
    ).reshape(units)

    qkv = projected.reshape(3 * heads, HEAD_DIM, 2 * patches)
    grad_out = cotangent.astype(F32)
    grad_branch_two = (gate_two * grad_out).astype(BF16)
    attended_t, lse, w_up, gb_two_all = attention(
        qkv, up_block, grad_branch_two, patches, sizes, 2
    )
    w_up = w_up.reshape(width, units)

    attended, branch_one, midway, hidden_two_all, w_down = middle(
        attended_t.reshape(head_width, 2 * patches),
        w_out,
        tokens,
        own_rows,
        down_weight,
        sizes,
        3,
    )
    attended = attended.reshape(width, rows)
    w_down = w_down.reshape(units, width)

    branch_half, grad_hidden_two, g_up, g_down, g_up_b = feed(
        hidden_two_all.reshape(2 * patches, width),
        gb_two_all.reshape(2 * patches, width),
        w_up,
        w_down,
        b_up[None, :],
        sizes,
        4,
    )
    g_up_b = g_up_b[0]
    g_down_b = jnp.sum(grad_branch_two.astype(F32), axis=0)
    block_rows = width // ring_size
    grad_midway, grad_mix, share_down, g_out, own_sums = back_to_heads(
        grad_hidden_two,
        midway,
        branch_one,
        cotangent,
        w_out,
        attended,
        own_rows,
        g_down.reshape(ring_size, units // ring_size, width),
        sizes,
        5,
    )
    grad_shift_two, grad_scale_two, grad_gate_one, g_out_b = (own_sums[at] for at in range(4))

    grad_projected, sum_up, branch_two = attention_back(
        qkv,
        grad_mix.reshape(heads, HEAD_DIM, 2 * patches),
        lse,
        g_up.reshape(ring_size, block_rows, units),
        branch_half,
        patches,
        sizes,
        6,
    )
    grad_projected = grad_projected.reshape(3 * head_width, 2 * patches)
    branch_two = branch_two + b_down
    output = (midway + gate_two * branch_two).astype(BF16)
    grad_gate_two = jnp.sum(grad_out * branch_two, axis=0)
    g_query_b = jnp.sum(grad_projected[:head_width].astype(F32), axis=1)
    g_value_b = jnp.sum(grad_projected[2 * head_width :].astype(F32), axis=1)

    frame_grads = jnp.stack([grad_gate_one, grad_shift_two, grad_scale_two, grad_gate_two])
    early = jnp.concatenate(
        [
            (own_rows[8 : 8 + clips, None] * frame_grads[None]).reshape(4 * clips, width),
            jnp.where(mine[:, None], g_query_b[None, :], 0.0).reshape(1, width),
            jnp.where(mine[:, None], g_value_b[None, :], 0.0).reshape(1, width),
            jnp.stack([g_out_b, g_down_b]),
            jnp.where(mine[None, :, None], g_up_b.reshape(ring_size, 1, -1), 0.0).reshape(
                -1, width
            ),
        ]
    )
    early = jnp.pad(early, ((0, -early.shape[0] % 8), (0, 0)))
    grad_hidden_one, sum_qkv, sum_out, early_sum, late_sum = back_to_tokens(
        grad_projected,
        hidden_one,
        tokens_all.reshape(2 * patches, width),
        w_qkv,
        g_out.reshape(ring_size, block_rows, width),
        early,
        own_rows[8:],
        clips,
        sizes,
        7,
    )
    first = late_sum[: 2 * clips].reshape(clips, 2 * width)
    second = early_sum[: 4 * clips].reshape(clips, 4 * width)
    mod_low = jnp.concatenate([first, second], axis=1).astype(BF16)
    query_b_all, value_b_all, out_b_all, down_b_all = (early_sum[4 * clips + at] for at in range(4))
    up_b_all = early_sum[4 * clips + 4 :].reshape(-1)[:hidden]

    def own(vector):
        length = vector.shape[0] // device_count
        return lax.dynamic_slice_in_dim(vector, device * length, length, 0)

    ada_bias_grad = own(jnp.sum(mod_low.astype(F32), axis=0))
    ada_weight_grad = lax.dot_general(
        silu_part, mod_low, (((0,), (0,)), ((), ())), preferred_element_type=F32
    )
    grad_silu_part = lax.dot_general(
        mod_low, ada_weight, (((1,), (1,)), ((), ())), preferred_element_type=F32
    )
    spread = jnp.where(mine_of_all[None, :, None], grad_silu_part[:, None, :], 0.0).reshape(-1)
    grad_silu, share_qkv, share_up, share_out = final(
        flat_block(spread),
        [item.reshape(group, share, -1) for item in (sum_qkv, sum_up, sum_out)],
        sizes,
        8,
    )
    grad_silu = grad_silu.reshape(-1)[: clips * width].reshape(clips, width)
    clip_grad = silu_back(grad_silu)[0]

    input_rows = tokens.astype(F32)
    normed_one, inv_one = layer_norm(input_rows)
    tokens_grad = (
        grad_midway + norm_back(grad_hidden_one * (1.0 + scale_one), normed_one, inv_one)
    ).astype(BF16)

    return (
        output[None],
        tokens_grad[None],
        clip_grad,
        ada_weight_grad,
        ada_bias_grad,
        share_qkv,
        own(query_b_all),
        own(value_b_all),
        share_out,
        own(out_b_all),
        share_up,
        own(up_b_all),
        share_down,
        own(down_b_all),
    )


def solution(mesh):
    frames, patch = mesh.shape["frames"], mesh.shape["patch"]
    inner = Mesh(mesh.devices.reshape(frames // 2, 2, patch), ("ring", "core", "patch"))
    every = ("ring", "core", "patch")
    tokens = P(("ring", "core"), "patch", None)
    matrix = P(every, None)
    vector = P(every)
    return jax.shard_map(
        per_device,
        mesh=inner,
        in_specs=(
            tokens,
            tokens,
            P(),
            P(),
            P(("ring", "core")),
            matrix,
            vector,
            matrix,
            vector,
            vector,
            matrix,
            vector,
            matrix,
            vector,
            matrix,
            vector,
        ),
        out_specs=(
            tokens,
            tokens,
            P(),
            matrix,
            vector,
            matrix,
            vector,
            vector,
            matrix,
            vector,
            matrix,
            vector,
            matrix,
            vector,
        ),
        check_vma=False,
    )
```

time: 541 us -> 443 us (0.82)
  Pallas kernels: 402 us -> 375 us
  matrix products: 27.8 us -> 2.33 us
  other arithmetic: 34.7 us -> 15.1 us
  local copies, waits for them, and re-layouts: 58.2 us -> 40 us
  waiting for transfers between devices: 6.14 us -> 0 us
    dot_general x6 -> x0, matrix products: 26.2 us -> none  [the longest x1 7.37 us: per_device(): lax.dot_general(grad_projected, w_qkv, (((0,), (1,)), ((), ())), preferre...]
    pallas_call x5 -> x4, Pallas kernels: 209 us -> 191 us  [the longest x1 71.8 us: entry(): pl.pallas_call(functools.partial(entry_kernel, sizes, clips, min(256, row...]
    reduce_sum x6 -> x1, other arithmetic: 11.5 us -> 0.78 us  [norm_back(): mean_grad = jnp.mean(grad_normed, axis=-1, keepdims=True)]
    reshape x18 -> x7, local copies, waits for them, and re-layouts: 12 us -> 3.61 us  [the longest x3 2.11 us: per_device(): item.reshape(group, share, -1)]
    unnamed x161 -> x85, local copies, waits for them, and re-layouts: 28.9 us -> 22.5 us
    ppermute x8 -> x0, waiting for transfers between devices: 6.14 us -> none  [the longest x4 6.13 us: from_patch(): lax.ppermute(array, 'patch', [((to + hops) % size, to) for to in range(si...]
  transfers between devices with their start and end apart: 8 -> 0, of which waited for: 2 -> 0; matrix products, arithmetic and copies ran while one was open for 4% -> 0% of each run, Pallas kernels for 7% -> 0%
where the time goes in v3:
time: 443 us; the launch traced here: 435 us
  Pallas kernels  375 us (85%)
  local copies, waits for them, and re-layouts  40 us (9%)
  other arithmetic  15.1 us (3%)
    pallas_call x1, Pallas kernels, entry(): pl.pallas_call(functools.partial(entry_kernel, sizes, clips, min(256, row...  71.8 us
    pallas_call x1, Pallas kernels, back_to_tokens(): pl.pallas_call(functools.partial(last_kernel, sizes, min(256, rows), 384,...  63.4 us
    pallas_call x1, Pallas kernels, feed(): pl.pallas_call(functools.partial(feed_kernel, sizes, min(256, rows), 384...  55.9 us
    pallas_call x1, Pallas kernels, middle(): pl.pallas_call(functools.partial(middle_kernel, sizes, parts), out_shape=...  46.7 us
    pallas_call x1, Pallas kernels, attention_back(): pl.pallas_call(functools.partial(attention_back_kernel, sizes, factor, mi...  44 us
    pallas_call x1, Pallas kernels, back_to_heads(): pl.pallas_call(functools.partial(return_kernel, sizes, parts, 384), out_s...  40.3 us
    pallas_call x1, Pallas kernels, attention(): pl.pallas_call(functools.partial(attention_kernel, sizes, factor, min(256...  37.8 us
    unnamed x85, local copies, waits for them, and re-layouts  22.5 us

profile of v3, /device:TPU:0, one launch (start us, length us, event | category | flops | bytes accessed | tf_op | source)
XLA Modules:
  0.0 434.5 jit_solution(5775725607363065066)
XLA Ops:
  10.9 71.8 %entry.1 = (bf16[2,2,512,1152]{3,2,1,0:T(8,128)(2,1)}, bf16[8,144,864]{2,1,0:T(8,128)(2,1)S(1)}, bf16[8,144,1152]{2,1,0:T(8,128)(2,1)}, bf16[144,1152]{1,0:T(8,1...) custom-call(bf16[512,1152]{1,0:T(8,128)(2,1)S(1)} %bitcast.47, ...), custom_call_target="tpu_custom_call" | custom-call | tf_op jit(solution)/shard_map/entry/pallas_call | solution.py:814
  84.3 2.0 copy-done.26
  86.4 37.8 %attention.1 = (bf16[4,72,2048]{2,1,0:T(8,128)(2,1)S(1)}, f32[4,1,2048]{2,1,0:T(1,128)S(1)}, bf16[8,144,1152]{2,1,0:T(8,128)(2,1)S(1)}, bf16[2,2,512,1152]{3,2,1,0:T(8,128)(2,1)S(1)}) custom-call(bf16[12,72,2048]{2,1,0:T(8,128)(2,1)S(1)} %bitcast.62, bf16[12,72,2048]{2,1,0:T(8,128)(2,1)S(1)} %bitcast.63, bf16[12,72,2048]{2,1,0:T(8,128)(2,1)S(1)} %bitcast.64, ...), custom_call_target="tpu_custom_call" | custom-call | flops 8589934592 | bytes 4718592 | tf_op jit(solution)/shard_map/attention/pallas_call | solution.py:908
  124.2 2.1 copy-done.5
  126.3 1.5 copy-done.6
  127.8 46.7 %middle.1 = (bf16[4,288,512]{2,1,0:T(8,128)(2,1)S(1)}, f32[512,1152]{1,0:T(8,128)S(1)}, f32[512,1152]{1,0:T(8,128)S(1)}, bf16[2,2,512,1152]{3,2,1,0:T(8,128)(2,1)}, bf16[8,144,1152]{2,1,0:T(8,128)(2,1)S(1)}) custom-call(bf16[288,2048]{1,0:T(8,128)(2,1)S(1)} %bitcast.57, bf16[1152,1152]{1,0:T(8,128)(2,1)S(1)} %bitcast.50, bf16[512,1152]{1,0:T(8,128)(2,1)S(1)} %bitcast.48, ...), custom_call_target="tpu_custom_call" | custom-call | tf_op jit(solution)/shard_map/middle/pallas_call | solution.py:1098
  174.5 1.4 copy-done.4
  175.9 1.5 copy-done.7
  177.4 1.4 copy-done.8
  179.4 1.4 reshape.310
  180.9 1.4 dynamic-slice_reduce_fusion
  182.3 1.4 broadcast_in_dim_reshape.3.refs_4_
  183.6 55.9 %feed.1 = (bf16[2,512,1152]{2,1,0:T(8,128)(2,1)}, f32[512,1152]{1,0:T(8,128)}, bf16[1152,1152]{1,0:T(8,128)(2,1)}, bf16[1152,1152]{1,0:T(8,128)(2,1)}, f32[1,1152]{1,0:T(1,128)}) custom-call(bf16[2048,1152]{1,0:T(8,128)(2,1)} %bitcast.68, bf16[2048,1152]{1,0:T(8,128)(2,1)} %bitcast.52, bf16[1152,1152]{1,0:T(8,128)(2,1)} %bitcast.53, ...), custom_call_target="tpu_custom_call" | custom-call | tf_op jit(solution)/shard_map/feed/pallas_call | solution.py:1201
  239.6 40.3 %back_to_heads.1 = (f32[512,1152]{1,0:T(8,128)}, bf16[288,2048]{1,0:T(8,128)(2,1)S(1)}, f32[144,1152]{1,0:T(8,128)S(1)}, bf16[1152,1152]{1,0:T(8,128)(2,1)}, f32[8,1152]{1,0:T(8,128)S(1)}) custom-call(f32[512,1152]{1,0:T(8,128)} %get-tuple-element.64.refs_0_, f32[512,1152]{1,0:T(8,128)} %copy-done.4, f32[512,1152]{1,0:T(8,128)} %copy-done.8, ...), custom_call_target="tpu_custom_call" | custom-call | tf_op jit(solution)/shard_map/back_to_heads/pallas_call | solution.py:1297
  280.8 44.0 %attention_back.1 = (bf16[3,4,72,2048]{3,2,1,0:T(8,128)(2,1)}, bf16[144,1152]{1,0:T(8,128)(2,1)S(1)}, f32[512,1152]{1,0:T(8,128)S(1)}) custom-call(bf16[12,72,2048]{2,1,0:T(8,128)(2,1)} %bitcast.59, bf16[12,72,2048]{2,1,0:T(8,128)(2,1)} %bitcast.60, bf16[12,72,2048]{2,1,0:T(8,128)(2,1)} %bitcast.61, bf16[4,72,2048]{2,1,0:T(8,128)(2,1)S(1)} %bitcast.65, ...), custom_call_target="tpu_custom_call" | custom-call | flops 21474836480 | bytes 9437184 | tf_op jit(solution)/shard_map/attention_back/pallas_call | solution.py:1005
  324.7 1.4 copy-done.9
  326.2 2.1 convert_reduce_fusion.2
  328.7 3.9 fusion.11
  333.1 1.3 concatenate.40.refs_5_
  335.0 63.4 %back_to_tokens.1 = (f32[512,1152]{1,0:T(8,128)}, bf16[144,864]{1,0:T(8,128)(2,1)}, bf16[144,1152]{1,0:T(8,128)(2,1)}, f32[16,1152]{1,0:T(8,128)}, f32[8,1152]{1,0:T(8,128)}) custom-call(bf16[864,2048]{1,0:T(8,128)(2,1)} %bitcast.66, bf16[2048,1152]{1,0:T(8,128)(2,1)} %get-tuple-element.75.refs_1_, bf16[2048,1152]{1,0:T(8,128)(2,1)} %bitcast.67, ...), custom_call_target="tpu_custom_call" | custom-call | tf_op jit(solution)/shard_map/back_to_tokens/pallas_call | solution.py:1427
  404.8 15.0 %final.1 = (f32[24,128]{1,0:T(8,128)S(1)}, f32[36,3456]{1,0:T(8,128)S(1)}, f32[36,4608]{1,0:T(8,128)S(1)}, f32[36,1152]{1,0:T(8,128)S(1)}) custom-call(f32[24,128]{1,0:T(8,128)S(1)} %pad_bitcast_fusion.refs_0_, bf16[4,36,864]{2,1,0:T(8,128)(2,1)S(1)} %reshape.322.refs_1_, bf16[4,36,1152]{2,1,0:T(8,128)(2,1)S(1)} %reshape.323.refs_2_, ...), custom_call_target="tpu_custom_call" | custom-call | tf_op jit(solution)/shard_map/final/pallas_call | solution.py:1501
  420.6 1.3 fusion.15
  421.9 2.1 fusion.26
  427.5 1.9 fusion.13
  (137 shorter events, 29.3 us)
Async XLA Ops:
  10.9 72.5 %copy-start.3 = (bf16[1,512,1152]{2,1,0:T(8,128)(2,1)S(1)}, bf16[1,512,1152]{2,1,0:T(8,128)(2,1)}, u32[]{:S(2)}) copy-start(bf16[1,512,1152]{2,1,0:T(8,128)(2,1)} %param.17) | copy-start | bytes 3538948
  82.7 41.5 %copy-start.10 = (bf16[8,144,864]{2,1,0:T(8,128)(2,1)}, bf16[8,144,864]{2,1,0:T(8,128)(2,1)S(1)}, u32[]{:S(2)}) copy-start(bf16[8,144,864]{2,1,0:T(8,128)(2,1)S(1)} %get-tuple-element.77) | copy-start | bytes 5971972
  82.7 45.1 %copy-start.13 = (f32[16,1152]{1,0:T(8,128)}, f32[16,1152]{1,0:T(8,128)S(1)}, u32[]{:S(2)}) copy-start(f32[16,1152]{1,0:T(8,128)S(1)} %get-tuple-element.55.refs_3_.refs_6_) | copy-start | bytes 221188
  84.3 2.0 copy-start.26
  86.3 41.4 %copy-start.1 = (bf16[1,512,1152]{2,1,0:T(8,128)(2,1)S(1)}, bf16[1,512,1152]{2,1,0:T(8,128)(2,1)}, u32[]{:S(2)}) copy-start(bf16[1,512,1152]{2,1,0:T(8,128)(2,1)} %param.16) | copy-start | bytes 3538948
  86.3 41.4 %copy-start.2 = (bf16[8,144,1152]{2,1,0:T(8,128)(2,1)S(1)}, bf16[8,144,1152]{2,1,0:T(8,128)(2,1)}, u32[]{:S(2)}) copy-start(bf16[8,144,1152]{2,1,0:T(8,128)(2,1)} %get-tuple-element.57) | copy-start | bytes 7962628
  86.3 41.4 %copy-start.19 = (bf16[144,1152]{1,0:T(8,128)(2,1)S(1)}, bf16[144,1152]{1,0:T(8,128)(2,1)}, u32[]{:S(2)}) copy-start(bf16[144,1152]{1,0:T(8,128)(2,1)} %refs_4_.1) | copy-start | bytes 995332
  124.2 2.1 copy-start.5
  127.8 46.7 %copy-start.27 = (f32[4,1,2048]{2,1,0:T(1,128)}, f32[4,1,2048]{2,1,0:T(1,128)S(1)}, u32[]{:S(2)}) copy-start(f32[4,1,2048]{2,1,0:T(1,128)S(1)} %get-tuple-element.69.refs_4_) | copy-start | bytes 98308
  183.6 55.9 %copy-start.14 = (f32[16,1152]{1,0:T(8,128)S(1)}, f32[16,1152]{1,0:T(8,128)}, u32[]{:S(2)}) copy-start(f32[16,1152]{1,0:T(8,128)} %copy-done.13) | copy-start | bytes 221188
  239.5 41.2 %copy-start.28 = (f32[4,1,2048]{2,1,0:T(1,128)S(1)}, f32[4,1,2048]{2,1,0:T(1,128)}, u32[]{:S(2)}) copy-start(f32[4,1,2048]{2,1,0:T(1,128)} %copy-done.27) | copy-start | bytes 98308
  280.8 44.0 %copy-start.24 = (f32[8,1152]{1,0:T(8,128)}, f32[8,1152]{1,0:T(8,128)S(1)}, u32[]{:S(2)}) copy-start(f32[8,1152]{1,0:T(8,128)S(1)} %get-tuple-element.79) | copy-start | bytes 110596
  326.2 2.5 copy-start.33
  326.2 2.5 copy-start.38
  328.7 4.0 copy-start.25
  328.7 4.0 copy-start.15
  328.7 4.1 copy-start.39
  328.7 4.4 %copy-start.37 = (f32[1152]{0:T(1024)S(1)}, f32[1152]{0:T(1024)}, u32[]{:S(2)}) copy-start(f32[1152]{0:T(1024)} %get-tuple-element.99) | copy-start | bytes 13828
  335.0 67.2 %copy-start.17 = (bf16[36,6912]{1,0:T(8,128)(2,1)S(1)}, bf16[36,6912]{1,0:T(8,128)(2,1)}, u32[]{:S(2)}) copy-start(bf16[36,6912]{1,0:T(8,128)(2,1)} %refs_5_.1) | copy-start | bytes 1492996
  398.4 22.1 %copy-start.35 = (f32[2,1152]{1,0:T(2,128)S(1)}, f32[2,1152]{1,0:T(2,128)}, u32[]{:S(2)}) copy-start(f32[2,1152]{1,0:T(2,128)} %copy-done.34) | copy-start | bytes 27652
  402.2 2.5 copy-start.31
  425.7 1.8 copy-start.30
  427.5 4.2 copy-start.22
  429.4 3.8 copy-start.12
  (16 other events, 17.7 us)
